TPU v7x, 256 devices: a whole 4x4x8 slice. The times are simulated.
256 devices in a mesh: gx: 128 (over z, y_hi, x, core), gz: 2 (over y_lo).
Axes of the slice: x: 4, y: 4 (y_hi: 2, y_lo: 2; y = y_hi * 2 + y_lo), z: 8, core: 2. Of those that a mesh axis runs over, the one named last changes fastest.
Arguments:
- thermal_anomaly: float32 [128, 768, 512], P('gz', 'gx'), may hold values from -6 to 6
- saltiness_anomaly: float32 [128, 768, 512], P('gz', 'gx'), may hold values from -6 to 6
- eastward_flow: float32 [128, 768, 512], P('gz', 'gx'), may hold values from -6 to 6
- advective_ratio: float32 [128, 768, 512], P('gz', 'gx'), may hold values from -0.8 to 0.8
- dual_thermal_final: float32 [128, 768, 512], P('gz', 'gx'), may hold values from -6 to 6
- dual_saltiness_final: float32 [128, 768, 512], P('gz', 'gx'), may hold values from -6 to 6
- dual_flow_final: float32 [128, 768, 512], P('gz', 'gx'), may hold values from -6 to 6
- dual_kinematic_head: float32 [128, 768, 512], P('gz', 'gx'), may hold values from -6 to 6
- depth_into_eigenbasis: float32 [128, 128], replicated, may hold values from -1 to 1.25
- eigenbasis_into_depth: float32 [128, 128], replicated, may hold values from -1 to 1.25
- spectral_magnitudes: float32 [128], replicated, may hold values from 0.003 to 1
Outputs:
- dual_thermal_initial: float32 [128, 768, 512], P('gz', 'gx')
- dual_saltiness_initial: float32 [128, 768, 512], P('gz', 'gx')
- dual_flow_initial: float32 [128, 768, 512], P('gz', 'gx')
- dual_interface_ratio: float32 [128, 768, 512], P('gz', 'gx')
- dual_poisson_forcing: float32 [128, 768, 512], P('gz', 'gx')
All inputs are finite; a program needn't handle non-finite values.
Results may differ from a plain program's by a relative error of at most 0.0003.
Values sent between devices are 32-bit elements; how exact they have to be, the bound alone decides.
No kernel may reach another device: no remote copies, remote signals or barrier semaphores. Data moves between devices by JAX's collectives and lax.ppermute only.
A program may use at most 192 MiB of HBM per device.

v0:
```python
import math

import jax
import jax.numpy as jnp
from jax import lax
from jax.sharding import PartitionSpec as P

smooth_floor = 0.01
highest = lax.Precision.HIGHEST


def with_halo(array, sides, width):
    for axis, dim in sides:
        size, length = (lax.axis_size(axis), array.shape[dim])
        up = [(i, (i + 1) % size) for i in range(size)]
        down = [(j, i) for i, j in up]
        last = lax.slice_in_dim(array, length - width, length, axis=dim)
        initial = lax.slice_in_dim(array, 0, width, axis=dim)
        before = lax.ppermute(last, axis, up)
        after = lax.ppermute(initial, axis, down)
        array = jnp.concatenate([before, array, after], axis=dim)
    return array


def passed_along(block, axis, distance):
    devices = range(lax.axis_size(axis))
    route = [((i - distance) % len(devices), i) for i in devices]
    return lax.ppermute(block, axis, route)


def reconstruct(far_left, near_left, center, near_right, far_right):
    first_poly = (2.0 * far_left - 7.0 * near_left + 11.0 * center) / 6.0
    second_poly = (-near_left + 5.0 * center + 2.0 * near_right) / 6.0
    third_poly = (2.0 * center + 5.0 * near_right - far_right) / 6.0
    first_smooth = (
        13.0 / 12.0 * (far_left - 2.0 * near_left + center) ** 2
        + 0.25 * (far_left - 4.0 * near_left + 3.0 * center) ** 2
    )
    second_smooth = (
        13.0 / 12.0 * (near_left - 2.0 * center + near_right) ** 2
        + 0.25 * (near_left - near_right) ** 2
    )
    third_smooth = (
        13.0 / 12.0 * (center - 2.0 * near_right + far_right) ** 2
        + 0.25 * (3.0 * center - 4.0 * near_right + far_right) ** 2
    )
    first_alpha = 0.1 / (smooth_floor + first_smooth) ** 2
    second_alpha = 0.6 / (smooth_floor + second_smooth) ** 2
    third_alpha = 0.3 / (smooth_floor + third_smooth) ** 2
    total = first_alpha + second_alpha + third_alpha
    return (
        first_alpha * first_poly + second_alpha * second_poly + third_alpha * third_poly
    ) / total


def face_flux(minus_three, minus_two, minus_one, middle, plus_one, plus_two, advective_ratio):
    upwind_left = reconstruct(minus_three, minus_two, minus_one, middle, plus_one)
    upwind_right = reconstruct(plus_two, plus_one, middle, minus_one, minus_two)
    return advective_ratio * jnp.where(advective_ratio >= 0.0, upwind_left, upwind_right)


def window_fluxes(window, courant_faces, face_count):
    slices = [lax.slice_in_dim(window, offset, offset + face_count, axis=1) for offset in range(6)]
    return face_flux(
        slices[0], slices[1], slices[2], slices[3], slices[4], slices[5], courant_faces
    )


def hartley_table(length):
    numbers = jnp.arange(length, dtype=jnp.int32)
    product = numbers[:, None] * numbers[None, :] % length
    angle = product.astype(jnp.float32) * (2.0 * math.pi / length)
    return jnp.cos(angle) + jnp.sin(angle)


def wave_squares(numbers, length):
    return 2.0 - 2.0 * jnp.cos(numbers * (2.0 * math.pi / length))


def vertical(stored_numbers_array, matrix):
    level_values = stored_numbers_array.shape[0]
    first_level = lax.axis_index("gz") * level_values
    row_block = lax.dynamic_slice_in_dim(matrix, first_level, level_values, 0)
    return jnp.einsum(
        "mz,zyk->myk",
        row_block,
        lax.all_gather(stored_numbers_array, "gz", axis=0, tiled=True),
        precision=highest,
    )


def pressure_solve(
    dual_kinematic_head, depth_into_eigenbasis, eigenbasis_into_depth, spectral_magnitudes
):
    level_values, lateral_sheets, columns = dual_kinematic_head.shape
    across = lax.axis_size("gx")
    zonal_length = lateral_sheets * across
    meridional_table = hartley_table(columns)
    zonal_table = hartley_table(zonal_length)
    zonal_blocks = zonal_table.reshape(zonal_length, across, lateral_sheets)
    zonal_waves = wave_squares(jnp.arange(zonal_length, dtype=jnp.float32), zonal_length)
    normalizer = zonal_length * columns
    meridional_spectrum = jnp.einsum(
        "ky,zay->kza", meridional_table, dual_kinematic_head, precision=highest
    )
    meridional_spectrum = meridional_spectrum.reshape(columns, level_values * lateral_sheets)
    meridional_share = columns // across
    received = lax.all_to_all(meridional_spectrum, "gx", split_axis=0, concat_axis=1, tiled=True)
    received = received.reshape(meridional_share, across, level_values, lateral_sheets)
    spectral = jnp.einsum("ysza,ksa->zyk", received, zonal_blocks, precision=highest)
    projected = vertical(spectral, depth_into_eigenbasis)
    mode_rates = lax.dynamic_slice_in_dim(
        spectral_magnitudes, lax.axis_index("gz") * level_values, level_values, 0
    )
    numbers_y = lax.axis_index("gx") * meridional_share + jnp.arange(
        meridional_share, dtype=jnp.int32
    )
    meridional_waves = wave_squares(numbers_y.astype(jnp.float32), columns)
    divisor = (
        mode_rates[:, None, None] + meridional_waves[None, :, None] + zonal_waves[None, None, :]
    )
    scaled = -projected / (divisor * normalizer)
    restored = vertical(scaled, eigenbasis_into_depth)
    physical = jnp.einsum("zyk,ksa->ysza", restored, zonal_blocks, precision=highest)
    physical = physical.reshape(meridional_share, across * level_values * lateral_sheets)
    returned = lax.all_to_all(physical, "gx", split_axis=1, concat_axis=0, tiled=True).reshape(
        columns, level_values, lateral_sheets
    )
    return jnp.einsum("kza,ky->zay", returned, meridional_table, precision=highest)


def face_adjoints(widened, margin, first_face, face_count, courant_faces, lateral_sheets):
    fields = widened[0:3]
    source = widened[6]
    tentative_flow_speed = widened[5][:, 1:] + source[:, :-1] - source[:, 1:]
    padded_star = jnp.concatenate(
        [jnp.zeros_like(tentative_flow_speed[:, :1]), tentative_flow_speed], axis=1
    )
    lambdas = jnp.stack([widened[3], widened[4], padded_star])
    face_cell = first_face + margin
    cotangents = (
        lambdas[:, :, face_cell : face_cell + face_count]
        - lambdas[:, :, face_cell - 1 : face_cell - 1 + face_count]
    )
    windows = fields[:, :, face_cell - 3 : face_cell + face_count + 2]

    def fluxes_of(window, rates):
        return window_fluxes(window, rates, face_count)

    def scalar_step(running, items):
        window, upstream_sensitivity = items
        unused, pullback = jax.vjp(fluxes_of, window, courant_faces)
        window_bar, rate_bar = pullback(upstream_sensitivity)
        return (running + rate_bar, window_bar)

    courant_total, window_bars = lax.scan(
        scalar_step, jnp.zeros_like(courant_faces), (windows, cotangents)
    )
    owned_part = lambdas[:, :, margin : margin + lateral_sheets]
    return (owned_part, window_bars, courant_total)


def shards(
    thermal_anomaly,
    saltiness_anomaly,
    eastward_flow,
    advective_ratio,
    dual_thermal_final,
    dual_saltiness_final,
    dual_flow_final,
    dual_kinematic_head,
    depth_into_eigenbasis,
    eigenbasis_into_depth,
    spectral_magnitudes,
):
    dual_poisson_forcing = pressure_solve(
        dual_kinematic_head, depth_into_eigenbasis, eigenbasis_into_depth, spectral_magnitudes
    )
    lateral_sheets = thermal_anomaly.shape[1]
    primal_sweep_run = jnp.stack([thermal_anomaly, saltiness_anomaly, eastward_flow])
    forward_wide = with_halo(primal_sweep_run, (("gx", 2),), 3)
    adjoint_list = jnp.stack(
        [dual_thermal_final, dual_saltiness_final, dual_flow_final, dual_poisson_forcing]
    )
    arrived = passed_along(adjoint_list[:, :, lateral_sheets - 2 : lateral_sheets], "gx", 1)
    adjoint_wide = jnp.concatenate(
        [
            jnp.zeros_like(adjoint_list[:, :, 0:1]),
            arrived,
            adjoint_list,
            jnp.zeros_like(adjoint_list[:, :, 0:3]),
        ],
        axis=2,
    )
    widened = jnp.concatenate([forward_wide, adjoint_wide], axis=0)
    owned_part, window_bars, courant_total = face_adjoints(
        widened, 3, 0, lateral_sheets, advective_ratio, lateral_sheets
    )
    before = owned_part + window_bars[:, :, 3 : lateral_sheets + 3]
    ghosts = jnp.concatenate(
        [
            window_bars[:, :, 0:3],
            window_bars[:, :, lateral_sheets + 3 : lateral_sheets + 5],
            jnp.zeros_like(window_bars[:, :, 0:1]),
        ],
        axis=2,
    )
    arrivals = with_halo(ghosts, (("gx", 2),), 3)
    before = before.at[:, :, 0:3].add(arrivals[:, :, 0:3])
    before = before.at[:, :, lateral_sheets - 3 : lateral_sheets].add(arrivals[:, :, 9:12])
    return (before[0], before[1], before[2], courant_total, dual_poisson_forcing)


def solution(mesh):
    in_specs = (
        P("gz", "gx", None),
        P("gz", "gx", None),
        P("gz", "gx", None),
        P("gz", "gx", None),
        P("gz", "gx", None),
        P("gz", "gx", None),
        P("gz", "gx", None),
        P("gz", "gx", None),
        P(),
        P(),
        P(),
    )
    out_specs = (
        P("gz", "gx", None),
        P("gz", "gx", None),
        P("gz", "gx", None),
        P("gz", "gx", None),
        P("gz", "gx", None),
    )
    return jax.shard_map(shards, mesh=mesh, in_specs=in_specs, out_specs=out_specs, check_vma=False)
```

profile of v0, /device:TPU:23, one launch (start us, length us, event | category | flops | bytes accessed | tf_op | source)
XLA Modules:
  0.0 404.4 jit_solution(15611146342828976260)
XLA Ops:
  7.2 1.1 copy-done
  8.3 6.2 %fusion.46 = f32[512,64,6]{0,1,2:T(8,128)S(1)} fusion(f32[64,6,512]{2,0,1:T(8,128)S(1)} %copy-done), kind=kOutput, calls=%fused_computation.129 | convolution fusion | flops 1211891712 | bytes 1572864 | tf_op jit(solution)/shard_map/ky,zay->kza/dot_general | solution.py:103
  14.5 13.8 %copy.74 = f32[512,64,6]{2,1,0:T(8,128)} copy(f32[512,64,6]{0,1,2:T(8,128)S(1)} %fusion.46) | data formatting | bytes 1572864 | tf_op jit(solution)/shard_map/ky,zay->kza/dot_general | solution.py:103
  28.3 13.7 %all_to_all.24 = f32[128,4,384]{2,1,0:T(4,128)} reshape(f32[512,64,6]{2,1,0:T(8,128)} %copy.74) | data formatting | bytes 1572864 | tf_op jit(solution)/shard_map/all_to_all | solution.py:108
  42.0 15.5 %all-to-all-start = ((f32[128,4,384]{2,1,0:T(4,128)}), f32[128,4,384]{2,1,0:T(4,128)S(1)}, u32[]{:S(2)}, u32[]{:S(2)}) async-start(f32[128,4,384]{2,1,0:T(4,128)} %all_to_all.24), calls=%async_computation | async-start | bytes 1572864 | tf_op jit(solution)/shard_map/all_to_all | solution.py:108
  57.7 22.4 %all-to-all-done = f32[128,4,384]{2,1,0:T(4,128)S(1)} async-done(((f32[128,4,384]{2,1,0:T(4,128)}), f32[128,4,384]{2,1,0:T(4,128)S(1)}, u32[]{:S(2)}, u32[]{:S(2)}) %all-to-all-start) | async-done | bytes 786464 | tf_op jit(solution)/shard_map/all_to_all | solution.py:108
  80.5 12.1 %fusion.22 = f32[64,4,768]{2,0,1:T(8,128)S(1)} fusion(s32[128,6]{0,1:T(8,128)S(1)} %multiply_add_fusion.7, f32[4,128,64,6]{1,0,3,2:T(4,128)S(1)} %bitcast.91), kind=kOutput, calls=%fused_computation.106 | convolution fusion | flops 1817837568 | bytes 1575936 | tf_op jit(solution)/shard_map/ysza,ksa->zyk/dot_general | solution.py:110
  92.6 1.4 copy.77
  94.3 28.5 %all-gather.3.cloned.1.call-done = f32[128,4,768]{2,1,0:T(4,128)} async-done(((f32[64,4,768]{2,1,0:T(4,128)}), f32[128,4,768]{2,1,0:T(4,128)}) %all-gather.3.cloned.1.call-update) | async-done | bytes 1572880 | tf_op jit(solution)/shard_map/all_gather | solution.py:87
  122.8 2.7 fusion.28
  125.5 1.4 copy.79
  126.9 33.5 %all-gather.5.cloned.1.call-done = f32[128,4,768]{2,1,0:T(4,128)} async-done(((f32[64,4,768]{2,1,0:T(4,128)}), f32[128,4,768]{2,1,0:T(4,128)}) %all-gather.5.cloned.1.call-update) | async-done | bytes 1572880 | tf_op jit(solution)/shard_map/all_gather | solution.py:87
  160.4 2.6 fusion.19
  163.0 12.3 %fusion.25 = f32[4,128,64,6]{1,2,0,3:T(8,128)S(1)} fusion(f32[64,4,768,1]{2,0,1,3:T(8,128)S(1)} %fusion.19, s32[128,6]{0,1:T(8,128)S(1)} %multiply_add_fusion.7), kind=kOutput, calls=%fused_computation.107 | convolution fusion | flops 1817837568 | bytes 1575936 | tf_op jit(solution)/shard_map/zyk,ksa->ysza/dot_general | solution.py:124
  175.3 0.5 copy.81
  175.8 1.2 copy.82
  177.0 14.0 %all-to-all-start.1 = ((f32[4,128,384]{2,0,1:T(4,128)}), f32[4,128,384]{2,0,1:T(4,128)S(1)}, u32[]{:S(2)}, u32[]{:S(2)}) async-start(f32[4,128,384]{2,0,1:T(4,128)} %copy.82), calls=%async_computation.1 | async-start | bytes 1572864 | tf_op jit(solution)/shard_map/all_to_all | solution.py:126
  191.3 1.7 fusion.72
  193.0 0.7 collective-permute-start.2
  193.7 5.9 %collective-permute-start.1 = (f32[3,64,3,512]{3,1,2,0:T(8,128)}, f32[3,64,3,512]{3,1,2,0:T(8,128)}, u32[]{:S(2)}, u32[]{:S(2)}) collective-permute-start(f32[3,64,3,512]{3,1,2,0:T(8,128)} %get-tuple-element.265), channel_id=1, source_target_pairs={{0,2},{2,4},{4,6},{6,8},{8,10},{10,12},{12,14},{14,16},{16,18},{18... | collective-permute-start | bytes 3538952 | tf_op jit(solution)/shard_map/ppermute | solution.py:19
  199.6 14.1 %all-to-all-done.1 = f32[4,128,384]{2,0,1:T(4,128)S(1)} async-done(((f32[4,128,384]{2,0,1:T(4,128)}), f32[4,128,384]{2,0,1:T(4,128)S(1)}, u32[]{:S(2)}, u32[]{:S(2)}) %all-to-all-start.1) | async-done | bytes 786464 | tf_op jit(solution)/shard_map/all_to_all | solution.py:126
  213.7 18.7 %reshape.161 = f32[512,64,6]{2,1,0:T(8,128)} reshape(f32[128,4,384]{2,1,0:T(4,128)S(1)} %bitcast.74) | data formatting | bytes 1572864 | tf_op jit(solution)/shard_map/reshape | solution.py:126
  232.4 10.8 %copy.83 = f32[512,64,6]{0,1,2:T(8,128)} copy(f32[512,64,6]{2,1,0:T(8,128)} %reshape.161) | data formatting | bytes 1572864 | tf_op jit(solution)/shard_map/reshape | solution.py:126
  243.2 7.4 %fusion.44 = f32[64,6,512]{2,0,1:T(8,128)S(1)} fusion(f32[512,64,6]{0,1,2:T(8,128)} %copy.83), kind=kOutput, calls=%fused_computation.127 | convolution fusion | flops 1211891712 | bytes 1572864 | tf_op jit(solution)/shard_map/kza,ky->zay/dot_general | solution.py:129
  250.7 1.2 pad_maximum_fusion.6
  251.8 4.5 %collective-permute-start = (f32[4,64,2,512]{3,1,2,0:T(8,128)}, f32[4,64,2,512]{3,1,2,0:T(8,128)}, u32[]{:S(2)}, u32[]{:S(2)}) collective-permute-start(f32[4,64,2,512]{3,1,2,0:T(8,128)} %pad_maximum_fusion.6), channel_id=1, source_target_pairs={{254,0},{0,2},{2,4},{4,6},{6,8},{8,10},{10,12},{12,14},{14,16},{16... | collective-permute-start | bytes 3145736 | tf_op jit(solution)/shard_map/ppermute | solution.py:28
  256.5 4.2 %pad_maximum_fusion = f32[3,64,11,512]{3,1,2,0:T(8,128)} fusion(f32[3,64,3,512]{3,1,2,0:T(8,128)} %collective-permute-done.2, f32[3,64,3,512]{3,1,2,0:T(8,128)} %collective-permute-done.1, f32[1,64,6,512]{3,1,2,0:T(8,128)S(1)} %bitcast.76, f32[1,64,6,512]{3,1,2,0:T(8,128)S(1)} %bitcast.78, f32[1,64,6,512]{3,1,2,0:T(8,128)S(1)} %bitcast.80), kind=kLoop, calls=%fused_computation.71 | loop fusion | flops 4325376 | bytes 9043968 | tf_op jit(solution)/shard_map/concatenate | solution.py:21
  260.7 7.7 %collective-permute-done = f32[4,64,2,512]{3,1,2,0:T(8,128)} collective-permute-done((f32[4,64,2,512]{3,1,2,0:T(8,128)}, f32[4,64,2,512]{3,1,2,0:T(8,128)}, u32[]{:S(2)}, u32[]{:S(2)}) %collective-permute-start) | collective-permute-done | bytes 1048608 | tf_op jit(solution)/shard_map/ppermute | solution.py:28
  268.4 2.0 maximum_maximum_fusion
  270.9 0.5 slice.189
  271.8 1.2 copy-done.26
  273.0 1.9 fusion.4
  274.9 90.6 %while.18 = (s32[]{:T(128)}, f32[64,6,512]{2,0,1:T(8,128)}, f32[3,64,11,512]{3,1,2,0:T(8,128)}, f32[3,64,6,512]{3,1,2,0:T(8,128)}, f32[64,6,512]{2,0,1:T(8,128)}...) while((s32[]{:T(128)}, f32[64,6,512]{2,0,1:T(8,128)}, f32[3,64,11,512]{3,1,2,0:T(8,128)}, ...), condition=%wide.region_1.2_spmd.clone, body=%wide.region_0.1_spmd.clone.sunk | while | flops 91652096 | bytes 185009008 | solution.py:156
  275.1 1.6 dynamic-slice_bitcast_fusion.2
  276.7 5.7 %multiply_add_fusion.14 = (f32[64,6,512]{2,0,1:T(8,128)}, f32[64,6,512]{2,0,1:T(8,128)S(1)}, f32[64,6,512]{2,0,1:T(8,128)S(1)}, f32[64,6,512]{2,0,1:T(8,128)S(1)...) fusion(f32[64,11,512]{2,0,1:T(8,128)S(1)} %dynamic-slice_bitcas, ...), kind=kLoop, calls=%fused_computation.26.clone.1 | loop fusion | flops 17891328 | bytes 16711684 | tf_op jit(solution)/shard_map/while/body/eval_jaxpr/transpose(jvp())/add_any | solution.py:32
  282.5 7.8 %negate_add_fusion.2 = (f32[64,6,512]{2,0,1:T(8,128)}, f32[64,6,512]{2,0,1:T(8,128)}, f32[64,6,512]{2,0,1:T(8,128)}, f32[64,6,512]{2,0,1:T(8,128)}, f32[64,6,512...) fusion(f32[64,6,512]{2,0,1:T(8,128)S(1)} %get-tuple-element.345, ...), kind=kLoop, calls=%fused_computation.18.clone.1 | loop fusion | flops 27918336 | bytes 22216704 | tf_op jit(solution)/shard_map/while/body/eval_jaxpr/transpose(jvp())/add_any | solution.py:34
  290.4 3.7 fusion.77
  294.3 5.1 %multiply_add_fusion.15 = (f32[64,6,512]{2,0,1:T(8,128)S(1)}, f32[64,6,512]{2,0,1:T(8,128)S(1)}, f32[64,6,512]{2,0,1:T(8,128)S(1)}, f32[64,6,512]{2,0,1:T(8,128)S(1)}) fusion(f32[64,6,512]{2,0,1:T(8,128)} %get-tuple-element.355, f32[64,6,512]{2,0,1:T(8,128)S(1)} %copy-done.6, f32[64,6,512]{2,0,1:T(8,128)S(1)} %copy-done.5, ...), kind=kLoop, calls=%fused_computation.11.clone.1 | loop fusion | flops 19857408 | bytes 19660800 | tf_op jit(solution)/shard_map/while/body/eval_jaxpr/transpose(jvp())/add_any | solution.py:33
  299.5 2.3 multiply_add_fusion.16
  301.9 1.4 multiply_add_fusion.17
  303.4 1.7 bitcast_dynamic-update-slice_fusion.2
  305.1 1.6 dynamic-slice_bitcast_fusion.2
  306.7 5.7 %multiply_add_fusion.14 = (f32[64,6,512]{2,0,1:T(8,128)}, f32[64,6,512]{2,0,1:T(8,128)S(1)}, f32[64,6,512]{2,0,1:T(8,128)S(1)}, f32[64,6,512]{2,0,1:T(8,128)S(1)...) fusion(f32[64,11,512]{2,0,1:T(8,128)S(1)} %dynamic-slice_bitcas, ...), kind=kLoop, calls=%fused_computation.26.clone.1 | loop fusion | flops 17891328 | bytes 16711684 | tf_op jit(solution)/shard_map/while/body/eval_jaxpr/transpose(jvp())/add_any | solution.py:32
  312.4 7.8 %negate_add_fusion.2 = (f32[64,6,512]{2,0,1:T(8,128)}, f32[64,6,512]{2,0,1:T(8,128)}, f32[64,6,512]{2,0,1:T(8,128)}, f32[64,6,512]{2,0,1:T(8,128)}, f32[64,6,512...) fusion(f32[64,6,512]{2,0,1:T(8,128)S(1)} %get-tuple-element.345, ...), kind=kLoop, calls=%fused_computation.18.clone.1 | loop fusion | flops 27918336 | bytes 22216704 | tf_op jit(solution)/shard_map/while/body/eval_jaxpr/transpose(jvp())/add_any | solution.py:34
  320.4 4.0 fusion.77
  324.5 5.1 %multiply_add_fusion.15 = (f32[64,6,512]{2,0,1:T(8,128)S(1)}, f32[64,6,512]{2,0,1:T(8,128)S(1)}, f32[64,6,512]{2,0,1:T(8,128)S(1)}, f32[64,6,512]{2,0,1:T(8,128)S(1)}) fusion(f32[64,6,512]{2,0,1:T(8,128)} %get-tuple-element.355, f32[64,6,512]{2,0,1:T(8,128)S(1)} %copy-done.6, f32[64,6,512]{2,0,1:T(8,128)S(1)} %copy-done.5, ...), kind=kLoop, calls=%fused_computation.11.clone.1 | loop fusion | flops 19857408 | bytes 19660800 | tf_op jit(solution)/shard_map/while/body/eval_jaxpr/transpose(jvp())/add_any | solution.py:33
  329.8 2.3 multiply_add_fusion.16
  332.1 1.4 multiply_add_fusion.17
  333.6 1.7 bitcast_dynamic-update-slice_fusion.2
  335.2 1.6 dynamic-slice_bitcast_fusion.2
  336.8 5.7 %multiply_add_fusion.14 = (f32[64,6,512]{2,0,1:T(8,128)}, f32[64,6,512]{2,0,1:T(8,128)S(1)}, f32[64,6,512]{2,0,1:T(8,128)S(1)}, f32[64,6,512]{2,0,1:T(8,128)S(1)...) fusion(f32[64,11,512]{2,0,1:T(8,128)S(1)} %dynamic-slice_bitcas, ...), kind=kLoop, calls=%fused_computation.26.clone.1 | loop fusion | flops 17891328 | bytes 16711684 | tf_op jit(solution)/shard_map/while/body/eval_jaxpr/transpose(jvp())/add_any | solution.py:32
  342.6 7.8 %negate_add_fusion.2 = (f32[64,6,512]{2,0,1:T(8,128)}, f32[64,6,512]{2,0,1:T(8,128)}, f32[64,6,512]{2,0,1:T(8,128)}, f32[64,6,512]{2,0,1:T(8,128)}, f32[64,6,512...) fusion(f32[64,6,512]{2,0,1:T(8,128)S(1)} %get-tuple-element.345, ...), kind=kLoop, calls=%fused_computation.18.clone.1 | loop fusion | flops 27918336 | bytes 22216704 | tf_op jit(solution)/shard_map/while/body/eval_jaxpr/transpose(jvp())/add_any | solution.py:34
  350.5 4.0 fusion.77
  354.7 5.1 %multiply_add_fusion.15 = (f32[64,6,512]{2,0,1:T(8,128)S(1)}, f32[64,6,512]{2,0,1:T(8,128)S(1)}, f32[64,6,512]{2,0,1:T(8,128)S(1)}, f32[64,6,512]{2,0,1:T(8,128)S(1)}) fusion(f32[64,6,512]{2,0,1:T(8,128)} %get-tuple-element.355, f32[64,6,512]{2,0,1:T(8,128)S(1)} %copy-done.6, f32[64,6,512]{2,0,1:T(8,128)S(1)} %copy-done.5, ...), kind=kLoop, calls=%fused_computation.11.clone.1 | loop fusion | flops 19857408 | bytes 19660800 | tf_op jit(solution)/shard_map/while/body/eval_jaxpr/transpose(jvp())/add_any | solution.py:33
  359.9 2.3 multiply_add_fusion.16
  362.3 1.4 multiply_add_fusion.17
  363.7 1.8 bitcast_dynamic-update-slice_fusion.2
  365.5 1.3 slice.171
  367.0 7.1 %collective-permute-start.3 = (f32[3,64,3,512]{3,1,2,0:T(8,128)S(1)}, f32[3,64,3,512]{3,1,2,0:T(8,128)S(1)}, u32[]{:S(2)}, u32[]{:S(2)}) collective-permute-start(f32[3,64,3,512]{3,1,2,0:T(8,128)S(1)} %concatenate.19), channel_id=1, source_target_pairs={{0,2},{2,4},{4,6},{6,8},{8,10},{10,12},{12,14},{14,16},{16,18},{18... | collective-permute-start | bytes 3538952 | tf_op jit(solution)/shard_map/ppermute | solution.py:19
  374.1 1.4 slice.173
  375.5 2.2 slice_add_fusion
  377.8 9.4 %collective-permute-done.3 = f32[3,64,3,512]{3,1,2,0:T(8,128)S(1)} collective-permute-done((f32[3,64,3,512]{3,1,2,0:T(8,128)S(1)}, f32[3,64,3,512]{3,1,2,0:T(8,128)S(1)}, u32[]{:S(2)}, u32[]{:S(2)}) %collective-permute-start.3) | collective-permute-done | bytes 1179680 | tf_op jit(solution)/shard_map/ppermute | solution.py:19
  387.5 8.1 %collective-permute-done.4 = f32[3,64,3,512]{3,1,2,0:T(8,128)S(1)} collective-permute-done((f32[3,64,3,512]{3,1,2,0:T(8,128)S(1)}, f32[3,64,3,512]{3,1,2,0:T(8,128)S(1)}, u32[]{:S(2)}, u32[]{:S(2)}) %collective-permute-start.4) | collective-permute-done | bytes 1179680 | tf_op jit(solution)/shard_map/ppermute | solution.py:20
  396.0 1.5 slice_bitcast_fusion.2
  (211 shorter events, 3.5 us)
Async XLA Ops:
  42.0 38.1 %all-to-all-start = ((f32[128,4,384]{2,1,0:T(4,128)}), f32[128,4,384]{2,1,0:T(4,128)S(1)}, u32[]{:S(2)}, u32[]{:S(2)}) async-start(f32[128,4,384]{2,1,0:T(4,128)} %all_to_all.24), calls=%async_computation | async-start | bytes 1572864 | tf_op jit(solution)/shard_map/all_to_all | solution.py:108
  57.5 65.4 %all-gather.3.cloned.1.call-start = ((), (), s32[]{:S(2)}) async-start(), calls=%async_computation.2 | async-start | bytes 2359296 | tf_op jit(solution)/shard_map/all_gather | solution.py:87
  92.6 30.3 %copy-start.42 = (f32[128,128]{1,0:T(8,128)S(1)}, f32[128,128]{1,0:T(8,128)}, u32[]{:S(2)}) copy-start(f32[128,128]{1,0:T(8,128)} %param.25) | copy-start | bytes 196612
  94.0 66.4 %all-gather.5.cloned.1.call-start = ((), (), s32[]{:S(2)}) async-start(), calls=%async_computation.3 | async-start | bytes 2359296 | tf_op jit(solution)/shard_map/all_gather | solution.py:87
  94.3 66.1 %copy-start.41 = (f32[128,128]{1,0:T(8,128)S(1)}, f32[128,128]{1,0:T(8,128)}, u32[]{:S(2)}) copy-start(f32[128,128]{1,0:T(8,128)} %param.26) | copy-start | bytes 196612
  175.3 15.8 %copy-start.31 = (f32[64,6,512]{2,0,1:T(8,128)S(1)}, f32[64,6,512]{2,0,1:T(8,128)}, u32[]{:S(2)}) copy-start(f32[64,6,512]{2,0,1:T(8,128)} %param.19) | copy-start | bytes 2359300
  175.3 15.8 %copy-start.32 = (f32[64,6,512]{2,0,1:T(8,128)S(1)}, f32[64,6,512]{2,0,1:T(8,128)}, u32[]{:S(2)}) copy-start(f32[64,6,512]{2,0,1:T(8,128)} %param.18) | copy-start | bytes 2359300
  175.3 15.8 %copy-start.33 = (f32[64,6,512]{2,0,1:T(8,128)S(1)}, f32[64,6,512]{2,0,1:T(8,128)}, u32[]{:S(2)}) copy-start(f32[64,6,512]{2,0,1:T(8,128)} %param.17) | copy-start | bytes 2359300
  177.0 36.7 %all-to-all-start.1 = ((f32[4,128,384]{2,0,1:T(4,128)}), f32[4,128,384]{2,0,1:T(4,128)S(1)}, u32[]{:S(2)}, u32[]{:S(2)}) async-start(f32[4,128,384]{2,0,1:T(4,128)} %copy.82), calls=%async_computation.1 | async-start | bytes 1572864 | tf_op jit(solution)/shard_map/all_to_all | solution.py:126
  193.0 63.5 %collective-permute-start.2 = (f32[3,64,3,512]{3,1,2,0:T(8,128)}, f32[3,64,3,512]{3,1,2,0:T(8,128)}, u32[]{:S(2)}, u32[]{:S(2)}) collective-permute-start(f32[3,64,3,512]{3,1,2,0:T(8,128)} %get-tuple-element.266), channel_id=1, source_target_pairs={{2,0},{4,2},{6,4},{8,6},{10,8},{12,10},{14,12},{16,14},{18,16},{20... | collective-permute-start | bytes 3538952 | tf_op jit(solution)/shard_map/ppermute | solution.py:20
  193.7 62.8 %collective-permute-start.1 = (f32[3,64,3,512]{3,1,2,0:T(8,128)}, f32[3,64,3,512]{3,1,2,0:T(8,128)}, u32[]{:S(2)}, u32[]{:S(2)}) collective-permute-start(f32[3,64,3,512]{3,1,2,0:T(8,128)} %get-tuple-element.265), channel_id=1, source_target_pairs={{0,2},{2,4},{4,6},{6,8},{8,10},{10,12},{12,14},{14,16},{16,18},{18... | collective-permute-start | bytes 3538952 | tf_op jit(solution)/shard_map/ppermute | solution.py:19
  243.2 7.4 %copy-start.34 = (f32[64,6,512]{2,0,1:T(8,128)S(1)}, f32[64,6,512]{2,0,1:T(8,128)}, u32[]{:S(2)}) copy-start(f32[64,6,512]{2,0,1:T(8,128)} %param.23) | copy-start | bytes 2359300
  243.2 7.4 %copy-start.35 = (f32[64,6,512]{2,0,1:T(8,128)S(1)}, f32[64,6,512]{2,0,1:T(8,128)}, u32[]{:S(2)}) copy-start(f32[64,6,512]{2,0,1:T(8,128)} %param.22) | copy-start | bytes 2359300
  243.2 7.4 %copy-start.37 = (f32[64,6,512]{2,0,1:T(8,128)S(1)}, f32[64,6,512]{2,0,1:T(8,128)}, u32[]{:S(2)}) copy-start(f32[64,6,512]{2,0,1:T(8,128)} %param.21) | copy-start | bytes 2359300
  251.8 16.6 %collective-permute-start = (f32[4,64,2,512]{3,1,2,0:T(8,128)}, f32[4,64,2,512]{3,1,2,0:T(8,128)}, u32[]{:S(2)}, u32[]{:S(2)}) collective-permute-start(f32[4,64,2,512]{3,1,2,0:T(8,128)} %pad_maximum_fusion.6), channel_id=1, source_target_pairs={{254,0},{0,2},{2,4},{4,6},{6,8},{8,10},{10,12},{12,14},{14,16},{16... | collective-permute-start | bytes 3145736 | tf_op jit(solution)/shard_map/ppermute | solution.py:28
  256.5 12.0 %copy-start.36 = (f32[64,6,512]{2,0,1:T(8,128)S(1)}, f32[64,6,512]{2,0,1:T(8,128)}, u32[]{:S(2)}) copy-start(f32[64,6,512]{2,0,1:T(8,128)} %param.22) | copy-start | bytes 2359300
  256.5 12.0 %copy-start.38 = (f32[64,6,512]{2,0,1:T(8,128)S(1)}, f32[64,6,512]{2,0,1:T(8,128)}, u32[]{:S(2)}) copy-start(f32[64,6,512]{2,0,1:T(8,128)} %param.21) | copy-start | bytes 2359300
  256.5 12.0 %copy-start.40 = (f32[64,6,512]{2,0,1:T(8,128)S(1)}, f32[64,6,512]{2,0,1:T(8,128)}, u32[]{:S(2)}) copy-start(f32[64,6,512]{2,0,1:T(8,128)} %copy-done.39) | copy-start | bytes 2359300
  282.4 7.8 %copy-start.7 = (f32[64,6,512]{2,0,1:T(8,128)}, f32[64,6,512]{2,0,1:T(8,128)S(1)}, u32[]{:S(2)}) copy-start(f32[64,6,512]{2,0,1:T(8,128)S(1)} %get-tuple-element.349) | copy-start | bytes 2359300 | tf_op jit(solution)/shard_map/while
  282.4 7.8 %copy-start.9 = (f32[64,6,512]{2,0,1:T(8,128)}, f32[64,6,512]{2,0,1:T(8,128)S(1)}, u32[]{:S(2)}) copy-start(f32[64,6,512]{2,0,1:T(8,128)S(1)} %get-tuple-element.351) | copy-start | bytes 2359300 | tf_op jit(solution)/shard_map/while
  282.4 7.8 %copy-start.11 = (f32[64,6,512]{2,0,1:T(8,128)}, f32[64,6,512]{2,0,1:T(8,128)S(1)}, u32[]{:S(2)}) copy-start(f32[64,6,512]{2,0,1:T(8,128)S(1)} %get-tuple-element.347) | copy-start | bytes 2359300 | tf_op jit(solution)/shard_map/while
  282.4 7.8 %copy-start.12 = (f32[64,6,512]{2,0,1:T(8,128)}, f32[64,6,512]{2,0,1:T(8,128)S(1)}, u32[]{:S(2)}) copy-start(f32[64,6,512]{2,0,1:T(8,128)S(1)} %get-tuple-element.350) | copy-start | bytes 2359300 | tf_op jit(solution)/shard_map/while
  282.5 7.8 %copy-start.13 = (f32[64,6,512]{2,0,1:T(8,128)}, f32[64,6,512]{2,0,1:T(8,128)S(1)}, u32[]{:S(2)}) copy-start(f32[64,6,512]{2,0,1:T(8,128)S(1)} %get-tuple-element.348) | copy-start | bytes 2359300 | tf_op jit(solution)/shard_map/while
  294.2 5.2 %copy-start.14 = (f32[64,6,512]{2,0,1:T(8,128)S(1)}, f32[64,6,512]{2,0,1:T(8,128)}, u32[]{:S(2)}) copy-start(f32[64,6,512]{2,0,1:T(8,128)} %get-tuple-element.361) | copy-start | bytes 2359300 | tf_op jit(solution)/shard_map/while
  294.2 5.2 %copy-start.15 = (f32[64,6,512]{2,0,1:T(8,128)S(1)}, f32[64,6,512]{2,0,1:T(8,128)}, u32[]{:S(2)}) copy-start(f32[64,6,512]{2,0,1:T(8,128)} %get-tuple-element.355) | copy-start | bytes 2359300 | tf_op jit(solution)/shard_map/while
  294.2 5.2 %copy-start.16 = (f32[64,6,512]{2,0,1:T(8,128)S(1)}, f32[64,6,512]{2,0,1:T(8,128)}, u32[]{:S(2)}) copy-start(f32[64,6,512]{2,0,1:T(8,128)} %get-tuple-element.365) | copy-start | bytes 2359300 | tf_op jit(solution)/shard_map/while
  294.2 5.2 %copy-start.17 = (f32[64,6,512]{2,0,1:T(8,128)S(1)}, f32[64,6,512]{2,0,1:T(8,128)}, u32[]{:S(2)}) copy-start(f32[64,6,512]{2,0,1:T(8,128)} %get-tuple-element.359) | copy-start | bytes 2359300 | tf_op jit(solution)/shard_map/while
  294.2 5.2 %copy-start.18 = (f32[64,6,512]{2,0,1:T(8,128)S(1)}, f32[64,6,512]{2,0,1:T(8,128)}, u32[]{:S(2)}) copy-start(f32[64,6,512]{2,0,1:T(8,128)} %get-tuple-element.362) | copy-start | bytes 2359300 | tf_op jit(solution)/shard_map/while
  294.2 5.2 %copy-start.19 = (f32[64,6,512]{2,0,1:T(8,128)S(1)}, f32[64,6,512]{2,0,1:T(8,128)}, u32[]{:S(2)}) copy-start(f32[64,6,512]{2,0,1:T(8,128)} %get-tuple-element.360) | copy-start | bytes 2359300 | tf_op jit(solution)/shard_map/while
  294.2 5.2 %copy-start.20 = (f32[64,6,512]{2,0,1:T(8,128)S(1)}, f32[64,6,512]{2,0,1:T(8,128)}, u32[]{:S(2)}) copy-start(f32[64,6,512]{2,0,1:T(8,128)} %get-tuple-element.367) | copy-start | bytes 2359300 | tf_op jit(solution)/shard_map/while
  294.3 5.2 %copy-start.21 = (f32[64,6,512]{2,0,1:T(8,128)S(1)}, f32[64,6,512]{2,0,1:T(8,128)}, u32[]{:S(2)}) copy-start(f32[64,6,512]{2,0,1:T(8,128)} %get-tuple-element.372) | copy-start | bytes 2359300 | tf_op jit(solution)/shard_map/while
  294.3 5.2 %copy-start.22 = (f32[64,6,512]{2,0,1:T(8,128)S(1)}, f32[64,6,512]{2,0,1:T(8,128)}, u32[]{:S(2)}) copy-start(f32[64,6,512]{2,0,1:T(8,128)} %get-tuple-element.370) | copy-start | bytes 2359300 | tf_op jit(solution)/shard_map/while
  294.3 5.3 %copy-start.23 = (f32[64,6,512]{2,0,1:T(8,128)S(1)}, f32[64,6,512]{2,0,1:T(8,128)}, u32[]{:S(2)}) copy-start(f32[64,6,512]{2,0,1:T(8,128)} %get-tuple-element.371) | copy-start | bytes 2359300 | tf_op jit(solution)/shard_map/while
  312.4 7.8 %copy-start.7 = (f32[64,6,512]{2,0,1:T(8,128)}, f32[64,6,512]{2,0,1:T(8,128)S(1)}, u32[]{:S(2)}) copy-start(f32[64,6,512]{2,0,1:T(8,128)S(1)} %get-tuple-element.349) | copy-start | bytes 2359300 | tf_op jit(solution)/shard_map/while
  312.4 7.8 %copy-start.9 = (f32[64,6,512]{2,0,1:T(8,128)}, f32[64,6,512]{2,0,1:T(8,128)S(1)}, u32[]{:S(2)}) copy-start(f32[64,6,512]{2,0,1:T(8,128)S(1)} %get-tuple-element.351) | copy-start | bytes 2359300 | tf_op jit(solution)/shard_map/while
  312.4 7.8 %copy-start.11 = (f32[64,6,512]{2,0,1:T(8,128)}, f32[64,6,512]{2,0,1:T(8,128)S(1)}, u32[]{:S(2)}) copy-start(f32[64,6,512]{2,0,1:T(8,128)S(1)} %get-tuple-element.347) | copy-start | bytes 2359300 | tf_op jit(solution)/shard_map/while
  312.4 7.8 %copy-start.12 = (f32[64,6,512]{2,0,1:T(8,128)}, f32[64,6,512]{2,0,1:T(8,128)S(1)}, u32[]{:S(2)}) copy-start(f32[64,6,512]{2,0,1:T(8,128)S(1)} %get-tuple-element.350) | copy-start | bytes 2359300 | tf_op jit(solution)/shard_map/while
  312.4 7.8 %copy-start.13 = (f32[64,6,512]{2,0,1:T(8,128)}, f32[64,6,512]{2,0,1:T(8,128)S(1)}, u32[]{:S(2)}) copy-start(f32[64,6,512]{2,0,1:T(8,128)S(1)} %get-tuple-element.348) | copy-start | bytes 2359300 | tf_op jit(solution)/shard_map/while
  324.4 5.2 %copy-start.14 = (f32[64,6,512]{2,0,1:T(8,128)S(1)}, f32[64,6,512]{2,0,1:T(8,128)}, u32[]{:S(2)}) copy-start(f32[64,6,512]{2,0,1:T(8,128)} %get-tuple-element.361) | copy-start | bytes 2359300 | tf_op jit(solution)/shard_map/while
  324.4 5.2 %copy-start.15 = (f32[64,6,512]{2,0,1:T(8,128)S(1)}, f32[64,6,512]{2,0,1:T(8,128)}, u32[]{:S(2)}) copy-start(f32[64,6,512]{2,0,1:T(8,128)} %get-tuple-element.355) | copy-start | bytes 2359300 | tf_op jit(solution)/shard_map/while
  324.4 5.2 %copy-start.16 = (f32[64,6,512]{2,0,1:T(8,128)S(1)}, f32[64,6,512]{2,0,1:T(8,128)}, u32[]{:S(2)}) copy-start(f32[64,6,512]{2,0,1:T(8,128)} %get-tuple-element.365) | copy-start | bytes 2359300 | tf_op jit(solution)/shard_map/while
  324.4 5.2 %copy-start.17 = (f32[64,6,512]{2,0,1:T(8,128)S(1)}, f32[64,6,512]{2,0,1:T(8,128)}, u32[]{:S(2)}) copy-start(f32[64,6,512]{2,0,1:T(8,128)} %get-tuple-element.359) | copy-start | bytes 2359300 | tf_op jit(solution)/shard_map/while
  324.4 5.2 %copy-start.18 = (f32[64,6,512]{2,0,1:T(8,128)S(1)}, f32[64,6,512]{2,0,1:T(8,128)}, u32[]{:S(2)}) copy-start(f32[64,6,512]{2,0,1:T(8,128)} %get-tuple-element.362) | copy-start | bytes 2359300 | tf_op jit(solution)/shard_map/while
  324.4 5.2 %copy-start.19 = (f32[64,6,512]{2,0,1:T(8,128)S(1)}, f32[64,6,512]{2,0,1:T(8,128)}, u32[]{:S(2)}) copy-start(f32[64,6,512]{2,0,1:T(8,128)} %get-tuple-element.360) | copy-start | bytes 2359300 | tf_op jit(solution)/shard_map/while
  324.5 5.3 %copy-start.23 = (f32[64,6,512]{2,0,1:T(8,128)S(1)}, f32[64,6,512]{2,0,1:T(8,128)}, u32[]{:S(2)}) copy-start(f32[64,6,512]{2,0,1:T(8,128)} %get-tuple-element.371) | copy-start | bytes 2359300 | tf_op jit(solution)/shard_map/while
  342.6 7.8 %copy-start.7 = (f32[64,6,512]{2,0,1:T(8,128)}, f32[64,6,512]{2,0,1:T(8,128)S(1)}, u32[]{:S(2)}) copy-start(f32[64,6,512]{2,0,1:T(8,128)S(1)} %get-tuple-element.349) | copy-start | bytes 2359300 | tf_op jit(solution)/shard_map/while
  342.6 7.8 %copy-start.9 = (f32[64,6,512]{2,0,1:T(8,128)}, f32[64,6,512]{2,0,1:T(8,128)S(1)}, u32[]{:S(2)}) copy-start(f32[64,6,512]{2,0,1:T(8,128)S(1)} %get-tuple-element.351) | copy-start | bytes 2359300 | tf_op jit(solution)/shard_map/while
  342.6 7.8 %copy-start.11 = (f32[64,6,512]{2,0,1:T(8,128)}, f32[64,6,512]{2,0,1:T(8,128)S(1)}, u32[]{:S(2)}) copy-start(f32[64,6,512]{2,0,1:T(8,128)S(1)} %get-tuple-element.347) | copy-start | bytes 2359300 | tf_op jit(solution)/shard_map/while
  342.6 7.8 %copy-start.12 = (f32[64,6,512]{2,0,1:T(8,128)}, f32[64,6,512]{2,0,1:T(8,128)S(1)}, u32[]{:S(2)}) copy-start(f32[64,6,512]{2,0,1:T(8,128)S(1)} %get-tuple-element.350) | copy-start | bytes 2359300 | tf_op jit(solution)/shard_map/while
  342.6 7.8 %copy-start.13 = (f32[64,6,512]{2,0,1:T(8,128)}, f32[64,6,512]{2,0,1:T(8,128)S(1)}, u32[]{:S(2)}) copy-start(f32[64,6,512]{2,0,1:T(8,128)S(1)} %get-tuple-element.348) | copy-start | bytes 2359300 | tf_op jit(solution)/shard_map/while
  354.6 5.2 %copy-start.14 = (f32[64,6,512]{2,0,1:T(8,128)S(1)}, f32[64,6,512]{2,0,1:T(8,128)}, u32[]{:S(2)}) copy-start(f32[64,6,512]{2,0,1:T(8,128)} %get-tuple-element.361) | copy-start | bytes 2359300 | tf_op jit(solution)/shard_map/while
  354.6 5.2 %copy-start.15 = (f32[64,6,512]{2,0,1:T(8,128)S(1)}, f32[64,6,512]{2,0,1:T(8,128)}, u32[]{:S(2)}) copy-start(f32[64,6,512]{2,0,1:T(8,128)} %get-tuple-element.355) | copy-start | bytes 2359300 | tf_op jit(solution)/shard_map/while
  354.6 5.2 %copy-start.16 = (f32[64,6,512]{2,0,1:T(8,128)S(1)}, f32[64,6,512]{2,0,1:T(8,128)}, u32[]{:S(2)}) copy-start(f32[64,6,512]{2,0,1:T(8,128)} %get-tuple-element.365) | copy-start | bytes 2359300 | tf_op jit(solution)/shard_map/while
  354.6 5.2 %copy-start.17 = (f32[64,6,512]{2,0,1:T(8,128)S(1)}, f32[64,6,512]{2,0,1:T(8,128)}, u32[]{:S(2)}) copy-start(f32[64,6,512]{2,0,1:T(8,128)} %get-tuple-element.359) | copy-start | bytes 2359300 | tf_op jit(solution)/shard_map/while
  354.6 5.2 %copy-start.18 = (f32[64,6,512]{2,0,1:T(8,128)S(1)}, f32[64,6,512]{2,0,1:T(8,128)}, u32[]{:S(2)}) copy-start(f32[64,6,512]{2,0,1:T(8,128)} %get-tuple-element.362) | copy-start | bytes 2359300 | tf_op jit(solution)/shard_map/while
  354.6 5.2 %copy-start.19 = (f32[64,6,512]{2,0,1:T(8,128)S(1)}, f32[64,6,512]{2,0,1:T(8,128)}, u32[]{:S(2)}) copy-start(f32[64,6,512]{2,0,1:T(8,128)} %get-tuple-element.360) | copy-start | bytes 2359300 | tf_op jit(solution)/shard_map/while
  354.6 5.2 %copy-start.20 = (f32[64,6,512]{2,0,1:T(8,128)S(1)}, f32[64,6,512]{2,0,1:T(8,128)}, u32[]{:S(2)}) copy-start(f32[64,6,512]{2,0,1:T(8,128)} %get-tuple-element.367) | copy-start | bytes 2359300 | tf_op jit(solution)/shard_map/while
  354.6 5.2 %copy-start.21 = (f32[64,6,512]{2,0,1:T(8,128)S(1)}, f32[64,6,512]{2,0,1:T(8,128)}, u32[]{:S(2)}) copy-start(f32[64,6,512]{2,0,1:T(8,128)} %get-tuple-element.372) | copy-start | bytes 2359300 | tf_op jit(solution)/shard_map/while
  354.6 5.2 %copy-start.22 = (f32[64,6,512]{2,0,1:T(8,128)S(1)}, f32[64,6,512]{2,0,1:T(8,128)}, u32[]{:S(2)}) copy-start(f32[64,6,512]{2,0,1:T(8,128)} %get-tuple-element.370) | copy-start | bytes 2359300 | tf_op jit(solution)/shard_map/while
  354.6 5.3 %copy-start.23 = (f32[64,6,512]{2,0,1:T(8,128)S(1)}, f32[64,6,512]{2,0,1:T(8,128)}, u32[]{:S(2)}) copy-start(f32[64,6,512]{2,0,1:T(8,128)} %get-tuple-element.371) | copy-start | bytes 2359300 | tf_op jit(solution)/shard_map/while
  365.5 10.0 %copy-start.30 = (f32[1,64,12,512]{3,1,2,0:T(8,128)S(1)}, f32[1,64,12,512]{3,1,2,0:T(8,128)}, u32[]{:S(2)}) copy-start(f32[1,64,12,512]{3,1,2,0:T(8,128)} %copy-done.29) | copy-start | bytes 4718596
  366.8 8.7 %copy-start.27 = (f32[2,64,12,512]{3,1,2,0:T(8,128)S(1)}, f32[2,64,12,512]{3,1,2,0:T(8,128)}, u32[]{:S(2)}) copy-start(f32[2,64,12,512]{3,1,2,0:T(8,128)} %copy-done.26) | copy-start | bytes 9437188
  367.0 20.2 %collective-permute-start.3 = (f32[3,64,3,512]{3,1,2,0:T(8,128)S(1)}, f32[3,64,3,512]{3,1,2,0:T(8,128)S(1)}, u32[]{:S(2)}, u32[]{:S(2)}) collective-permute-start(f32[3,64,3,512]{3,1,2,0:T(8,128)S(1)} %concatenate.19), channel_id=1, source_target_pairs={{0,2},{2,4},{4,6},{6,8},{8,10},{10,12},{12,14},{14,16},{16,18},{18... | collective-permute-start | bytes 3538952 | tf_op jit(solution)/shard_map/ppermute | solution.py:19
  375.4 20.2 %collective-permute-start.4 = (f32[3,64,3,512]{3,1,2,0:T(8,128)S(1)}, f32[3,64,3,512]{3,1,2,0:T(8,128)S(1)}, u32[]{:S(2)}, u32[]{:S(2)}) collective-permute-start(f32[3,64,3,512]{3,1,2,0:T(8,128)S(1)} %slice.173), channel_id=1, source_target_pairs={{2,0},{4,2},{6,4},{8,6},{10,8},{12,10},{14,12},{16,14},{18,16},{20... | collective-permute-start | bytes 3538952 | tf_op jit(solution)/shard_map/ppermute | solution.py:20
  (39 other events, 121.7 us)
Sparse Core Ops, SparseCore 0:
  94.1 28.6 all-gather.2
  127.0 33.2 all-gather.4
where the time goes:
time: 411 us; the launch traced here: 404 us
  waiting for transfers between devices  124 us (30%)
  other arithmetic  96.9 us (24%)
  local copies, waits for them, and re-layouts  76.6 us (19%)
  starting transfers between devices  48.1 us (12%)
  matrix products  43.2 us (11%)
  between operations  14.6 us (4%)
    all_gather x2, waiting for transfers between devices, vertical(): lax.all_gather(stored_numbers_array, 'gz', axis=0, tiled=True)  62 us
    reshape x2, local copies, waits for them, and re-layouts, pressure_solve(): lax.all_to_all(physical, 'gx', split_axis=1, concat_axis=0, tiled=True)  29.5 us
    add_any x9, other arithmetic, reconstruct(): first_poly = (2.0 * far_left - 7.0 * near_left + 11.0 * center) / 6.0  28.4 us
    add_any x3, other arithmetic, reconstruct(): third_poly = (2.0 * center + 5.0 * near_right - far_right) / 6.0  23.4 us
    all_to_all x1, waiting for transfers between devices, pressure_solve(): lax.all_to_all(meridional_spectrum, 'gx', split_axis=0, concat_axis=1, ti...  22.4 us
    all_to_all x1, starting transfers between devices, pressure_solve(): lax.all_to_all(meridional_spectrum, 'gx', split_axis=0, concat_axis=1, ti...  15.5 us
    add_any x3, other arithmetic, reconstruct(): second_poly = (-near_left + 5.0 * center + 2.0 * near_right) / 6.0  15.3 us
    all_to_all x1, waiting for transfers between devices, pressure_solve(): lax.all_to_all(physical, 'gx', split_axis=1, concat_axis=0, tiled=True)  14.1 us
  transfers between devices with their start and end apart: 9, of which 7 were waited for; matrix products, arithmetic and copies ran while one was open for 12% of the time, Pallas kernels for 0%

commit v1 on v0

v1 whole, which is shorter than its diff:
```python
import math

import jax
import jax.numpy as jnp
import numpy as np
from jax import lax
from jax.experimental import pallas as pl
from jax.experimental.pallas import tpu as pltpu
from jax.sharding import Mesh, PartitionSpec as P

f32 = jnp.float32
bf16 = jnp.bfloat16
highest = lax.Precision.HIGHEST
LANES = 128
ROWS = 8
SPLIT = {128: (8, 2, 4, 2)}
ALONG = ("z", "yh", "x", "c")
GROUP = ("yh", "x", "c")
GROUP_ALL = ("yh", "x", "c", "gz")


def hartley_table(length):
    numbers = np.arange(length)
    angle = (numbers[:, None] * numbers[None, :] % length) * (2.0 * math.pi / length)
    return np.cos(angle) + np.sin(angle)


def halves(value):
    upper = value.astype(bf16)
    return upper, (value - upper.astype(f32)).astype(bf16)


def exact_dot(a, b):
    return jnp.dot(a, b, precision=highest, preferred_element_type=f32)


def split_dot(a, b):
    (a_hi, a_lo), (b_hi, b_lo) = a, b

    def dot(p, q):
        return jnp.dot(p, q, preferred_element_type=f32)

    return dot(a_hi, b_hi) + (dot(a_hi, b_lo) + dot(a_lo, b_hi))


def inverse(value):
    guess = pl.reciprocal(value, approx=True)
    return guess * (2.0 - value * guess)


def face_terms(edges, ratio):
    positive = ratio >= 0.0
    d1 = jnp.where(positive, edges[0], edges[4])
    d2 = jnp.where(positive, edges[1], edges[3])
    d3 = edges[2]
    d4 = jnp.where(positive, edges[3], edges[1])
    s1, s2, s3 = d2 - d1, d3 - d2, d4 - d3
    e0, e1, e2 = (d2 + d2) + s1, d2 + d3, (d3 + d3) - s3
    t0, t1, t2 = (13.0 / 3.0) * s1, (13.0 / 3.0) * s2, (13.0 / 3.0) * s3
    r0 = inverse(t0 * s1 + (e0 * e0 + 0.04))
    r1 = inverse(t1 * s2 + (e1 * e1 + 0.04))
    r2 = inverse(t2 * s3 + (e2 * e2 + 0.04))
    u0, u1, u2 = (1.0 / 6.0) * (r0 * r0), r1 * r1, 0.5 * (r2 * r2)
    norm = inverse(u0 + u1 + u2)
    w0, w1, w2 = u0 * norm, u1 * norm, u2 * norm
    bend = s1 - s2
    a2, cc = bend + bend, s2 - s3
    z = w0 * a2 + w2 * cc
    total = (e1 + d3) + z
    n0, n1, n2 = w0 * r0 * (z - a2), w1 * r1 * z, w2 * r2 * (z - cc)
    p0, q0 = n0 * t0, n0 * e0
    p1, q1 = n1 * t1, n1 * e1
    p2, q2 = n2 * t2, n2 * e2
    left, right = p0 + q0, q2 - p2
    g1 = -(0.5 * w0 + left)
    g2 = (1.25 * w0 + 0.25 * w1) + (left + (q0 + q0)) + (q1 - p1)
    g3 = (0.5 * w1 + w2) + (right + (q2 + q2)) + (p1 + q1)
    g4 = -(0.25 * w2 + right)
    return positive, total, (g1, g2, g3, g4)


def weno_tile(field, ratio, cotangent, faces, cells, owned):
    edge_of, edge_bar, cell_bar, ratio_bar = {}, {}, {}, {}

    def edge(x):
        if x not in edge_of:
            edge_of[x] = field(x + 1) - field(x)
        return edge_of[x]

    def add(store, key, value):
        store[key] = store[key] + value if key in store else value

    for f in faces:
        c, e = ratio(f), cotangent(f)
        positive, total, (g1, g2, g3, g4) = face_terms([edge(f - 3 + k) for k in range(5)], c)
        gain = (2.0 / 3.0) * (jnp.abs(c) * e)
        g1, g2, g3, g4 = gain * g1, gain * g2, gain * g3, gain * g4
        zero = jnp.zeros_like(g1)
        add(edge_bar, f - 3, jnp.where(positive, g1, zero))
        add(edge_bar, f - 2, jnp.where(positive, g2, g4))
        add(edge_bar, f - 1, g3)
        add(edge_bar, f, jnp.where(positive, g4, g2))
        add(edge_bar, f + 1, jnp.where(positive, zero, g1))
        add(cell_bar, f - 1, jnp.maximum(c, 0.0) * e)
        add(cell_bar, f, jnp.minimum(c, 0.0) * e)
        if f in owned:
            center = jnp.where(positive, field(f - 1), field(f))
            sixth = total * (1.0 / 6.0)
            ratio_bar[f] = e * (center + jnp.where(positive, sixth, -sixth))
    bars = {}
    for x in cells:
        parts = []
        if x - 1 in edge_bar:
            parts.append(edge_bar[x - 1])
        if x in edge_bar:
            parts.append(-edge_bar[x])
        if x in cell_bar:
            parts.append(cell_bar[x])
        bars[x] = sum(parts[1:], parts[0])
    return bars, ratio_bar


def planes(own, before, after, own_count, before_at, before_count, after_at, lanes):
    def read(x):
        if x < 0:
            return before[before_at + before_count + x, :, lanes]
        if x >= own_count:
            return after[after_at + x - own_count, :, lanes]
        return own[x, :, lanes]

    return read


def tracer_kernel(t, s, c, lt, ls, before, after, t_out, s_out, c_out, left_out, right_out):
    n, _, width = t.shape

    def tile(l, carry):
        lanes = pl.ds(pl.multiple_of(l * LANES, LANES), LANES)
        sums = {}
        for k, (own, dual, out) in enumerate(((t, lt, t_out), (s, ls, s_out))):
            field = planes(own, before, after, n, 3 * k, 3, 2 * k, lanes)
            lam = planes(dual, before, after, n, 6 + k, 1, 0, lanes)
            bars, ratio_bar = weno_tile(
                field,
                lambda f: c[f, :, lanes],
                lambda f: lam(f) - lam(f - 1),
                range(n),
                range(-3, n + 2),
                range(n),
            )
            for x in range(n):
                out[x, :, lanes] = dual[x, :, lanes] + bars[x]
                sums[x] = sums[x] + ratio_bar[x] if x in sums else ratio_bar[x]
            for x in range(3):
                left_out[3 * k + x, :, lanes] = bars[x - 3]
            for x in range(2):
                right_out[2 * k + x, :, lanes] = bars[n + x]
        for x in range(n):
            c_out[x, :, lanes] = sums[x]
        return carry

    lax.fori_loop(0, width // LANES, tile, 0)


def flow_kernel(
    u, c, df, before, after, phi, phi_edge, t_in, s_in, c_in, from_left, from_right,
    t_out, s_out, u_out, c_out,
):
    n, _, width = u.shape

    def tile(l, carry):
        lanes = pl.ds(pl.multiple_of(l * LANES, LANES), LANES)
        field = planes(u, before, after, n, 0, 5, 0, lanes)
        ratio = planes(c, before, after, n, 5, 2, 5, lanes)
        dual = planes(df, before, after, n, 7, 3, 8, lanes)
        head = planes(phi, phi_edge, phi_edge, n, 0, 3, 3, lanes)
        step = {x: head(x) - head(x - 1) for x in range(-2, n + 2)}

        def bend(x):
            if x == -3:
                return phi_edge[5, :, lanes]
            if x == n + 1:
                return phi_edge[6, :, lanes]
            return step[x] - step[x + 1]

        bars, ratio_bar = weno_tile(
            field,
            ratio,
            lambda f: (dual(f) - dual(f - 1)) + bend(f - 1),
            range(-2, n + 3),
            range(n),
            range(n),
        )
        for x in range(n):
            u_out[x, :, lanes] = (df[x, :, lanes] - step[x]) + bars[x]
            c_out[x, :, lanes] = c_in[x, :, lanes] + ratio_bar[x]
        for k, (base, out) in enumerate(((t_in, t_out), (s_in, s_out))):
            for x in range(n):
                value = base[x, :, lanes]
                if x < 2:
                    value = value + from_left[2 * k + x, :, lanes]
                if x >= n - 3:
                    value = value + from_right[3 * k + x - (n - 3), :, lanes]
                out[x, :, lanes] = value
        return carry

    lax.fori_loop(0, width // LANES, tile, 0)


def moments_kernel(rows, blocks, head, table, depth, rates, waves, spec, coeff, sums, a_acc, b_acc, power):
    j, last = pl.program_id(0), pl.num_programs(0) - 1
    half = depth.shape[1] // 2
    columns = table.shape[1]
    width = columns // blocks

    @pl.when(j == 0)
    def _():
        a = rates[...] + waves[...]
        root = jnp.sqrt(a * (1.0 + 0.25 * a))
        rho = 1.0 / ((1.0 + 0.5 * a) + root)
        coeff[0] = rho
        coeff[1] = 0.5 / root
        coeff[2] = a
        a_acc[...] = jnp.zeros_like(a_acc)
        b_acc[...] = jnp.zeros_like(b_acc)
        power[...] = jnp.ones_like(power)

    values = exact_dot(head[0], table[...])
    spec[0] = values
    first = lax.axis_index("gz") == 0
    share = jnp.where(first, depth[:, :half], depth[:, half:])
    part = exact_dot(share * (-1.0 / columns), values)
    rho = coeff[0]
    a_acc[...] = a_acc[...] * rho + part
    b_acc[...] = b_acc[...] + power[...] * part
    power[...] = power[...] * rho

    @pl.when(j == last)
    def _():
        for n in range(sums.shape[0]):
            m, r = n // blocks * rows, n % blocks * width
            sums[n, 0] = a_acc[m : m + rows, r : r + width]
            sums[n, 1] = b_acc[m : m + rows, r : r + width]


def halo_kernel(left, right, table, spec):
    value = jnp.concatenate([left[...], right[...]], axis=0)
    count, levels, columns = value.shape
    spec[...] = exact_dot(value.reshape(count * levels, columns), table[...]).reshape(value.shape)


def chunk_decay(rows, blocks, coeff, sheets):
    n = lax.axis_index("yh")
    for name in GROUP_ALL[1:]:
        n = n * lax.axis_size(name) + lax.axis_index(name)
    width = coeff.shape[2] // blocks
    m = pl.multiple_of(n // blocks * rows, rows)
    r = pl.multiple_of(n % blocks * width, width)
    rho = coeff[0, pl.ds(m, rows), pl.ds(r, width)]
    square = rho * rho
    result = jnp.ones_like(rho)
    for _ in range(sheets // 2):
        result = result * square
    return result * rho if sheets % 2 else result


def repeated(value, times):
    result, power = None, value
    while times:
        if times & 1:
            result = power if result is None else result * power
        power, times = power * power, times >> 1
    return result


def group_kernel(rows, blocks, sheets, got, coeff, out):
    decay = chunk_decay(rows, blocks, coeff, sheets)
    places, rings = got.shape[0], out.shape[0]
    forward, backward = None, None
    for p in range(places):
        a, b = got[p, 0, 0] + got[p, 1, 0], got[places - 1 - p, 0, 1] + got[places - 1 - p, 1, 1]
        forward = a if forward is None else forward * decay + a
        backward = b if backward is None else backward * decay + b
    mine = lax.axis_index("z")
    factor = repeated(decay, places)
    for k in range(rings):
        out[lax.rem(mine + 1 + k, rings), 0] = forward
        out[lax.rem(mine + 2 * rings - 1 - k, rings), 1] = backward
        forward, backward = forward * factor, backward * factor


def carry_kernel(rows, blocks, sheets, got, rings, coeff, out):
    decay = chunk_decay(rows, blocks, coeff, sheets)
    places, around = got.shape[0], rings.shape[0]
    closing = 1.0 / (1.0 - repeated(decay, places * around))
    left, right = rings[0, 0], rings[0, 1]
    for k in range(1, around):
        left, right = left + rings[k, 0], right + rings[k, 1]
    left, right = left * closing, right * closing
    for p in range(places):
        q = places - 1 - p
        for g in range(2):
            out[p, g, 0] = left
            out[q, g, 1] = right
        left = left * decay + (got[p, 0, 0] + got[p, 1, 0])
        right = right * decay + (got[q, 0, 1] + got[q, 1, 1])


def source_kernel(own, edge, own_other, edge_other, depth, out, full):
    half = own.shape[1]
    mine = lax.axis_index("gz")
    here = pl.ds(pl.multiple_of(mine * half, half), half)
    there = pl.ds(pl.multiple_of((1 - mine) * half, half), half)
    scale = -1.0 / own.shape[2]
    matrix = depth[...] * scale
    n = own.shape[0]

    def inner(j, carry):
        full[here, :] = own[j]
        full[there, :] = own_other[j]
        out[3 + j] = exact_dot(matrix, full[...])
        return carry

    def outer(j, carry):
        full[here, :] = edge[j]
        full[there, :] = edge_other[j]
        out[jnp.where(j < 3, j, j + n)] = exact_dot(matrix, full[...])
        return carry

    lax.fori_loop(0, n, inner, 0)
    lax.fori_loop(0, edge.shape[0], outer, 0)


def solve_kernel(rows, blocks, source, carries, coeff, basis, table_hi, table_lo, phi, phi_edge, solved, levels_hi, levels_lo):
    count = source.shape[0]
    n = count - 5
    columns = source.shape[2]
    width = columns // blocks
    half = basis.shape[0] // 2

    def chunk(i, carry):
        m = pl.ds(pl.multiple_of(i // blocks * rows, rows), rows)
        r = pl.ds(pl.multiple_of(i % blocks * width, width), width)
        rho, kappa, a = coeff[0, m, r], coeff[1, m, r], coeff[2, m, r]
        growth = (2.0 + a) - rho
        f = [source[j, m, r] for j in range(count)]
        c, b = [None] * count, [None] * count
        c[2] = carries[i, 0]
        c[1] = (c[2] - f[2]) * growth
        c[0] = (c[1] - f[1]) * growth
        for j in range(3, count):
            c[j] = f[j] + rho * c[j - 1]
        b[n + 3] = carries[i, 1]
        b[n + 4] = (b[n + 3] - f[n + 3]) * growth
        for j in range(n + 2, -1, -1):
            b[j] = f[j] + rho * b[j + 1]
        values = [kappa * ((c[j] - f[j]) + b[j]) for j in range(count)]
        values.append(f[0] - a * values[0])
        values.append(f[count - 1] - a * values[count - 1])
        for j, value in enumerate(values):
            solved[j, m, r] = value
        return carry

    lax.fori_loop(0, carries.shape[0], chunk, 0)
    first = lax.axis_index("gz") == 0
    share = halves(jnp.where(first, basis[:half, :], basis[half:, :]))

    def plane(j, carry):
        value = split_dot(share, halves(solved[j]))
        here = pl.ds(pl.multiple_of(j * half, half), half)
        levels_hi[here, :], levels_lo[here, :] = halves(value)
        return carry

    lax.fori_loop(0, count + 2, plane, 0)
    result = split_dot((levels_hi[...], levels_lo[...]), (table_hi[...], table_lo[...]))
    result = result.reshape(count + 2, half, columns)
    phi[...] = result[3 : 3 + n]
    phi_edge[0:3] = result[0:3]
    phi_edge[3:7] = result[3 + n :]


WHOLE = pl.BlockSpec(memory_space=pltpu.VMEM)


def params():
    return pltpu.CompilerParams(vmem_limit_bytes=48 * 1024 * 1024)


def cost(us):
    return pl.CostEstimate(flops=int(us * 1e6), bytes_accessed=int(us * 3e6), transcendentals=0)


def call(kernel, outs, *args, scratch=(), us=2.0, name):
    many = isinstance(outs, (list, tuple))
    return pl.pallas_call(
        kernel,
        out_shape=outs,
        in_specs=[WHOLE] * len(args),
        out_specs=[WHOLE] * len(outs) if many else WHOLE,
        scratch_shapes=list(scratch),
        compiler_params=params(),
        cost_estimate=cost(us),
        name=name,
    )(*args)


def by_rows(kernel, outs, *args, us, name):
    levels, columns = args[0].shape[1:]

    def spec(a):
        return pl.BlockSpec((a.shape[0], ROWS, columns), lambda i: (0, i, 0))

    return pl.pallas_call(
        kernel,
        grid=(levels // ROWS,),
        out_shape=outs,
        in_specs=[spec(a) for a in args],
        out_specs=[spec(o) for o in outs],
        compiler_params=params(),
        cost_estimate=cost(us),
        name=name,
    )(*args)


def shards(
    thermal_anomaly,
    saltiness_anomaly,
    eastward_flow,
    advective_ratio,
    dual_thermal_final,
    dual_saltiness_final,
    dual_flow_final,
    dual_kinematic_head,
    depth_into_eigenbasis,
    eigenbasis_into_depth,
    spectral_magnitudes,
):
    t, s, u, c, lt, ls, df, head = (
        jnp.transpose(a, (1, 0, 2))
        for a in (
            thermal_anomaly,
            saltiness_anomaly,
            eastward_flow,
            advective_ratio,
            dual_thermal_final,
            dual_saltiness_final,
            dual_flow_final,
            dual_kinematic_head,
        )
    )
    n, levels, columns = t.shape
    modes = depth_into_eigenbasis.shape[0]
    across = lax.axis_size(ALONG)
    places = lax.axis_size(GROUP)
    rings = lax.axis_size("z")
    chunks = places * lax.axis_size("gz")
    rows = max(ROWS, modes // chunks)
    blocks = chunks * rows // modes
    width = columns // blocks

    def to_right(block):
        return lax.ppermute(block, ALONG, [(i, (i + 1) % across) for i in range(across)])

    def to_left(block):
        return lax.ppermute(block, ALONG, [((i + 1) % across, i) for i in range(across)])

    def other_half(block):
        return lax.ppermute(block, "gz", [(0, 1), (1, 0)])

    def like(*shape):
        return jax.ShapeDtypeStruct(shape, f32)

    exact = hartley_table(columns)
    table = jnp.asarray(exact.astype(np.float32))
    upper = exact.astype(np.float32).astype(jnp.bfloat16)
    table_hi = jnp.asarray(upper)
    table_lo = jnp.asarray((exact - upper.astype(np.float64)).astype(jnp.bfloat16))
    waves = jnp.asarray(
        (2.0 - 2.0 * np.cos(np.arange(columns) * (2.0 * math.pi / columns))).astype(np.float32)
    ).reshape(1, columns)

    head_left = to_right(head[n - 3 :])
    head_right = to_left(head[:2])
    tracer_before = to_right(jnp.concatenate([t[n - 3 :], s[n - 3 :], lt[n - 1 :], ls[n - 1 :]]))
    tracer_after = to_left(jnp.concatenate([t[:2], s[:2]]))
    flow_before = to_right(jnp.concatenate([u[n - 5 :], c[n - 2 :], df[n - 3 :]]))
    flow_after = to_left(jnp.concatenate([u[:5], c[:3], df[:3]]))

    whole = lambda *shape: pl.BlockSpec(shape, lambda j: (0,) * len(shape))
    spec, coeff, sums = pl.pallas_call(
        lambda *refs: moments_kernel(rows, blocks, *refs),
        grid=(n,),
        out_shape=[
            like(n, levels, columns),
            like(3, modes, columns),
            like(chunks, 2, rows, width),
        ],
        in_specs=[
            pl.BlockSpec((1, levels, columns), lambda j: (j, 0, 0)),
            whole(columns, columns),
            whole(modes, modes),
            whole(modes, 1),
            whole(1, columns),
        ],
        out_specs=[
            pl.BlockSpec((1, levels, columns), lambda j: (j, 0, 0)),
            whole(3, modes, columns),
            whole(chunks, 2, rows, width),
        ],
        scratch_shapes=[pltpu.VMEM((modes, columns), f32)] * 3,
        compiler_params=params(),
        cost_estimate=cost(4.0),
        name="block_moments",
    )(head, table, depth_into_eigenbasis, spectral_magnitudes.reshape(modes, 1), waves)
    gathered = lax.all_to_all(sums, GROUP_ALL, 0, 0, tiled=True)
    gathered = gathered.reshape(places, chunks // places, 2, rows, width)
    spec_other = other_half(spec)
    edge = call(halo_kernel, like(5, levels, columns), head_left, head_right, table, us=3.0, name="edge_spectrum")
    edge_other = other_half(edge)

    t_base, s_base, c_base, to_left_part, to_right_part = by_rows(
        tracer_kernel,
        [like(n, levels, columns)] * 3 + [like(6, levels, columns), like(4, levels, columns)],
        t, s, c, lt, ls, tracer_before, tracer_after,
        us=10.0,
        name="tracers",
    )
    from_right = to_left(to_left_part)
    from_left = to_right(to_right_part)

    ring = call(
        lambda *refs: group_kernel(rows, blocks, n, *refs),
        like(rings, 2, rows, width),
        gathered, coeff,
        us=1.0,
        name="group_moments",
    )
    ring = lax.all_to_all(ring, "z", 0, 0, tiled=True)
    carries = call(
        lambda *refs: carry_kernel(rows, blocks, n, *refs),
        like(places, chunks // places, 2, rows, width),
        gathered, ring, coeff,
        us=1.0,
        name="group_carries",
    )
    carries = lax.all_to_all(carries.reshape(chunks, 2, rows, width), GROUP_ALL, 0, 0, tiled=True)

    source = call(
        source_kernel,
        like(n + 5, modes, columns),
        spec, edge, spec_other, edge_other, depth_into_eigenbasis,
        scratch=[pltpu.VMEM((modes, columns), f32)],
        us=4.0,
        name="mode_source",
    )
    phi, phi_edge = call(
        lambda *refs: solve_kernel(rows, blocks, *refs),
        [like(n, levels, columns), like(7, levels, columns)],
        source, carries, coeff, eigenbasis_into_depth, table_hi, table_lo,
        scratch=[pltpu.VMEM((n + 7, modes, columns), f32)]
        + [pltpu.VMEM(((n + 7) * levels, columns), bf16)] * 2,
        us=7.0,
        name="pressure",
    )
    t_bar, s_bar, u_bar, c_bar = by_rows(
        flow_kernel,
        [like(n, levels, columns)] * 4,
        u, c, df, flow_before, flow_after, phi, phi_edge,
        t_base, s_base, c_base, from_left, from_right,
        us=7.0,
        name="flow",
    )
    return tuple(jnp.transpose(a, (1, 0, 2)) for a in (t_bar, s_bar, u_bar, c_bar, phi))


def solution(mesh):
    gx, gz = mesh.shape["gx"], mesh.shape["gz"]
    inner = Mesh(mesh.devices.reshape(SPLIT[gx] + (gz,)), ALONG + ("gz",))
    field = P("gz", ALONG, None)
    return jax.shard_map(
        shards,
        mesh=inner,
        in_specs=(field,) * 8 + (P(),) * 3,
        out_specs=(field,) * 5,
        check_vma=False,
    )
```

time: 411 us -> 142 us (0.35)
  the two profiles are of different devices: /device:TPU:23 before, /device:TPU:32 now
where the time goes in v1:
time: 142 us; the launch traced here: 140 us
  Pallas kernels  45.1 us (32%)
  starting transfers between devices  40.7 us (29%)
  waiting for transfers between devices  29.1 us (20%)
  local copies, waits for them, and re-layouts  20 us (14%)
  other arithmetic  4.42 us (3%)
    pallas_call x2, Pallas kernels, by_rows(): pl.pallas_call(kernel, grid=(levels // ROWS,), out_shape=outs, in_specs=[...  20.1 us
    pallas_call x5, Pallas kernels, call(): pl.pallas_call(kernel, out_shape=outs, in_specs=[WHOLE] * len(args), out_...  17.2 us
    ppermute x4, starting transfers between devices, to_left(): lax.ppermute(block, ALONG, [((i + 1) % across, i) for i in range(across)])  17.1 us
    unnamed x66, local copies, waits for them, and re-layouts  16.2 us
    ppermute x2, waiting for transfers between devices, other_half(): return lax.ppermute(block, 'gz', [(0, 1), (1, 0)])  15.3 us
    all_to_all x1, waiting for transfers between devices, shards(): gathered = lax.all_to_all(sums, GROUP_ALL, 0, 0, tiled=True)  8.66 us
    all_to_all x1, starting transfers between devices, shards(): ring = lax.all_to_all(ring, 'z', 0, 0, tiled=True)  8.57 us
    all_to_all x1, starting transfers between devices, shards(): gathered = lax.all_to_all(sums, GROUP_ALL, 0, 0, tiled=True)  8.38 us
  transfers between devices with their start and end apart: 13, of which 3 were waited for; matrix products, arithmetic and copies ran while one was open for 5% of the time, Pallas kernels for 19%

profile of v1, /device:TPU:32, one launch (start us, length us, event | category | flops | bytes accessed | tf_op | source)
XLA Modules:
  0.0 140.3 jit_solution(1142432774166006908)
XLA Ops:
  0.6 0.8 copy.20.refs_3_
  1.4 1.2 copy-done.6
  2.6 1.1 copy-done.10
  3.8 0.8 copy-done.27
  4.6 0.7 copy-done.32
  5.3 7.7 %block_moments.1 = (f32[6,64,512]{2,1,0:T(8,128)}, f32[3,128,512]{2,1,0:T(8,128)S(1)}, f32[32,2,8,256]{3,2,1,0:T(8,128)}) custom-call(f32[6,64,512]{2,1,0:T(8,128)S(1)} %bitcast.26, f32[512,512]{1,0:T(8,128)S(1)} %copy-done.6, f32[128,128]{1,0:T(8,128)S(1)} %copy-done.27, f32[128,1]{1,0:T(8,128)S(1)} %copy.20.refs_3_, f32[1,512]{1,0:T(1,128)S(1)} %copy-done.32), custom_call_target="tpu_custom_call" | custom-call | flops 4000000 | bytes 12000000 | tf_op jit(solution)/shard_map/block_moments/pallas_call | solution.py:490
  13.0 1.6 %collective-permute-start.4 = (f32[6,64,512]{2,1,0:T(8,128)}, f32[6,64,512]{2,1,0:T(8,128)}, u32[]{:S(2)}, u32[]{:S(2)}) collective-permute-start(f32[6,64,512]{2,1,0:T(8,128)} %get-tuple-element.19.own), channel_id=1, source_target_pairs={{0,1},{1,0},{2,3},{3,2},{4,5},{5,4},{6,7},{7,6},{8,9},{9,8},{10,11... | collective-permute-start | bytes 2359304 | tf_op jit(solution)/shard_map/ppermute | solution.py:468
  14.7 0.9 slice.66
  15.6 0.9 slice.67
  16.5 1.1 pad_maximum_fusion.2
  17.6 0.0 collective-permute-start.6
  17.6 0.8 pad_maximum_fusion.3
  18.5 6.3 %collective-permute-start.7 = (f32[4,64,512]{2,1,0:T(8,128)}, f32[4,64,512]{2,1,0:T(8,128)S(1)}, u32[]{:S(2)}, u32[]{:S(2)}) collective-permute-start(f32[4,64,512]{2,1,0:T(8,128)} %pad_maximum_fusion.3), channel_id=1, source_target_pairs={{2,0},{4,2},{6,4},{8,6},{10,8},{12,10},{14,12},{16,14},{18,16},{20... | collective-permute-start | bytes 1572872 | tf_op jit(solution)/shard_map/ppermute | solution.py:465
  24.8 0.1 fusion.1
  24.8 0.1 fusion
  25.0 1.3 pad_maximum_fusion
  26.3 1.0 collective-permute-start.1
  27.3 0.0 copy-start.11
  27.3 1.2 pad_maximum_fusion.1
  28.6 0.0 collective-permute-start
  28.6 8.4 %all-to-all-start = ((f32[32,2,8,256]{3,2,1,0:T(8,128)}), f32[32,2,8,256]{3,2,1,0:T(8,128)S(1)}, u32[]{:S(2)}, u32[]{:S(2)}) async-start(f32[32,2,8,256]{3,2,1,0:T(8,128)} %get-tuple-element.20), calls=%async_computation | async-start | bytes 1048576 | tf_op jit(solution)/shard_map/all_to_all | solution.py:515
  37.0 0.0 copy-start.14
  37.0 0.8 slice.62
  37.8 0.0 collective-permute-done.7.after
  37.8 0.3 collective-permute-start.2
  38.1 0.0 collective-permute-done.6.before
  38.1 6.1 %collective-permute-start.3 = (f32[2,64,512]{2,1,0:T(8,128)S(1)}, f32[2,64,512]{2,1,0:T(8,128)S(1)}, u32[]{:S(2)}, u32[]{:S(2)}) collective-permute-start(f32[2,64,512]{2,1,0:T(8,128)S(1)} %slice.63), channel_id=1, source_target_pairs={{2,0},{4,2},{6,4},{8,6},{10,8},{12,10},{14,12},{16,14},{18,16},{20... | collective-permute-start | bytes 786440 | tf_op jit(solution)/shard_map/ppermute | solution.py:465
  44.2 10.1 %tracers.1 = (f32[6,64,512]{2,1,0:T(8,128)S(1)}, f32[6,64,512]{2,1,0:T(8,128)S(1)}, f32[6,64,512]{2,1,0:T(8,128)S(1)}, f32[6,64,512]{2,1,0:T(8,128)}, f32[4,64,512]{2,1,0:T(8,128)}) custom-call(f32[6,64,512]{2,1,0:T(8,128)S(1)} %bitcast.31, f32[6,64,512]{2,1,0:T(8,128)S(1)} %bitcast.34, f32[6,64,512]{2,1,0:T(8,128)} %bitcast.16, f32[6,64,512]{2,1,0:T(8,128)} %bitcast.37, ...), custom_call_target="tpu_custom_call" | custom-call | flops 10000000 | bytes 30000000 | tf_op jit(solution)/shard_map/tracers/pallas_call | solution.py:413
  54.2 0.9 copy-done.16
  55.1 0.9 copy-done.18
  56.0 0.9 copy-done.20
  56.9 0.0 collective-permute-done.3.right
  56.9 0.7 copy-done.29
  57.6 3.8 %collective-permute-start.9 = (f32[6,64,512]{2,1,0:T(8,128)}, f32[6,64,512]{2,1,0:T(8,128)}, u32[]{:S(2)}, u32[]{:S(2)}) collective-permute-start(f32[6,64,512]{2,1,0:T(8,128)} %get-tuple-element.28), channel_id=1, source_target_pairs={{2,0},{4,2},{6,4},{8,6},{10,8},{12,10},{14,12},{16,14},{18,16},{20... | collective-permute-start | bytes 2359304 | tf_op jit(solution)/shard_map/ppermute | solution.py:465
  61.4 8.7 %all-to-all-done = f32[32,2,8,256]{3,2,1,0:T(8,128)S(1)} async-done(((f32[32,2,8,256]{3,2,1,0:T(8,128)}), f32[32,2,8,256]{3,2,1,0:T(8,128)S(1)}, u32[]{:S(2)}, u32[]{:S(2)}) %all-to-all-start) | async-done | bytes 524320 | tf_op jit(solution)/shard_map/all_to_all | solution.py:515
  70.1 0.7 group_moments.1
  70.8 8.6 %all-to-all-start.1 = ((f32[8,2,8,256]{3,2,1,0:T(8,128)}), f32[8,2,8,256]{3,2,1,0:T(8,128)S(1)}, u32[]{:S(2)}, u32[]{:S(2)}) async-start(f32[8,2,8,256]{3,2,1,0:T(8,128)} %group_moments.1), calls=%async_computation.1 | async-start | bytes 262144 | tf_op jit(solution)/shard_map/all_to_all | solution.py:538
  79.3 0.0 collective-permute-done.2.left
  79.4 2.2 %edge_spectrum.1.edge = f32[5,64,512]{2,1,0:T(8,128)S(1)} custom-call(f32[3,64,512]{2,1,0:T(8,128)} %collective-permute-done.2.left, f32[2,64,512]{2,1,0:T(8,128)S(1)} %copy-done.30, f32[512,512]{1,0:T(8,128)S(1)} %copy-done.7), custom_call_target="tpu_custom_call" | custom-call | flops 3000000 | bytes 9000000 | tf_op jit(solution)/shard_map/edge_spectrum/pallas_call | solution.py:395
  81.6 0.2 collective-permute-start.5
  81.8 0.0 collective-permute-done.4.own_other
  81.8 0.0 collective-permute-start.8
  81.8 5.1 %all-to-all-done.1.refs_1_ = f32[8,2,8,256]{3,2,1,0:T(8,128)S(1)} async-done(((f32[8,2,8,256]{3,2,1,0:T(8,128)}), f32[8,2,8,256]{3,2,1,0:T(8,128)S(1)}, u32[]{:S(2)}, u32[]{:S(2)}) %all-to-all-start.1) | async-done | bytes 131104 | tf_op jit(solution)/shard_map/all_to_all | solution.py:538
  87.0 0.8 group_carries.1
  87.8 4.6 %all-to-all-start.2 = ((f32[32,2,8,256]{3,2,1,0:T(8,128)}), f32[32,2,8,256]{3,2,1,0:T(8,128)}, u32[]{:S(2)}, u32[]{:S(2)}) async-start(f32[32,2,8,256]{3,2,1,0:T(8,128)} %bitcast.6), calls=%async_computation.2 | async-start | bytes 1048576 | tf_op jit(solution)/shard_map/all_to_all | solution.py:546
  92.4 15.3 %collective-permute-done.5.edge_other = f32[5,64,512]{2,1,0:T(8,128)S(1)} collective-permute-done((f32[5,64,512]{2,1,0:T(8,128)S(1)}, f32[5,64,512]{2,1,0:T(8,128)S(1)}, u32[]{:S(2)}, u32[]{:S(2)}) %collective-permute-start.5) | collective-permute-done | bytes 655392 | tf_op jit(solution)/shard_map/ppermute | solution.py:468
  107.8 0.8 copy-done.23
  108.6 1.1 copy-done.24
  109.7 0.8 copy-done.28
  110.5 6.1 %mode_source.1.refs_0_ = f32[11,128,512]{2,1,0:T(8,128)S(1)} custom-call(f32[6,64,512]{2,1,0:T(8,128)} %get-tuple-element.19.own, f32[5,64,512]{2,1,0:T(8,128)S(1)} %edge_spectrum.1.edge, f32[6,64,512]{2,1,0:T(8,128)} %collective-permute-done.4.own_other, f32[5,64,512]{2,1,0:T(8,128)S(1)} %copy-done.24, f32[128,128]{1,0:T(8,128)S(1)} %copy-done.28), custom_call_target="tpu_custom_call" | custom-call | flops 4000000 | bytes 12000000 | tf_op jit(solution)/shard_map/mode_source/pallas_call | solution.py:395
  116.6 0.0 all-to-all-done.2.refs_1_
  116.6 0.0 copy-start.1
  116.6 1.1 copy-done.1
  117.7 1.0 copy-done.25
  118.8 1.0 copy-done.26
  119.8 0.8 copy-done.31
  120.7 7.4 %pressure.1 = (f32[6,64,512]{2,1,0:T(8,128)}, f32[7,64,512]{2,1,0:T(8,128)S(1)}) custom-call(f32[11,128,512]{2,1,0:T(8,128)S(1)} %mode_source.1.refs_0_, f32[32,2,8,256]{3,2,1,0:T(8,128)} %all-to-all-done.2.refs_1_, f32[3,128,512]{2,1,0:T(8,128)S(1)} %copy-done.1, f32[128,128]{1,0:T(8,128)S(1)} %copy-done.31, bf16[512,512]{1,0:T(8,128)(2,1)S(1)} %copy-done.26, ...), custom_call_target="tpu_custom_call" | custom-call | flops 7000000 | bytes 21000000 | tf_op jit(solution)/shard_map/pressure/pallas_call | solution.py:395
  128.1 0.9 copy-done.15
  129.0 0.0 collective-permute-done.before
  129.0 0.0 collective-permute-done.8.from_left
  129.0 0.0 collective-permute-done.9.from_right
  129.1 0.0 copy-start.22
  129.1 1.1 copy-done.22
  130.2 10.1 %flow.1 = (f32[6,64,512]{2,1,0:T(8,128)}, f32[6,64,512]{2,1,0:T(8,128)}, f32[6,64,512]{2,1,0:T(8,128)}, f32[6,64,512]{2,1,0:T(8,128)}) custom-call(f32[6,64,512]{2,1,0:T(8,128)S(1)} %bitcast.21, f32[6,64,512]{2,1,0:T(8,128)S(1)} %bitcast.19, f32[6,64,512]{2,1,0:T(8,128)S(1)} %bitcast.25, f32[10,64,512]{2,1,0:T(8,128)} %collective-permute-done.before, ...), custom_call_target="tpu_custom_call" | custom-call | flops 7000000 | bytes 21000000 | tf_op jit(solution)/shard_map/flow/pallas_call | solution.py:413
  (53 shorter events, 0.2 us)
Async XLA Ops:
  1.4 1.2 copy-start.6
  2.6 1.1 copy-start.10
  3.8 0.8 copy-start.27
  4.6 0.7 copy-start.32
  5.3 9.3 %copy-start.12 = (f32[64,6,512]{2,0,1:T(8,128)S(1)}, f32[64,6,512]{2,0,1:T(8,128)}, u32[]{:S(2)}) copy-start(f32[64,6,512]{2,0,1:T(8,128)} %param.15) | copy-start | bytes 2359300
  5.3 9.3 %copy-start.13 = (f32[64,6,512]{2,0,1:T(8,128)S(1)}, f32[64,6,512]{2,0,1:T(8,128)}, u32[]{:S(2)}) copy-start(f32[64,6,512]{2,0,1:T(8,128)} %param.16) | copy-start | bytes 2359300
  13.0 74.0 %copy-start = (f32[3,128,512]{2,1,0:T(8,128)}, f32[3,128,512]{2,1,0:T(8,128)S(1)}, u32[]{:S(2)}) copy-start(f32[3,128,512]{2,1,0:T(8,128)S(1)} %get-tuple-element.21.refs_1_.refs_2_) | copy-start | bytes 2359300
  13.0 68.8 %collective-permute-start.4 = (f32[6,64,512]{2,1,0:T(8,128)}, f32[6,64,512]{2,1,0:T(8,128)}, u32[]{:S(2)}, u32[]{:S(2)}) collective-permute-start(f32[6,64,512]{2,1,0:T(8,128)} %get-tuple-element.19.own), channel_id=1, source_target_pairs={{0,1},{1,0},{2,3},{3,2},{4,5},{5,4},{6,7},{7,6},{8,9},{9,8},{10,11... | collective-permute-start | bytes 2359304 | tf_op jit(solution)/shard_map/ppermute | solution.py:468
  17.6 7.2 %copy-start.2 = (f32[64,6,512]{2,0,1:T(8,128)S(1)}, f32[64,6,512]{2,0,1:T(8,128)}, u32[]{:S(2)}) copy-start(f32[64,6,512]{2,0,1:T(8,128)} %param.18) | copy-start | bytes 2359300
  17.6 7.2 %copy-start.8 = (f32[64,6,512]{2,0,1:T(8,128)S(1)}, f32[64,6,512]{2,0,1:T(8,128)}, u32[]{:S(2)}) copy-start(f32[64,6,512]{2,0,1:T(8,128)} %param.21) | copy-start | bytes 2359300
  17.6 20.5 %collective-permute-start.6 = (f32[8,64,512]{2,1,0:T(8,128)}, f32[8,64,512]{2,1,0:T(8,128)}, u32[]{:S(2)}, u32[]{:S(2)}) collective-permute-start(f32[8,64,512]{2,1,0:T(8,128)} %pad_maximum_fusion.2), channel_id=1, source_target_pairs={{0,2},{2,4},{4,6},{6,8},{8,10},{10,12},{12,14},{14,16},{16,18},{18... | collective-permute-start | bytes 3145736 | tf_op jit(solution)/shard_map/ppermute | solution.py:462
  18.5 6.4 %copy-start.4 = (f32[64,6,512]{2,0,1:T(8,128)S(1)}, f32[64,6,512]{2,0,1:T(8,128)}, u32[]{:S(2)}) copy-start(f32[64,6,512]{2,0,1:T(8,128)} %param.17) | copy-start | bytes 2359300
  18.5 19.3 %collective-permute-start.7 = (f32[4,64,512]{2,1,0:T(8,128)}, f32[4,64,512]{2,1,0:T(8,128)S(1)}, u32[]{:S(2)}, u32[]{:S(2)}) collective-permute-start(f32[4,64,512]{2,1,0:T(8,128)} %pad_maximum_fusion.3), channel_id=1, source_target_pairs={{2,0},{4,2},{6,4},{8,6},{10,8},{12,10},{14,12},{16,14},{18,16},{20... | collective-permute-start | bytes 1572872 | tf_op jit(solution)/shard_map/ppermute | solution.py:465
  26.3 102.7 %collective-permute-start.1 = (f32[11,64,512]{2,1,0:T(8,128)}, f32[11,64,512]{2,1,0:T(8,128)}, u32[]{:S(2)}, u32[]{:S(2)}) collective-permute-start(f32[11,64,512]{2,1,0:T(8,128)} %pad_maximum_fusion), channel_id=1, source_target_pairs={{2,0},{4,2},{6,4},{8,6},{10,8},{12,10},{14,12},{16,14},{18,16},{20... | collective-permute-start | bytes 4325384 | tf_op jit(solution)/shard_map/ppermute | solution.py:465
  27.3 9.6 %copy-start.11 = (f32[64,6,512]{2,0,1:T(8,128)S(1)}, f32[64,6,512]{2,0,1:T(8,128)}, u32[]{:S(2)}) copy-start(f32[64,6,512]{2,0,1:T(8,128)} %param.22) | copy-start | bytes 2359300
  28.6 100.4 %collective-permute-start = (f32[10,64,512]{2,1,0:T(8,128)}, f32[10,64,512]{2,1,0:T(8,128)}, u32[]{:S(2)}, u32[]{:S(2)}) collective-permute-start(f32[10,64,512]{2,1,0:T(8,128)} %pad_maximum_fusion.1), channel_id=1, source_target_pairs={{0,2},{2,4},{4,6},{6,8},{8,10},{10,12},{12,14},{14,16},{16,18},{18... | collective-permute-start | bytes 3932168 | tf_op jit(solution)/shard_map/ppermute | solution.py:462
  28.6 41.5 %all-to-all-start = ((f32[32,2,8,256]{3,2,1,0:T(8,128)}), f32[32,2,8,256]{3,2,1,0:T(8,128)S(1)}, u32[]{:S(2)}, u32[]{:S(2)}) async-start(f32[32,2,8,256]{3,2,1,0:T(8,128)} %get-tuple-element.20), calls=%async_computation | async-start | bytes 1048576 | tf_op jit(solution)/shard_map/all_to_all | solution.py:515
  37.0 7.2 %copy-start.14 = (f32[64,6,512]{2,0,1:T(8,128)S(1)}, f32[64,6,512]{2,0,1:T(8,128)}, u32[]{:S(2)}) copy-start(f32[64,6,512]{2,0,1:T(8,128)} %param.16) | copy-start | bytes 2359300
  37.8 41.6 %collective-permute-start.2 = (f32[3,64,512]{2,1,0:T(8,128)}, f32[3,64,512]{2,1,0:T(8,128)}, u32[]{:S(2)}, u32[]{:S(2)}) collective-permute-start(f32[3,64,512]{2,1,0:T(8,128)} %slice.62), channel_id=1, source_target_pairs={{0,2},{2,4},{4,6},{6,8},{8,10},{10,12},{12,14},{14,16},{16,18},{18... | collective-permute-start | bytes 1179656 | tf_op jit(solution)/shard_map/ppermute | solution.py:462
  38.1 18.8 %collective-permute-start.3 = (f32[2,64,512]{2,1,0:T(8,128)S(1)}, f32[2,64,512]{2,1,0:T(8,128)S(1)}, u32[]{:S(2)}, u32[]{:S(2)}) collective-permute-start(f32[2,64,512]{2,1,0:T(8,128)S(1)} %slice.63), channel_id=1, source_target_pairs={{2,0},{4,2},{6,4},{8,6},{10,8},{12,10},{14,12},{16,14},{18,16},{20... | collective-permute-start | bytes 786440 | tf_op jit(solution)/shard_map/ppermute | solution.py:465
  54.2 0.9 copy-start.16
  55.1 0.9 copy-start.18
  56.0 0.9 copy-start.20
  56.9 22.4 %copy-start.7 = (f32[512,512]{1,0:T(8,128)S(1)}, f32[512,512]{1,0:T(8,128)}, u32[]{:S(2)}) copy-start(f32[512,512]{1,0:T(8,128)} %constant.8.clone.refs_1_.table) | copy-start | bytes 3145732
  56.9 0.7 copy-start.29
  57.6 21.7 %copy-start.30 = (f32[2,64,512]{2,1,0:T(8,128)S(1)}, f32[2,64,512]{2,1,0:T(8,128)}, u32[]{:S(2)}) copy-start(f32[2,64,512]{2,1,0:T(8,128)} %copy-done.29) | copy-start | bytes 786436
  57.6 71.4 %collective-permute-start.9 = (f32[6,64,512]{2,1,0:T(8,128)}, f32[6,64,512]{2,1,0:T(8,128)}, u32[]{:S(2)}, u32[]{:S(2)}) collective-permute-start(f32[6,64,512]{2,1,0:T(8,128)} %get-tuple-element.28), channel_id=1, source_target_pairs={{2,0},{4,2},{6,4},{8,6},{10,8},{12,10},{14,12},{16,14},{18,16},{20... | collective-permute-start | bytes 2359304 | tf_op jit(solution)/shard_map/ppermute | solution.py:465
  70.8 16.2 %all-to-all-start.1 = ((f32[8,2,8,256]{3,2,1,0:T(8,128)}), f32[8,2,8,256]{3,2,1,0:T(8,128)S(1)}, u32[]{:S(2)}, u32[]{:S(2)}) async-start(f32[8,2,8,256]{3,2,1,0:T(8,128)} %group_moments.1), calls=%async_computation.1 | async-start | bytes 262144 | tf_op jit(solution)/shard_map/all_to_all | solution.py:538
  81.6 26.2 %collective-permute-start.5 = (f32[5,64,512]{2,1,0:T(8,128)S(1)}, f32[5,64,512]{2,1,0:T(8,128)S(1)}, u32[]{:S(2)}, u32[]{:S(2)}) collective-permute-start(f32[5,64,512]{2,1,0:T(8,128)S(1)} %edge_spectrum.1.edge), channel_id=1, source_target_pairs={{0,1},{1,0},{2,3},{3,2},{4,5},{5,4},{6,7},{7,6},{8,9},{9,8},{10,11... | collective-permute-start | bytes 1966088 | tf_op jit(solution)/shard_map/ppermute | solution.py:468
  81.8 47.2 %collective-permute-start.8 = (f32[4,64,512]{2,1,0:T(8,128)}, f32[4,64,512]{2,1,0:T(8,128)}, u32[]{:S(2)}, u32[]{:S(2)}) collective-permute-start(f32[4,64,512]{2,1,0:T(8,128)} %get-tuple-element.27), channel_id=1, source_target_pairs={{0,2},{2,4},{4,6},{6,8},{8,10},{10,12},{12,14},{14,16},{16,18},{18... | collective-permute-start | bytes 1572872 | tf_op jit(solution)/shard_map/ppermute | solution.py:462
  87.8 28.8 %all-to-all-start.2 = ((f32[32,2,8,256]{3,2,1,0:T(8,128)}), f32[32,2,8,256]{3,2,1,0:T(8,128)}, u32[]{:S(2)}, u32[]{:S(2)}) async-start(f32[32,2,8,256]{3,2,1,0:T(8,128)} %bitcast.6), calls=%async_computation.2 | async-start | bytes 1048576 | tf_op jit(solution)/shard_map/all_to_all | solution.py:546
  107.8 0.8 copy-start.23
  108.6 1.1 copy-start.24
  109.7 0.8 copy-start.28
  116.6 1.1 copy-start.1
  117.7 1.0 copy-start.25
  118.8 1.0 copy-start.26
  119.8 0.8 copy-start.31
  120.7 8.4 %copy-start.3 = (f32[64,6,512]{2,0,1:T(8,128)S(1)}, f32[64,6,512]{2,0,1:T(8,128)}, u32[]{:S(2)}) copy-start(f32[64,6,512]{2,0,1:T(8,128)} %param.18) | copy-start | bytes 2359300
  120.7 8.4 %copy-start.5 = (f32[64,6,512]{2,0,1:T(8,128)S(1)}, f32[64,6,512]{2,0,1:T(8,128)}, u32[]{:S(2)}) copy-start(f32[64,6,512]{2,0,1:T(8,128)} %param.17) | copy-start | bytes 2359300
  120.7 8.4 %copy-start.9 = (f32[64,6,512]{2,0,1:T(8,128)S(1)}, f32[64,6,512]{2,0,1:T(8,128)}, u32[]{:S(2)}) copy-start(f32[64,6,512]{2,0,1:T(8,128)} %param.21) | copy-start | bytes 2359300
  120.7 8.4 %copy-start.17 = (f32[6,64,512]{2,1,0:T(8,128)S(1)}, f32[6,64,512]{2,1,0:T(8,128)}, u32[]{:S(2)}) copy-start(f32[6,64,512]{2,1,0:T(8,128)} %copy-done.16) | copy-start | bytes 2359300
  120.7 8.4 %copy-start.19 = (f32[6,64,512]{2,1,0:T(8,128)S(1)}, f32[6,64,512]{2,1,0:T(8,128)}, u32[]{:S(2)}) copy-start(f32[6,64,512]{2,1,0:T(8,128)} %copy-done.18) | copy-start | bytes 2359300
  120.7 8.4 %copy-start.21 = (f32[6,64,512]{2,1,0:T(8,128)S(1)}, f32[6,64,512]{2,1,0:T(8,128)}, u32[]{:S(2)}) copy-start(f32[6,64,512]{2,1,0:T(8,128)} %copy-done.20) | copy-start | bytes 2359300
  128.1 0.9 copy-start.15
  129.1 1.1 copy-start.22

commit v2 on v1

--- a/solution.py
+++ b/solution.py
@@ -10,7 +10,6 @@
 
 f32 = jnp.float32
 bf16 = jnp.bfloat16
-highest = lax.Precision.HIGHEST
 LANES = 128
 ROWS = 8
 SPLIT = {128: (8, 2, 4, 2)}
@@ -30,8 +29,12 @@
     return upper, (value - upper.astype(f32)).astype(bf16)
 
 
-def exact_dot(a, b):
-    return jnp.dot(a, b, precision=highest, preferred_element_type=f32)
+def thrice_left(pair):
+    return jnp.concatenate([pair[0], pair[0], pair[1]], axis=1)
+
+
+def thrice_right(pair):
+    return jnp.concatenate([pair[0], pair[1], pair[0]], axis=0)
 
 
 def split_dot(a, b):
@@ -41,11 +44,6 @@
         return jnp.dot(p, q, preferred_element_type=f32)
 
     return dot(a_hi, b_hi) + (dot(a_hi, b_lo) + dot(a_lo, b_hi))
-
-
-def inverse(value):
-    guess = pl.reciprocal(value, approx=True)
-    return guess * (2.0 - value * guess)
 
 
 def face_terms(edges, ratio):
@@ -57,11 +55,11 @@
     s1, s2, s3 = d2 - d1, d3 - d2, d4 - d3
     e0, e1, e2 = (d2 + d2) + s1, d2 + d3, (d3 + d3) - s3
     t0, t1, t2 = (13.0 / 3.0) * s1, (13.0 / 3.0) * s2, (13.0 / 3.0) * s3
-    r0 = inverse(t0 * s1 + (e0 * e0 + 0.04))
-    r1 = inverse(t1 * s2 + (e1 * e1 + 0.04))
-    r2 = inverse(t2 * s3 + (e2 * e2 + 0.04))
+    r0 = 1.0 / (t0 * s1 + (e0 * e0 + 0.04))
+    r1 = 1.0 / (t1 * s2 + (e1 * e1 + 0.04))
+    r2 = 1.0 / (t2 * s3 + (e2 * e2 + 0.04))
     u0, u1, u2 = (1.0 / 6.0) * (r0 * r0), r1 * r1, 0.5 * (r2 * r2)
-    norm = inverse(u0 + u1 + u2)
+    norm = 1.0 / (u0 + u1 + u2)
     w0, w1, w2 = u0 * norm, u1 * norm, u2 * norm
     bend = s1 - s2
     a2, cc = bend + bend, s2 - s3
@@ -71,12 +69,12 @@
     p0, q0 = n0 * t0, n0 * e0
     p1, q1 = n1 * t1, n1 * e1
     p2, q2 = n2 * t2, n2 * e2
-    left, right = p0 + q0, q2 - p2
-    g1 = -(0.5 * w0 + left)
-    g2 = (1.25 * w0 + 0.25 * w1) + (left + (q0 + q0)) + (q1 - p1)
-    g3 = (0.5 * w1 + w2) + (right + (q2 + q2)) + (p1 + q1)
-    g4 = -(0.25 * w2 + right)
-    return positive, total, (g1, g2, g3, g4)
+    h0, h2 = 0.5 * w0, 0.25 * w2
+    lean = h0 - h2
+    m1, m4 = h0 + (p0 + q0), h2 + (q2 - p2)
+    g2 = ((0.25 + lean) + m1) + ((q0 + q0) + (q1 - p1))
+    g3 = ((0.5 - lean) + m4) + ((q2 + q2) + (p1 + q1))
+    return positive, total, (m1, g2, g3, m4)
 
 
 def weno_tile(field, ratio, cotangent, faces, cells, owned):
@@ -87,20 +85,23 @@
             edge_of[x] = field(x + 1) - field(x)
         return edge_of[x]
 
-    def add(store, key, value):
-        store[key] = store[key] + value if key in store else value
+    def add(store, key, value, less=False):
+        if key in store:
+            store[key] = store[key] - value if less else store[key] + value
+        else:
+            store[key] = -value if less else value
 
     for f in faces:
         c, e = ratio(f), cotangent(f)
-        positive, total, (g1, g2, g3, g4) = face_terms([edge(f - 3 + k) for k in range(5)], c)
+        positive, total, (m1, g2, g3, m4) = face_terms([edge(f - 3 + k) for k in range(5)], c)
         gain = (2.0 / 3.0) * (jnp.abs(c) * e)
-        g1, g2, g3, g4 = gain * g1, gain * g2, gain * g3, gain * g4
-        zero = jnp.zeros_like(g1)
-        add(edge_bar, f - 3, jnp.where(positive, g1, zero))
-        add(edge_bar, f - 2, jnp.where(positive, g2, g4))
+        m1, g2, g3, m4 = gain * m1, gain * g2, gain * g3, gain * m4
+        zero = jnp.zeros_like(m1)
+        add(edge_bar, f - 3, jnp.where(positive, m1, zero), True)
+        add(edge_bar, f - 2, jnp.where(positive, g2, -m4))
         add(edge_bar, f - 1, g3)
-        add(edge_bar, f, jnp.where(positive, g4, g2))
-        add(edge_bar, f + 1, jnp.where(positive, zero, g1))
+        add(edge_bar, f, jnp.where(positive, -m4, g2))
+        add(edge_bar, f + 1, jnp.where(positive, zero, m1), True)
         add(cell_bar, f - 1, jnp.maximum(c, 0.0) * e)
         add(cell_bar, f, jnp.minimum(c, 0.0) * e)
         if f in owned:
@@ -207,46 +208,87 @@
     lax.fori_loop(0, width // LANES, tile, 0)
 
 
-def moments_kernel(rows, blocks, head, table, depth, rates, waves, spec, coeff, sums, a_acc, b_acc, power):
-    j, last = pl.program_id(0), pl.num_programs(0) - 1
-    half = depth.shape[1] // 2
-    columns = table.shape[1]
+def moments_kernel(rows, blocks, head, table_hi, table_lo, depth, rates, waves, u, c, df, spec, coeff, sums, flow_right, flow_left, sems):
+    n, levels, columns = head.shape
     width = columns // blocks
-
-    @pl.when(j == 0)
-    def _():
-        a = rates[...] + waves[...]
-        root = jnp.sqrt(a * (1.0 + 0.25 * a))
-        rho = 1.0 / ((1.0 + 0.5 * a) + root)
-        coeff[0] = rho
-        coeff[1] = 0.5 / root
-        coeff[2] = a
-        a_acc[...] = jnp.zeros_like(a_acc)
-        b_acc[...] = jnp.zeros_like(b_acc)
-        power[...] = jnp.ones_like(power)
-
-    values = exact_dot(head[0], table[...])
-    spec[0] = values
+    copies = [
+        pltpu.make_async_copy(source, target, sems.at[k])
+        for k, (source, target) in enumerate(
+            (
+                (u.at[n - 5 : n], flow_right.at[0:5]),
+                (c.at[n - 2 : n], flow_right.at[5:7]),
+                (df.at[n - 3 : n], flow_right.at[7:10]),
+                (u.at[0:5], flow_left.at[0:5]),
+                (c.at[0:3], flow_left.at[5:8]),
+                (df.at[0:3], flow_left.at[8:11]),
+            )
+        )
+    ]
+    for copy in copies:
+        copy.start()
+    a = jnp.transpose(jnp.broadcast_to(rates[...], (columns, rates.shape[1]))) + waves[...]
+    root = jnp.sqrt(a * (1.0 + 0.25 * a))
+    rho = 1.0 / ((1.0 + 0.5 * a) + root)
+    coeff[0] = rho
+    coeff[1] = 0.5 / root
+    coeff[2] = a
+    values = head[...].reshape(n * levels, columns)
+    values = split_dot(halves(values), (table_hi[...], table_lo[...]))
+    spec[...] = values.reshape(n, levels, columns)
     first = lax.axis_index("gz") == 0
-    share = jnp.where(first, depth[:, :half], depth[:, half:])
-    part = exact_dot(share * (-1.0 / columns), values)
-    rho = coeff[0]
-    a_acc[...] = a_acc[...] * rho + part
-    b_acc[...] = b_acc[...] + power[...] * part
-    power[...] = power[...] * rho
-
-    @pl.when(j == last)
-    def _():
-        for n in range(sums.shape[0]):
-            m, r = n // blocks * rows, n % blocks * width
-            sums[n, 0] = a_acc[m : m + rows, r : r + width]
-            sums[n, 1] = b_acc[m : m + rows, r : r + width]
-
-
-def halo_kernel(left, right, table, spec):
-    value = jnp.concatenate([left[...], right[...]], axis=0)
-    count, levels, columns = value.shape
-    spec[...] = exact_dot(value.reshape(count * levels, columns), table[...]).reshape(value.shape)
+    share = jnp.where(first, depth[:, :levels], depth[:, levels:])
+    share = thrice_left(halves(share * (-1.0 / columns)))
+    for j in range(n):
+        part = jnp.dot(share, thrice_right(halves(spec[j])), preferred_element_type=f32)
+        if j == 0:
+            forward, backward, power = part, part, coeff[0]
+        else:
+            forward = forward * coeff[0] + part
+            backward = backward + power * part
+            power = power * coeff[0]
+    for i in range(sums.shape[0]):
+        m, r = i // blocks * rows, i % blocks * width
+        sums[i, 0] = forward[m : m + rows, r : r + width]
+        sums[i, 1] = backward[m : m + rows, r : r + width]
+    for copy in copies:
+        copy.wait()
+
+
+def pack_kernel(head, t, s, lt, ls, right, left, sems):
+    n = head.shape[0]
+    copies = [
+        pltpu.make_async_copy(source, target, sems.at[k])
+        for k, (source, target) in enumerate(
+            (
+                (t.at[n - 3 : n], right.at[0:3]),
+                (s.at[n - 3 : n], right.at[3:6]),
+                (lt.at[n - 1 : n], right.at[6:7]),
+                (ls.at[n - 1 : n], right.at[7:8]),
+                (head.at[n - 3 : n], right.at[8:11]),
+                (t.at[0:2], left.at[0:2]),
+                (s.at[0:2], left.at[2:4]),
+                (head.at[0:2], left.at[4:6]),
+            )
+        )
+    ]
+    for copy in copies:
+        copy.start()
+    for copy in copies:
+        copy.wait()
+
+
+def halo_kernel(before, after, table_hi, table_lo, spec, planes, sems):
+    copies = [
+        pltpu.make_async_copy(before.at[8:11], planes.at[0:3], sems.at[0]),
+        pltpu.make_async_copy(after.at[4:6], planes.at[3:5], sems.at[1]),
+    ]
+    for copy in copies:
+        copy.start()
+    for copy in copies:
+        copy.wait()
+    count, levels, columns = planes.shape
+    value = planes[...].reshape(count * levels, columns)
+    spec[...] = split_dot(halves(value), (table_hi[...], table_lo[...])).reshape(planes.shape)
 
 
 def chunk_decay(rows, blocks, coeff, sheets):
@@ -306,29 +348,23 @@
         right = right * decay + (got[q, 0, 1] + got[q, 1, 1])
 
 
-def source_kernel(own, edge, own_other, edge_other, depth, out, full):
+def source_kernel(own, edge, own_other, edge_other, depth, out):
     half = own.shape[1]
-    mine = lax.axis_index("gz")
-    here = pl.ds(pl.multiple_of(mine * half, half), half)
-    there = pl.ds(pl.multiple_of((1 - mine) * half, half), half)
-    scale = -1.0 / own.shape[2]
-    matrix = depth[...] * scale
     n = own.shape[0]
-
-    def inner(j, carry):
-        full[here, :] = own[j]
-        full[there, :] = own_other[j]
-        out[3 + j] = exact_dot(matrix, full[...])
-        return carry
-
-    def outer(j, carry):
-        full[here, :] = edge[j]
-        full[there, :] = edge_other[j]
-        out[jnp.where(j < 3, j, j + n)] = exact_dot(matrix, full[...])
-        return carry
-
-    lax.fori_loop(0, n, inner, 0)
-    lax.fori_loop(0, edge.shape[0], outer, 0)
+    first = lax.axis_index("gz") == 0
+    matrix = depth[...] * (-1.0 / own.shape[2])
+    here = jnp.where(first, matrix[:, :half], matrix[:, half:])
+    there = jnp.where(first, matrix[:, half:], matrix[:, :half])
+    matrix = thrice_left(halves(jnp.concatenate([here, there], axis=1)))
+
+    def product(mine, other):
+        full = halves(jnp.concatenate([mine, other], axis=0))
+        return jnp.dot(matrix, thrice_right(full), preferred_element_type=f32)
+
+    for j in range(n):
+        out[3 + j] = product(own[j], own_other[j])
+    for j in range(5):
+        out[j if j < 3 else j + n] = product(edge[j], edge_other[j])
 
 
 def solve_kernel(rows, blocks, source, carries, coeff, basis, table_hi, table_lo, phi, phi_edge, solved, levels_hi, levels_lo):
@@ -363,10 +399,10 @@
 
     lax.fori_loop(0, carries.shape[0], chunk, 0)
     first = lax.axis_index("gz") == 0
-    share = halves(jnp.where(first, basis[:half, :], basis[half:, :]))
+    share = thrice_left(halves(jnp.where(first, basis[:half, :], basis[half:, :])))
 
     def plane(j, carry):
-        value = split_dot(share, halves(solved[j]))
+        value = jnp.dot(share, thrice_right(halves(solved[j])), preferred_element_type=f32)
         here = pl.ds(pl.multiple_of(j * half, half), half)
         levels_hi[here, :], levels_lo[here, :] = halves(value)
         return carry
@@ -379,24 +415,31 @@
     phi_edge[3:7] = result[3 + n :]
 
 
-WHOLE = pl.BlockSpec(memory_space=pltpu.VMEM)
+AWAY = pl.BlockSpec(memory_space=pl.ANY)
 
 
 def params():
-    return pltpu.CompilerParams(vmem_limit_bytes=48 * 1024 * 1024)
+    return pltpu.CompilerParams(vmem_limit_bytes=63 * 1024 * 1024)
 
 
 def cost(us):
     return pl.CostEstimate(flops=int(us * 1e6), bytes_accessed=int(us * 3e6), transcendentals=0)
 
 
-def call(kernel, outs, *args, scratch=(), us=2.0, name):
+def call(kernel, outs, *args, scratch=(), us=2.0, name, away=(), out_away=()):
     many = isinstance(outs, (list, tuple))
+
+    def whole(a):
+        return pl.BlockSpec(a.shape, lambda i: (0,) * len(a.shape), pipeline_mode=pl.Buffered(1))
+
     return pl.pallas_call(
         kernel,
+        grid=(1,),
         out_shape=outs,
-        in_specs=[WHOLE] * len(args),
-        out_specs=[WHOLE] * len(outs) if many else WHOLE,
+        in_specs=[AWAY if k in away else whole(a) for k, a in enumerate(args)],
+        out_specs=[AWAY if k in out_away else whole(a) for k, a in enumerate(outs)]
+        if many
+        else whole(outs),
         scratch_shapes=list(scratch),
         compiler_params=params(),
         cost_estimate=cost(us),
@@ -404,17 +447,17 @@
     )(*args)
 
 
-def by_rows(kernel, outs, *args, us, name):
+def by_rows(kernel, outs, *args, us, name, counts={}):
     levels, columns = args[0].shape[1:]
 
-    def spec(a):
-        return pl.BlockSpec((a.shape[0], ROWS, columns), lambda i: (0, i, 0))
+    def spec(a, count=None):
+        return pl.BlockSpec((count or a.shape[0], ROWS, columns), lambda i: (0, i, 0))
 
     return pl.pallas_call(
         kernel,
         grid=(levels // ROWS,),
         out_shape=outs,
-        in_specs=[spec(a) for a in args],
+        in_specs=[spec(a, counts.get(k)) for k, a in enumerate(args)],
         out_specs=[spec(o) for o in outs],
         compiler_params=params(),
         cost_estimate=cost(us),
@@ -471,7 +514,6 @@
         return jax.ShapeDtypeStruct(shape, f32)
 
     exact = hartley_table(columns)
-    table = jnp.asarray(exact.astype(np.float32))
     upper = exact.astype(np.float32).astype(jnp.bfloat16)
     table_hi = jnp.asarray(upper)
     table_lo = jnp.asarray((exact - upper.astype(np.float64)).astype(jnp.bfloat16))
@@ -479,51 +521,60 @@
         (2.0 - 2.0 * np.cos(np.arange(columns) * (2.0 * math.pi / columns))).astype(np.float32)
     ).reshape(1, columns)
 
-    head_left = to_right(head[n - 3 :])
-    head_right = to_left(head[:2])
-    tracer_before = to_right(jnp.concatenate([t[n - 3 :], s[n - 3 :], lt[n - 1 :], ls[n - 1 :]]))
-    tracer_after = to_left(jnp.concatenate([t[:2], s[:2]]))
-    flow_before = to_right(jnp.concatenate([u[n - 5 :], c[n - 2 :], df[n - 3 :]]))
-    flow_after = to_left(jnp.concatenate([u[:5], c[:3], df[:3]]))
-
-    whole = lambda *shape: pl.BlockSpec(shape, lambda j: (0,) * len(shape))
-    spec, coeff, sums = pl.pallas_call(
+    right, left = call(
+        pack_kernel,
+        [like(11, levels, columns), like(6, levels, columns)],
+        head, t, s, lt, ls,
+        scratch=[pltpu.SemaphoreType.DMA((8,))],
+        away=range(5),
+        out_away=range(2),
+        us=2.0,
+        name="pack",
+    )
+    before, after = to_right(right), to_left(left)
+
+    spec, coeff, sums, flow_right, flow_left = call(
         lambda *refs: moments_kernel(rows, blocks, *refs),
-        grid=(n,),
-        out_shape=[
+        [
             like(n, levels, columns),
             like(3, modes, columns),
             like(chunks, 2, rows, width),
+            like(10, levels, columns),
+            like(11, levels, columns),
         ],
-        in_specs=[
-            pl.BlockSpec((1, levels, columns), lambda j: (j, 0, 0)),
-            whole(columns, columns),
-            whole(modes, modes),
-            whole(modes, 1),
-            whole(1, columns),
-        ],
-        out_specs=[
-            pl.BlockSpec((1, levels, columns), lambda j: (j, 0, 0)),
-            whole(3, modes, columns),
-            whole(chunks, 2, rows, width),
-        ],
-        scratch_shapes=[pltpu.VMEM((modes, columns), f32)] * 3,
-        compiler_params=params(),
-        cost_estimate=cost(4.0),
+        head, table_hi, table_lo, depth_into_eigenbasis,
+        spectral_magnitudes.reshape(1, modes), waves, u, c, df,
+        scratch=[pltpu.SemaphoreType.DMA((6,))],
+        away=(6, 7, 8),
+        out_away=(3, 4),
+        us=5.0,
         name="block_moments",
-    )(head, table, depth_into_eigenbasis, spectral_magnitudes.reshape(modes, 1), waves)
+    )
     gathered = lax.all_to_all(sums, GROUP_ALL, 0, 0, tiled=True)
+    gathered, late, flow_right, flow_left = lax.optimization_barrier(
+        (gathered, spec, flow_right, flow_left)
+    )
     gathered = gathered.reshape(places, chunks // places, 2, rows, width)
-    spec_other = other_half(spec)
-    edge = call(halo_kernel, like(5, levels, columns), head_left, head_right, table, us=3.0, name="edge_spectrum")
+    edge = call(
+        halo_kernel,
+        like(5, levels, columns),
+        before, after, table_hi, table_lo,
+        scratch=[pltpu.VMEM((5, levels, columns), f32), pltpu.SemaphoreType.DMA((2,))],
+        away=(0, 1),
+        us=2.0,
+        name="edge_spectrum",
+    )
+    spec_other = other_half(late)
     edge_other = other_half(edge)
+    flow_before, flow_after = to_right(flow_right), to_left(flow_left)
 
     t_base, s_base, c_base, to_left_part, to_right_part = by_rows(
         tracer_kernel,
         [like(n, levels, columns)] * 3 + [like(6, levels, columns), like(4, levels, columns)],
-        t, s, c, lt, ls, tracer_before, tracer_after,
-        us=10.0,
+        t, s, c, lt, ls, before, after,
+        us=9.0,
         name="tracers",
+        counts={5: 8, 6: 4},
     )
     from_right = to_left(to_left_part)
     from_left = to_right(to_right_part)
@@ -549,7 +600,6 @@
         source_kernel,
         like(n + 5, modes, columns),
         spec, edge, spec_other, edge_other, depth_into_eigenbasis,
-        scratch=[pltpu.VMEM((modes, columns), f32)],
         us=4.0,
         name="mode_source",
     )

time: 142 us -> 274 us (1.93)
  the two profiles are of different devices: /device:TPU:32 before, /device:TPU:103 now
where the time goes in v2:
time: 274 us; the launch traced here: 273 us
  Pallas kernels  198 us (72%)
  starting transfers between devices  48.4 us (18%)
  waiting for transfers between devices  24.3 us (9%)
    pallas_call x7, Pallas kernels, call(): pl.pallas_call(kernel, grid=(1,), out_shape=outs, in_specs=[AWAY if k in...  177 us
    ppermute x3, starting transfers between devices, to_left(): lax.ppermute(block, ALONG, [((i + 1) % across, i) for i in range(across)])  24.7 us
    pallas_call x2, Pallas kernels, by_rows(): pl.pallas_call(kernel, grid=(levels // ROWS,), out_shape=outs, in_specs=[...  20.7 us
    ppermute x2, waiting for transfers between devices, other_half(): return lax.ppermute(block, 'gz', [(0, 1), (1, 0)])  14.2 us
    all_to_all x1, waiting for transfers between devices, shards(): gathered = lax.all_to_all(sums, GROUP_ALL, 0, 0, tiled=True)  10 us
    all_to_all x1, starting transfers between devices, shards(): gathered = lax.all_to_all(sums, GROUP_ALL, 0, 0, tiled=True)  7.49 us
  transfers between devices with their start and end apart: 11, of which 3 were waited for; matrix products, arithmetic and copies ran while one was open for 0% of the time, Pallas kernels for 44%

profile of v2, /device:TPU:103, one launch (start us, length us, event | category | flops | bytes accessed | tf_op | source)
XLA Modules:
  0.0 272.9 jit_solution(6590738774472180697)
XLA Ops:
  0.6 68.7 %pack.1 = (f32[11,64,512]{2,1,0:T(8,128)}, f32[6,64,512]{2,1,0:T(8,128)}) custom-call(f32[6,64,512]{2,1,0:T(8,128)} %bitcast.33, f32[6,64,512]{2,1,0:T(8,128)} %bitcast.21, f32[6,64,512]{2,1,0:T(8,128)} %bitcast.23, f32[6,64,512]{2,1,0:T(8,128)} %bitcast.25, f32[6,64,512]{2,1,0:T(8,128)} %bitcast.27), custom_call_target="tpu_custom_call" | custom-call | flops 2000000 | bytes 6000000 | tf_op jit(solution)/shard_map/pack/pallas_call | solution.py:435
  69.3 3.5 %collective-permute-start.2 = (f32[11,64,512]{2,1,0:T(8,128)}, f32[11,64,512]{2,1,0:T(8,128)}, u32[]{:S(2)}, u32[]{:S(2)}) collective-permute-start(f32[11,64,512]{2,1,0:T(8,128)} %get-tuple-element.33), channel_id=1, source_target_pairs={{0,2},{2,4},{4,6},{6,8},{8,10},{10,12},{12,14},{14,16},{16,18},{18... | collective-permute-start | bytes 4325384 | tf_op jit(solution)/shard_map/ppermute | solution.py:505
  72.8 87.3 %block_moments.1 = (f32[6,64,512]{2,1,0:T(8,128)}, f32[3,128,512]{2,1,0:T(8,128)}, f32[32,2,8,256]{3,2,1,0:T(8,128)}, f32[10,64,512]{2,1,0:T(8,128)}, f32[11,64,512]{2,1,0:T(8,128)}) custom-call(f32[6,64,512]{2,1,0:T(8,128)} %bitcast.34, bf16[512,512]{1,0:T(8,128)(2,1)} %constant.6.clone.refs_1_.table_hi.refs_4_, ...), custom_call_target="tpu_custom_call" | custom-call | flops 5000000 | bytes 15000000 | tf_op jit(solution)/shard_map/block_moments/pallas_call | solution.py:435
  160.1 7.5 %all-to-all-start = ((f32[32,2,8,256]{3,2,1,0:T(8,128)}), f32[32,2,8,256]{3,2,1,0:T(8,128)S(1)}, u32[]{:S(2)}, u32[]{:S(2)}) async-start(f32[32,2,8,256]{3,2,1,0:T(8,128)} %get-tuple-element.27), calls=%async_computation | async-start | bytes 1048576 | tf_op jit(solution)/shard_map/all_to_all | solution.py:553
  167.6 0.4 collective-permute-start.3
  168.0 10.0 %all-to-all-done = f32[32,2,8,256]{3,2,1,0:T(8,128)S(1)} async-done(((f32[32,2,8,256]{3,2,1,0:T(8,128)}), f32[32,2,8,256]{3,2,1,0:T(8,128)S(1)}, u32[]{:S(2)}, u32[]{:S(2)}) %all-to-all-start) | async-done | bytes 524320 | tf_op jit(solution)/shard_map/all_to_all | solution.py:553
  178.1 0.0 copy-start
  178.1 23.7 %collective-permute-start.1 = (f32[11,64,512]{2,1,0:T(8,128)}, f32[11,64,512]{2,1,0:T(8,128)}, u32[]{:S(2)}, u32[]{:S(2)}) collective-permute-start(f32[11,64,512]{2,1,0:T(8,128)} %get-tuple-element.32), channel_id=1, source_target_pairs={{2,0},{4,2},{6,4},{8,6},{10,8},{12,10},{14,12},{16,14},{18,16},{20... | collective-permute-start | bytes 4325384 | tf_op jit(solution)/shard_map/ppermute | solution.py:508
  201.8 0.0 collective-permute-start.4
  201.8 0.0 collective-permute-start
  201.8 0.0 collective-permute-done.3.after
  201.8 0.0 collective-permute-done.2.before
  201.8 10.2 %tracers.1 = (f32[6,64,512]{2,1,0:T(8,128)}, f32[6,64,512]{2,1,0:T(8,128)}, f32[6,64,512]{2,1,0:T(8,128)}, f32[6,64,512]{2,1,0:T(8,128)}, f32[4,64,512]{2,1,0:T(8,128)}) custom-call(f32[6,64,512]{2,1,0:T(8,128)} %bitcast.22, f32[6,64,512]{2,1,0:T(8,128)} %bitcast.24, f32[6,64,512]{2,1,0:T(8,128)} %bitcast.17, f32[6,64,512]{2,1,0:T(8,128)} %bitcast.26, ...), custom_call_target="tpu_custom_call" | custom-call | flops 9000000 | bytes 27000000 | tf_op jit(solution)/shard_map/tracers/pallas_call | solution.py:456
  212.1 0.0 copy-done
  212.1 0.6 collective-permute-start.7
  212.6 2.0 group_moments.1
  214.6 5.0 %all-to-all-start.1 = ((f32[8,2,8,256]{3,2,1,0:T(8,128)}), f32[8,2,8,256]{3,2,1,0:T(8,128)S(1)}, u32[]{:S(2)}, u32[]{:S(2)}) async-start(f32[8,2,8,256]{3,2,1,0:T(8,128)} %group_moments.1), calls=%async_computation.1 | async-start | bytes 262144 | tf_op jit(solution)/shard_map/all_to_all | solution.py:589
  219.7 3.8 %edge_spectrum.1.edge = f32[5,64,512]{2,1,0:T(8,128)} custom-call(f32[11,64,512]{2,1,0:T(8,128)} %collective-permute-done.2.before, f32[6,64,512]{2,1,0:T(8,128)} %collective-permute-done.3.after, bf16[512,512]{1,0:T(8,128)(2,1)} %constant.6.clone.refs_1_.table_hi.refs_4_, bf16[512,512]{1,0:T(8,128)(2,1)} %constant.7.clone.refs_2_.table_lo.refs_5_), custom_call_target="tpu_custom_call" | custom-call | flops 2000000 | bytes 6000000 | tf_op jit(solution)/shard_map/edge_spectrum/pallas_call | solution.py:435
  223.5 1.5 collective-permute-start.5
  225.0 5.0 %collective-permute-done.4.own_other = f32[6,64,512]{2,1,0:T(8,128)} collective-permute-done((f32[6,64,512]{2,1,0:T(8,128)}, f32[6,64,512]{2,1,0:T(8,128)}, u32[]{:S(2)}, u32[]{:S(2)}) %collective-permute-start.4) | collective-permute-done | bytes 786464 | tf_op jit(solution)/shard_map/ppermute | solution.py:511
  230.0 1.4 collective-permute-start.6
  231.3 0.0 all-to-all-done.1.refs_1_
  231.3 0.0 copy-start.2
  231.3 0.6 copy-done.2
  232.0 2.2 group_carries.1
  234.2 4.8 %all-to-all-start.2 = ((f32[32,2,8,256]{3,2,1,0:T(8,128)}), f32[32,2,8,256]{3,2,1,0:T(8,128)S(1)}, u32[]{:S(2)}, u32[]{:S(2)}) async-start(f32[32,2,8,256]{3,2,1,0:T(8,128)} %bitcast.35), calls=%async_computation.2 | async-start | bytes 1048576 | tf_op jit(solution)/shard_map/all_to_all | solution.py:597
  239.0 9.3 %collective-permute-done.5.edge_other = f32[5,64,512]{2,1,0:T(8,128)} collective-permute-done((f32[5,64,512]{2,1,0:T(8,128)}, f32[5,64,512]{2,1,0:T(8,128)}, u32[]{:S(2)}, u32[]{:S(2)}) %collective-permute-start.5) | collective-permute-done | bytes 655392 | tf_op jit(solution)/shard_map/ppermute | solution.py:511
  248.2 4.4 %mode_source.1.refs_0_ = f32[11,128,512]{2,1,0:T(8,128)} custom-call(f32[6,64,512]{2,1,0:T(8,128)} %get-tuple-element.35.own, f32[5,64,512]{2,1,0:T(8,128)} %edge_spectrum.1.edge, f32[6,64,512]{2,1,0:T(8,128)} %collective-permute-done.4.own_other, f32[5,64,512]{2,1,0:T(8,128)} %collective-permute-done.5.edge_other, f32[128,128]{1,0:T(8,128)} %depth.1), custom_call_target="tpu_custom_call" | custom-call | flops 4000000 | bytes 12000000 | tf_op jit(solution)/shard_map/mode_source/pallas_call | solution.py:435
  252.6 0.0 all-to-all-done.2.refs_1_
  252.6 0.0 copy-start.1
  252.6 0.8 copy-done.1
  253.4 8.9 %pressure.1 = (f32[6,64,512]{2,1,0:T(8,128)}, f32[7,64,512]{2,1,0:T(8,128)}) custom-call(f32[11,128,512]{2,1,0:T(8,128)} %mode_source.1.refs_0_, f32[32,2,8,256]{3,2,1,0:T(8,128)} %copy-done.1, f32[3,128,512]{2,1,0:T(8,128)} %get-tuple-element.37.refs_1_.refs_2_, f32[128,128]{1,0:T(8,128)} %refs_3_.3, ...), custom_call_target="tpu_custom_call" | custom-call | flops 7000000 | bytes 21000000 | tf_op jit(solution)/shard_map/pressure/pallas_call | solution.py:435
  262.3 0.0 collective-permute-done.before
  262.3 0.0 collective-permute-done.1.after
  262.3 0.0 collective-permute-done.6.from_left
  262.3 0.0 collective-permute-done.7.from_right
  262.3 10.5 %flow.1 = (f32[6,64,512]{2,1,0:T(8,128)}, f32[6,64,512]{2,1,0:T(8,128)}, f32[6,64,512]{2,1,0:T(8,128)}, f32[6,64,512]{2,1,0:T(8,128)}) custom-call(f32[6,64,512]{2,1,0:T(8,128)} %bitcast.30, f32[6,64,512]{2,1,0:T(8,128)} %bitcast.18, f32[6,64,512]{2,1,0:T(8,128)} %bitcast.32, f32[10,64,512]{2,1,0:T(8,128)} %collective-permute-done.before, ...), custom_call_target="tpu_custom_call" | custom-call | flops 7000000 | bytes 21000000 | tf_op jit(solution)/shard_map/flow/pallas_call | solution.py:456
Async XLA Ops:
  69.3 132.5 %collective-permute-start.2 = (f32[11,64,512]{2,1,0:T(8,128)}, f32[11,64,512]{2,1,0:T(8,128)}, u32[]{:S(2)}, u32[]{:S(2)}) collective-permute-start(f32[11,64,512]{2,1,0:T(8,128)} %get-tuple-element.33), channel_id=1, source_target_pairs={{0,2},{2,4},{4,6},{6,8},{8,10},{10,12},{12,14},{14,16},{16,18},{18... | collective-permute-start | bytes 4325384 | tf_op jit(solution)/shard_map/ppermute | solution.py:505
  160.1 18.0 %all-to-all-start = ((f32[32,2,8,256]{3,2,1,0:T(8,128)}), f32[32,2,8,256]{3,2,1,0:T(8,128)S(1)}, u32[]{:S(2)}, u32[]{:S(2)}) async-start(f32[32,2,8,256]{3,2,1,0:T(8,128)} %get-tuple-element.27), calls=%async_computation | async-start | bytes 1048576 | tf_op jit(solution)/shard_map/all_to_all | solution.py:553
  167.6 34.2 %collective-permute-start.3 = (f32[6,64,512]{2,1,0:T(8,128)}, f32[6,64,512]{2,1,0:T(8,128)}, u32[]{:S(2)}, u32[]{:S(2)}) collective-permute-start(f32[6,64,512]{2,1,0:T(8,128)} %get-tuple-element.34), channel_id=1, source_target_pairs={{2,0},{4,2},{6,4},{8,6},{10,8},{12,10},{14,12},{16,14},{18,16},{20... | collective-permute-start | bytes 2359304 | tf_op jit(solution)/shard_map/ppermute | solution.py:508
  178.1 34.0 %copy-start = (f32[32,2,8,256]{3,2,1,0:T(8,128)}, f32[32,2,8,256]{3,2,1,0:T(8,128)S(1)}, u32[]{:S(2)}) copy-start(f32[32,2,8,256]{3,2,1,0:T(8,128)S(1)} %all-to-all-done) | copy-start | bytes 1572868
  178.1 84.3 %collective-permute-start.1 = (f32[11,64,512]{2,1,0:T(8,128)}, f32[11,64,512]{2,1,0:T(8,128)}, u32[]{:S(2)}, u32[]{:S(2)}) collective-permute-start(f32[11,64,512]{2,1,0:T(8,128)} %get-tuple-element.32), channel_id=1, source_target_pairs={{2,0},{4,2},{6,4},{8,6},{10,8},{12,10},{14,12},{16,14},{18,16},{20... | collective-permute-start | bytes 4325384 | tf_op jit(solution)/shard_map/ppermute | solution.py:508
  201.8 28.2 %collective-permute-start.4 = (f32[6,64,512]{2,1,0:T(8,128)}, f32[6,64,512]{2,1,0:T(8,128)}, u32[]{:S(2)}, u32[]{:S(2)}) collective-permute-start(f32[6,64,512]{2,1,0:T(8,128)} %get-tuple-element.35.own), channel_id=1, source_target_pairs={{0,1},{1,0},{2,3},{3,2},{4,5},{5,4},{6,7},{7,6},{8,9},{9,8},{10,11... | collective-permute-start | bytes 2359304 | tf_op jit(solution)/shard_map/ppermute | solution.py:511
  201.8 60.5 %collective-permute-start = (f32[10,64,512]{2,1,0:T(8,128)}, f32[10,64,512]{2,1,0:T(8,128)}, u32[]{:S(2)}, u32[]{:S(2)}) collective-permute-start(f32[10,64,512]{2,1,0:T(8,128)} %get-tuple-element.31), channel_id=1, source_target_pairs={{0,2},{2,4},{4,6},{6,8},{8,10},{10,12},{12,14},{14,16},{16,18},{18... | collective-permute-start | bytes 3932168 | tf_op jit(solution)/shard_map/ppermute | solution.py:505
  212.1 50.3 %collective-permute-start.7 = (f32[6,64,512]{2,1,0:T(8,128)}, f32[6,64,512]{2,1,0:T(8,128)}, u32[]{:S(2)}, u32[]{:S(2)}) collective-permute-start(f32[6,64,512]{2,1,0:T(8,128)} %get-tuple-element.44), channel_id=1, source_target_pairs={{2,0},{4,2},{6,4},{8,6},{10,8},{12,10},{14,12},{16,14},{18,16},{20... | collective-permute-start | bytes 2359304 | tf_op jit(solution)/shard_map/ppermute | solution.py:508
  214.6 16.7 %all-to-all-start.1 = ((f32[8,2,8,256]{3,2,1,0:T(8,128)}), f32[8,2,8,256]{3,2,1,0:T(8,128)S(1)}, u32[]{:S(2)}, u32[]{:S(2)}) async-start(f32[8,2,8,256]{3,2,1,0:T(8,128)} %group_moments.1), calls=%async_computation.1 | async-start | bytes 262144 | tf_op jit(solution)/shard_map/all_to_all | solution.py:589
  223.5 24.8 %collective-permute-start.5 = (f32[5,64,512]{2,1,0:T(8,128)}, f32[5,64,512]{2,1,0:T(8,128)}, u32[]{:S(2)}, u32[]{:S(2)}) collective-permute-start(f32[5,64,512]{2,1,0:T(8,128)} %edge_spectrum.1.edge), channel_id=1, source_target_pairs={{0,1},{1,0},{2,3},{3,2},{4,5},{5,4},{6,7},{7,6},{8,9},{9,8},{10,11... | collective-permute-start | bytes 1966088 | tf_op jit(solution)/shard_map/ppermute | solution.py:511
  230.0 32.4 %collective-permute-start.6 = (f32[4,64,512]{2,1,0:T(8,128)}, f32[4,64,512]{2,1,0:T(8,128)}, u32[]{:S(2)}, u32[]{:S(2)}) collective-permute-start(f32[4,64,512]{2,1,0:T(8,128)} %get-tuple-element.43), channel_id=1, source_target_pairs={{0,2},{2,4},{4,6},{6,8},{8,10},{10,12},{12,14},{14,16},{16,18},{18... | collective-permute-start | bytes 1572872 | tf_op jit(solution)/shard_map/ppermute | solution.py:505
  231.3 0.6 copy-start.2
  234.2 18.4 %all-to-all-start.2 = ((f32[32,2,8,256]{3,2,1,0:T(8,128)}), f32[32,2,8,256]{3,2,1,0:T(8,128)S(1)}, u32[]{:S(2)}, u32[]{:S(2)}) async-start(f32[32,2,8,256]{3,2,1,0:T(8,128)} %bitcast.35), calls=%async_computation.2 | async-start | bytes 1048576 | tf_op jit(solution)/shard_map/all_to_all | solution.py:597
  252.6 0.8 copy-start.1

commit v3 on v2

--- a/solution.py
+++ b/solution.py
@@ -291,19 +291,17 @@
     spec[...] = split_dot(halves(value), (table_hi[...], table_lo[...])).reshape(planes.shape)
 
 
-def chunk_decay(rows, blocks, coeff, sheets):
+def chunk_decay(rows, blocks, coeff, chunk, sem, sheets):
     n = lax.axis_index("yh")
     for name in GROUP_ALL[1:]:
         n = n * lax.axis_size(name) + lax.axis_index(name)
-    width = coeff.shape[2] // blocks
+    width = chunk.shape[1]
     m = pl.multiple_of(n // blocks * rows, rows)
     r = pl.multiple_of(n % blocks * width, width)
-    rho = coeff[0, pl.ds(m, rows), pl.ds(r, width)]
-    square = rho * rho
-    result = jnp.ones_like(rho)
-    for _ in range(sheets // 2):
-        result = result * square
-    return result * rho if sheets % 2 else result
+    copy = pltpu.make_async_copy(coeff.at[0, pl.ds(m, rows), pl.ds(r, width)], chunk, sem)
+    copy.start()
+    copy.wait()
+    return repeated(chunk[...], sheets)
 
 
 def repeated(value, times):
@@ -315,8 +313,8 @@
     return result
 
 
-def group_kernel(rows, blocks, sheets, got, coeff, out):
-    decay = chunk_decay(rows, blocks, coeff, sheets)
+def group_kernel(rows, blocks, sheets, got, coeff, out, chunk, sem):
+    decay = chunk_decay(rows, blocks, coeff, chunk, sem, sheets)
     places, rings = got.shape[0], out.shape[0]
     forward, backward = None, None
     for p in range(places):
@@ -331,8 +329,8 @@
         forward, backward = forward * factor, backward * factor
 
 
-def carry_kernel(rows, blocks, sheets, got, rings, coeff, out):
-    decay = chunk_decay(rows, blocks, coeff, sheets)
+def carry_kernel(rows, blocks, sheets, got, rings, coeff, out, chunk, sem):
+    decay = chunk_decay(rows, blocks, coeff, chunk, sem, sheets)
     places, around = got.shape[0], rings.shape[0]
     closing = 1.0 / (1.0 - repeated(decay, places * around))
     left, right = rings[0, 0], rings[0, 1]
@@ -367,7 +365,12 @@
         out[j if j < 3 else j + n] = product(edge[j], edge_other[j])
 
 
-def solve_kernel(rows, blocks, source, carries, coeff, basis, table_hi, table_lo, phi, phi_edge, solved, levels_hi, levels_lo):
+def solve_kernel(rows, blocks, source, carries, coeff_at, basis_at, hi_at, lo_at, phi, phi_edge, solved, levels_hi, levels_lo, coeff, basis, table_hi, table_lo, sems):
+    pairs = ((coeff_at, coeff), (basis_at, basis), (hi_at, table_hi), (lo_at, table_lo))
+    copies = [pltpu.make_async_copy(p, q, sems.at[k]) for k, (p, q) in enumerate(pairs)]
+    for copy in copies:
+        copy.start()
+    copies[0].wait()
     count = source.shape[0]
     n = count - 5
     columns = source.shape[2]
@@ -398,6 +401,8 @@
         return carry
 
     lax.fori_loop(0, carries.shape[0], chunk, 0)
+    for copy in copies[1:]:
+        copy.wait()
     first = lax.axis_index("gz") == 0
     share = thrice_left(halves(jnp.where(first, basis[:half, :], basis[half:, :])))
 
@@ -527,7 +532,6 @@
         head, t, s, lt, ls,
         scratch=[pltpu.SemaphoreType.DMA((8,))],
         away=range(5),
-        out_away=range(2),
         us=2.0,
         name="pack",
     )
@@ -546,7 +550,6 @@
         spectral_magnitudes.reshape(1, modes), waves, u, c, df,
         scratch=[pltpu.SemaphoreType.DMA((6,))],
         away=(6, 7, 8),
-        out_away=(3, 4),
         us=5.0,
         name="block_moments",
     )
@@ -579,18 +582,24 @@
     from_right = to_left(to_left_part)
     from_left = to_right(to_right_part)
 
+    decay_scratch = [pltpu.VMEM((rows, width), f32), pltpu.SemaphoreType.DMA]
     ring = call(
         lambda *refs: group_kernel(rows, blocks, n, *refs),
         like(rings, 2, rows, width),
         gathered, coeff,
+        scratch=decay_scratch,
+        away=(1,),
         us=1.0,
         name="group_moments",
     )
     ring = lax.all_to_all(ring, "z", 0, 0, tiled=True)
+    ring, t_base = lax.optimization_barrier((ring, t_base))
     carries = call(
         lambda *refs: carry_kernel(rows, blocks, n, *refs),
         like(places, chunks // places, 2, rows, width),
         gathered, ring, coeff,
+        scratch=decay_scratch,
+        away=(2,),
         us=1.0,
         name="group_carries",
     )
@@ -608,7 +617,15 @@
         [like(n, levels, columns), like(7, levels, columns)],
         source, carries, coeff, eigenbasis_into_depth, table_hi, table_lo,
         scratch=[pltpu.VMEM((n + 7, modes, columns), f32)]
-        + [pltpu.VMEM(((n + 7) * levels, columns), bf16)] * 2,
+        + [pltpu.VMEM(((n + 7) * levels, columns), bf16)] * 2
+        + [
+            pltpu.VMEM((3, modes, columns), f32),
+            pltpu.VMEM((modes, modes), f32),
+            pltpu.VMEM((columns, columns), bf16),
+            pltpu.VMEM((columns, columns), bf16),
+            pltpu.SemaphoreType.DMA((4,)),
+        ],
+        away=(2, 3, 4, 5),
         us=7.0,
         name="pressure",
     )

time: 274 us -> 124 us (0.45)
  Pallas kernels: 198 us -> 52.3 us
  starting transfers between devices: 48.4 us -> 29.3 us
  waiting for transfers between devices: 24.3 us -> 39 us
    pallas_call x7, Pallas kernels: 177 us -> 31.5 us  [call(): pl.pallas_call(kernel, grid=(1,), out_shape=outs, in_specs=[AWAY if k in...]
    ppermute x3, starting transfers between devices: 24.7 us -> 0.58 us  [to_left(): lax.ppermute(block, ALONG, [((i + 1) % across, i) for i in range(across)])]
    ppermute x2, waiting for transfers between devices: 14.2 us -> 26.6 us  [other_half(): return lax.ppermute(block, 'gz', [(0, 1), (1, 0)])]
    ppermute x3, starting transfers between devices: 4.82 us -> 8.77 us  [to_right(): lax.ppermute(block, ALONG, [(i, (i + 1) % across) for i in range(across)])]
  transfers between devices with their start and end apart: 11 -> 11, of which waited for: 3 -> 4; matrix products, arithmetic and copies ran while one was open for 0% -> 0% of each run, Pallas kernels for 44% -> 32%
where the time goes in v3:
time: 124 us; the launch traced here: 123 us
  Pallas kernels  52.3 us (42%)
  waiting for transfers between devices  39 us (31%)
  starting transfers between devices  29.3 us (24%)
  local copies, waits for them, and re-layouts  1.44 us (1%)
    pallas_call x7, Pallas kernels, call(): pl.pallas_call(kernel, grid=(1,), out_shape=outs, in_specs=[AWAY if k in...  31.5 us
    ppermute x2, waiting for transfers between devices, other_half(): return lax.ppermute(block, 'gz', [(0, 1), (1, 0)])  26.6 us
    pallas_call x2, Pallas kernels, by_rows(): pl.pallas_call(kernel, grid=(levels // ROWS,), out_shape=outs, in_specs=[...  20.7 us
    all_to_all x1, waiting for transfers between devices, shards(): gathered = lax.all_to_all(sums, GROUP_ALL, 0, 0, tiled=True)  10.1 us
    ppermute x3, starting transfers between devices, to_right(): lax.ppermute(block, ALONG, [(i, (i + 1) % across) for i in range(across)])  8.77 us
    all_to_all x1, starting transfers between devices, shards(): gathered = lax.all_to_all(sums, GROUP_ALL, 0, 0, tiled=True)  7.49 us
    all_to_all x1, starting transfers between devices, shards(): lax.all_to_all(carries.reshape(chunks, 2, rows, width), GROUP_ALL, 0, 0,...  6.06 us
    all_to_all x1, starting transfers between devices, shards(): ring = lax.all_to_all(ring, 'z', 0, 0, tiled=True)  5.65 us
  transfers between devices with their start and end apart: 11, of which 4 were waited for; matrix products, arithmetic and copies ran while one was open for 0% of the time, Pallas kernels for 32%

profile of v3, /device:TPU:103, one launch (start us, length us, event | category | flops | bytes accessed | tf_op | source)
XLA Modules:
  0.0 122.8 jit_solution(16830860223382168445)
XLA Ops:
  0.6 3.0 %pack.1 = (f32[11,64,512]{2,1,0:T(8,128)}, f32[6,64,512]{2,1,0:T(8,128)}) custom-call(f32[6,64,512]{2,1,0:T(8,128)} %bitcast.33, f32[6,64,512]{2,1,0:T(8,128)} %bitcast.21, f32[6,64,512]{2,1,0:T(8,128)} %bitcast.23, f32[6,64,512]{2,1,0:T(8,128)} %bitcast.25, f32[6,64,512]{2,1,0:T(8,128)} %bitcast.27), custom_call_target="tpu_custom_call" | custom-call | flops 2000000 | bytes 6000000 | tf_op jit(solution)/shard_map/pack/pallas_call | solution.py:440
  3.6 3.5 %collective-permute-start.2 = (f32[11,64,512]{2,1,0:T(8,128)}, f32[11,64,512]{2,1,0:T(8,128)}, u32[]{:S(2)}, u32[]{:S(2)}) collective-permute-start(f32[11,64,512]{2,1,0:T(8,128)} %get-tuple-element.35), channel_id=1, source_target_pairs={{0,2},{2,4},{4,6},{6,8},{8,10},{10,12},{12,14},{14,16},{16,18},{18... | collective-permute-start | bytes 4325384 | tf_op jit(solution)/shard_map/ppermute | solution.py:510
  7.1 5.9 %block_moments.1 = (f32[6,64,512]{2,1,0:T(8,128)}, f32[3,128,512]{2,1,0:T(8,128)}, f32[32,2,8,256]{3,2,1,0:T(8,128)}, f32[10,64,512]{2,1,0:T(8,128)}, f32[11,64,512]{2,1,0:T(8,128)}) custom-call(f32[6,64,512]{2,1,0:T(8,128)} %bitcast.34, bf16[512,512]{1,0:T(8,128)(2,1)} %constant.6.clone.refs_1_.table_hi.refs_4_, ...), custom_call_target="tpu_custom_call" | custom-call | flops 5000000 | bytes 15000000 | tf_op jit(solution)/shard_map/block_moments/pallas_call | solution.py:440
  12.9 7.5 %all-to-all-start = ((f32[32,2,8,256]{3,2,1,0:T(8,128)}), f32[32,2,8,256]{3,2,1,0:T(8,128)S(1)}, u32[]{:S(2)}, u32[]{:S(2)}) async-start(f32[32,2,8,256]{3,2,1,0:T(8,128)} %get-tuple-element.29), calls=%async_computation | async-start | bytes 1048576 | tf_op jit(solution)/shard_map/all_to_all | solution.py:556
  20.4 0.4 collective-permute-start.3
  20.9 10.1 %all-to-all-done = f32[32,2,8,256]{3,2,1,0:T(8,128)S(1)} async-done(((f32[32,2,8,256]{3,2,1,0:T(8,128)}), f32[32,2,8,256]{3,2,1,0:T(8,128)S(1)}, u32[]{:S(2)}, u32[]{:S(2)}) %all-to-all-start) | async-done | bytes 524320 | tf_op jit(solution)/shard_map/all_to_all | solution.py:556
  31.0 0.0 copy-start
  31.0 0.1 collective-permute-start.1
  31.0 5.3 %collective-permute-start = (f32[10,64,512]{2,1,0:T(8,128)}, f32[10,64,512]{2,1,0:T(8,128)}, u32[]{:S(2)}, u32[]{:S(2)}) collective-permute-start(f32[10,64,512]{2,1,0:T(8,128)} %get-tuple-element.33), channel_id=1, source_target_pairs={{0,2},{2,4},{4,6},{6,8},{8,10},{10,12},{12,14},{14,16},{16,18},{18... | collective-permute-start | bytes 3932168 | tf_op jit(solution)/shard_map/ppermute | solution.py:510
  36.3 0.0 collective-permute-start.4
  36.4 2.2 %collective-permute-done.3.after = f32[6,64,512]{2,1,0:T(8,128)} collective-permute-done((f32[6,64,512]{2,1,0:T(8,128)}, f32[6,64,512]{2,1,0:T(8,128)}, u32[]{:S(2)}, u32[]{:S(2)}) %collective-permute-start.3) | collective-permute-done | bytes 786464 | tf_op jit(solution)/shard_map/ppermute | solution.py:513
  38.6 0.0 collective-permute-done.2.before
  38.6 10.2 %tracers.1 = (f32[6,64,512]{2,1,0:T(8,128)}, f32[6,64,512]{2,1,0:T(8,128)}, f32[6,64,512]{2,1,0:T(8,128)}, f32[6,64,512]{2,1,0:T(8,128)}, f32[4,64,512]{2,1,0:T(8,128)}) custom-call(f32[6,64,512]{2,1,0:T(8,128)} %bitcast.22, f32[6,64,512]{2,1,0:T(8,128)} %bitcast.24, f32[6,64,512]{2,1,0:T(8,128)} %bitcast.17, f32[6,64,512]{2,1,0:T(8,128)} %bitcast.26, ...), custom_call_target="tpu_custom_call" | custom-call | flops 9000000 | bytes 27000000 | tf_op jit(solution)/shard_map/tracers/pallas_call | solution.py:461
  48.8 0.0 copy-done
  48.8 0.1 collective-permute-start.7
  48.9 2.5 %group_moments.1 = f32[8,2,8,256]{3,2,1,0:T(8,128)} custom-call(f32[16,2,2,8,256]{4,3,2,1,0:T(8,128)} %bitcast.19, f32[3,128,512]{2,1,0:T(8,128)} %get-tuple-element.39.refs_1_.refs_2_), custom_call_target="tpu_custom_call" | custom-call | flops 1000000 | bytes 3000000 | tf_op jit(solution)/shard_map/group_moments/pallas_call | solution.py:440
  51.4 5.7 %all-to-all-start.1 = ((f32[8,2,8,256]{3,2,1,0:T(8,128)}), f32[8,2,8,256]{3,2,1,0:T(8,128)S(1)}, u32[]{:S(2)}, u32[]{:S(2)}) async-start(f32[8,2,8,256]{3,2,1,0:T(8,128)} %group_moments.1), calls=%async_computation.1 | async-start | bytes 262144 | tf_op jit(solution)/shard_map/all_to_all | solution.py:595
  57.0 3.8 %edge_spectrum.1.edge = f32[5,64,512]{2,1,0:T(8,128)} custom-call(f32[11,64,512]{2,1,0:T(8,128)} %collective-permute-done.2.before, f32[6,64,512]{2,1,0:T(8,128)} %collective-permute-done.3.after, bf16[512,512]{1,0:T(8,128)(2,1)} %constant.6.clone.refs_1_.table_hi.refs_4_, bf16[512,512]{1,0:T(8,128)(2,1)} %constant.7.clone.refs_2_.table_lo.refs_5_), custom_call_target="tpu_custom_call" | custom-call | flops 2000000 | bytes 6000000 | tf_op jit(solution)/shard_map/edge_spectrum/pallas_call | solution.py:440
  60.8 0.8 collective-permute-start.5
  61.6 18.5 %collective-permute-done.4.own_other = f32[6,64,512]{2,1,0:T(8,128)} collective-permute-done((f32[6,64,512]{2,1,0:T(8,128)}, f32[6,64,512]{2,1,0:T(8,128)}, u32[]{:S(2)}, u32[]{:S(2)}) %collective-permute-start.4) | collective-permute-done | bytes 786464 | tf_op jit(solution)/shard_map/ppermute | solution.py:516
  80.1 0.0 collective-permute-start.6
  80.1 0.0 all-to-all-done.1.refs_1_
  80.2 0.0 copy-start.2
  80.2 0.6 copy-done.2
  80.8 2.6 %group_carries.1 = f32[16,2,2,8,256]{4,3,2,1,0:T(8,128)} custom-call(f32[16,2,2,8,256]{4,3,2,1,0:T(8,128)} %bitcast.20, f32[8,2,8,256]{3,2,1,0:T(8,128)} %copy-done.2, f32[3,128,512]{2,1,0:T(8,128)} %get-tuple-element.39.refs_1_.refs_2_), custom_call_target="tpu_custom_call" | custom-call | flops 1000000 | bytes 3000000 | tf_op jit(solution)/shard_map/group_carries/pallas_call | solution.py:440
  83.4 6.1 %all-to-all-start.2 = ((f32[32,2,8,256]{3,2,1,0:T(8,128)}), f32[32,2,8,256]{3,2,1,0:T(8,128)S(1)}, u32[]{:S(2)}, u32[]{:S(2)}) async-start(f32[32,2,8,256]{3,2,1,0:T(8,128)} %bitcast.35), calls=%async_computation.2 | async-start | bytes 1048576 | tf_op jit(solution)/shard_map/all_to_all | solution.py:606
  89.5 8.1 %collective-permute-done.5.edge_other = f32[5,64,512]{2,1,0:T(8,128)} collective-permute-done((f32[5,64,512]{2,1,0:T(8,128)}, f32[5,64,512]{2,1,0:T(8,128)}, u32[]{:S(2)}, u32[]{:S(2)}) %collective-permute-start.5) | collective-permute-done | bytes 655392 | tf_op jit(solution)/shard_map/ppermute | solution.py:516
  97.6 4.4 %mode_source.1.refs_0_ = f32[11,128,512]{2,1,0:T(8,128)} custom-call(f32[6,64,512]{2,1,0:T(8,128)} %get-tuple-element.37.own, f32[5,64,512]{2,1,0:T(8,128)} %edge_spectrum.1.edge, f32[6,64,512]{2,1,0:T(8,128)} %collective-permute-done.4.own_other, f32[5,64,512]{2,1,0:T(8,128)} %collective-permute-done.5.edge_other, f32[128,128]{1,0:T(8,128)} %depth.1), custom_call_target="tpu_custom_call" | custom-call | flops 4000000 | bytes 12000000 | tf_op jit(solution)/shard_map/mode_source/pallas_call | solution.py:440
  101.9 0.0 all-to-all-done.2.refs_1_
  101.9 0.0 copy-start.1
  101.9 0.8 copy-done.1
  102.7 9.5 %pressure.1 = (f32[6,64,512]{2,1,0:T(8,128)}, f32[7,64,512]{2,1,0:T(8,128)}) custom-call(f32[11,128,512]{2,1,0:T(8,128)} %mode_source.1.refs_0_, f32[32,2,8,256]{3,2,1,0:T(8,128)} %copy-done.1, f32[3,128,512]{2,1,0:T(8,128)} %get-tuple-element.39.refs_1_.refs_2_, f32[128,128]{1,0:T(8,128)} %refs_3_.3, ...), custom_call_target="tpu_custom_call" | custom-call | flops 7000000 | bytes 21000000 | tf_op jit(solution)/shard_map/pressure/pallas_call | solution.py:440
  112.2 0.0 collective-permute-done.before
  112.2 0.0 collective-permute-done.1.after
  112.2 0.0 collective-permute-done.6.from_left
  112.3 0.0 collective-permute-done.7.from_right
  112.3 10.5 %flow.1 = (f32[6,64,512]{2,1,0:T(8,128)}, f32[6,64,512]{2,1,0:T(8,128)}, f32[6,64,512]{2,1,0:T(8,128)}, f32[6,64,512]{2,1,0:T(8,128)}) custom-call(f32[6,64,512]{2,1,0:T(8,128)} %bitcast.30, f32[6,64,512]{2,1,0:T(8,128)} %bitcast.18, f32[6,64,512]{2,1,0:T(8,128)} %bitcast.32, f32[10,64,512]{2,1,0:T(8,128)} %collective-permute-done.before, ...), custom_call_target="tpu_custom_call" | custom-call | flops 7000000 | bytes 21000000 | tf_op jit(solution)/shard_map/flow/pallas_call | solution.py:461
Async XLA Ops:
  3.6 35.0 %collective-permute-start.2 = (f32[11,64,512]{2,1,0:T(8,128)}, f32[11,64,512]{2,1,0:T(8,128)}, u32[]{:S(2)}, u32[]{:S(2)}) collective-permute-start(f32[11,64,512]{2,1,0:T(8,128)} %get-tuple-element.35), channel_id=1, source_target_pairs={{0,2},{2,4},{4,6},{6,8},{8,10},{10,12},{12,14},{14,16},{16,18},{18... | collective-permute-start | bytes 4325384 | tf_op jit(solution)/shard_map/ppermute | solution.py:510
  12.9 18.0 %all-to-all-start = ((f32[32,2,8,256]{3,2,1,0:T(8,128)}), f32[32,2,8,256]{3,2,1,0:T(8,128)S(1)}, u32[]{:S(2)}, u32[]{:S(2)}) async-start(f32[32,2,8,256]{3,2,1,0:T(8,128)} %get-tuple-element.29), calls=%async_computation | async-start | bytes 1048576 | tf_op jit(solution)/shard_map/all_to_all | solution.py:556
  20.4 18.2 %collective-permute-start.3 = (f32[6,64,512]{2,1,0:T(8,128)}, f32[6,64,512]{2,1,0:T(8,128)}, u32[]{:S(2)}, u32[]{:S(2)}) collective-permute-start(f32[6,64,512]{2,1,0:T(8,128)} %get-tuple-element.36), channel_id=1, source_target_pairs={{2,0},{4,2},{6,4},{8,6},{10,8},{12,10},{14,12},{16,14},{18,16},{20... | collective-permute-start | bytes 2359304 | tf_op jit(solution)/shard_map/ppermute | solution.py:513
  31.0 17.9 %copy-start = (f32[32,2,8,256]{3,2,1,0:T(8,128)}, f32[32,2,8,256]{3,2,1,0:T(8,128)S(1)}, u32[]{:S(2)}) copy-start(f32[32,2,8,256]{3,2,1,0:T(8,128)S(1)} %all-to-all-done) | copy-start | bytes 1572868
  31.0 81.3 %collective-permute-start.1 = (f32[11,64,512]{2,1,0:T(8,128)}, f32[11,64,512]{2,1,0:T(8,128)}, u32[]{:S(2)}, u32[]{:S(2)}) collective-permute-start(f32[11,64,512]{2,1,0:T(8,128)} %get-tuple-element.34), channel_id=1, source_target_pairs={{2,0},{4,2},{6,4},{8,6},{10,8},{12,10},{14,12},{16,14},{18,16},{20... | collective-permute-start | bytes 4325384 | tf_op jit(solution)/shard_map/ppermute | solution.py:513
  31.0 81.2 %collective-permute-start = (f32[10,64,512]{2,1,0:T(8,128)}, f32[10,64,512]{2,1,0:T(8,128)}, u32[]{:S(2)}, u32[]{:S(2)}) collective-permute-start(f32[10,64,512]{2,1,0:T(8,128)} %get-tuple-element.33), channel_id=1, source_target_pairs={{0,2},{2,4},{4,6},{6,8},{8,10},{10,12},{12,14},{14,16},{16,18},{18... | collective-permute-start | bytes 3932168 | tf_op jit(solution)/shard_map/ppermute | solution.py:510
  36.3 43.8 %collective-permute-start.4 = (f32[6,64,512]{2,1,0:T(8,128)}, f32[6,64,512]{2,1,0:T(8,128)}, u32[]{:S(2)}, u32[]{:S(2)}) collective-permute-start(f32[6,64,512]{2,1,0:T(8,128)} %get-tuple-element.37.own), channel_id=1, source_target_pairs={{0,1},{1,0},{2,3},{3,2},{4,5},{5,4},{6,7},{7,6},{8,9},{9,8},{10,11... | collective-permute-start | bytes 2359304 | tf_op jit(solution)/shard_map/ppermute | solution.py:516
  48.8 63.4 %collective-permute-start.7 = (f32[6,64,512]{2,1,0:T(8,128)}, f32[6,64,512]{2,1,0:T(8,128)}, u32[]{:S(2)}, u32[]{:S(2)}) collective-permute-start(f32[6,64,512]{2,1,0:T(8,128)} %get-tuple-element.48), channel_id=1, source_target_pairs={{2,0},{4,2},{6,4},{8,6},{10,8},{12,10},{14,12},{16,14},{18,16},{20... | collective-permute-start | bytes 2359304 | tf_op jit(solution)/shard_map/ppermute | solution.py:513
  51.4 28.8 %all-to-all-start.1 = ((f32[8,2,8,256]{3,2,1,0:T(8,128)}), f32[8,2,8,256]{3,2,1,0:T(8,128)S(1)}, u32[]{:S(2)}, u32[]{:S(2)}) async-start(f32[8,2,8,256]{3,2,1,0:T(8,128)} %group_moments.1), calls=%async_computation.1 | async-start | bytes 262144 | tf_op jit(solution)/shard_map/all_to_all | solution.py:595
  60.8 36.7 %collective-permute-start.5 = (f32[5,64,512]{2,1,0:T(8,128)}, f32[5,64,512]{2,1,0:T(8,128)}, u32[]{:S(2)}, u32[]{:S(2)}) collective-permute-start(f32[5,64,512]{2,1,0:T(8,128)} %edge_spectrum.1.edge), channel_id=1, source_target_pairs={{0,1},{1,0},{2,3},{3,2},{4,5},{5,4},{6,7},{7,6},{8,9},{9,8},{10,11... | collective-permute-start | bytes 1966088 | tf_op jit(solution)/shard_map/ppermute | solution.py:516
  80.1 32.1 %collective-permute-start.6 = (f32[4,64,512]{2,1,0:T(8,128)}, f32[4,64,512]{2,1,0:T(8,128)}, u32[]{:S(2)}, u32[]{:S(2)}) collective-permute-start(f32[4,64,512]{2,1,0:T(8,128)} %get-tuple-element.47), channel_id=1, source_target_pairs={{0,2},{2,4},{4,6},{6,8},{8,10},{10,12},{12,14},{14,16},{16,18},{18... | collective-permute-start | bytes 1572872 | tf_op jit(solution)/shard_map/ppermute | solution.py:510
  80.2 0.6 copy-start.2
  83.4 18.5 %all-to-all-start.2 = ((f32[32,2,8,256]{3,2,1,0:T(8,128)}), f32[32,2,8,256]{3,2,1,0:T(8,128)S(1)}, u32[]{:S(2)}, u32[]{:S(2)}) async-start(f32[32,2,8,256]{3,2,1,0:T(8,128)} %bitcast.35), calls=%async_computation.2 | async-start | bytes 1048576 | tf_op jit(solution)/shard_map/all_to_all | solution.py:606
  101.9 0.8 copy-start.1

commit v4 on v3

--- a/solution.py
+++ b/solution.py
@@ -27,6 +27,18 @@
 def halves(value):
     upper = value.astype(bf16)
     return upper, (value - upper.astype(f32)).astype(bf16)
+
+
+def stacked_left(pair):
+    upper = jnp.concatenate([pair[0], pair[0]], axis=1)
+    lower = jnp.concatenate([pair[1], jnp.zeros_like(pair[1])], axis=1)
+    return jnp.concatenate([upper, lower], axis=0)
+
+
+def stacked_dot(left, pair):
+    both = jnp.dot(left, jnp.concatenate(pair, axis=0), preferred_element_type=f32)
+    half = both.shape[0] // 2
+    return both[:half] + both[half:]
 
 
 def thrice_left(pair):
@@ -208,7 +220,7 @@
     lax.fori_loop(0, width // LANES, tile, 0)
 
 
-def moments_kernel(rows, blocks, head, table_hi, table_lo, depth, rates, waves, u, c, df, spec, coeff, sums, flow_right, flow_left, sems):
+def moments_kernel(rows, blocks, head, table_hi, table_lo, depth, rates, waves, u, c, df, spec, coeff, sums, decay, flow_right, flow_left, sems):
     n, levels, columns = head.shape
     width = columns // blocks
     copies = [
@@ -250,6 +262,8 @@
         m, r = i // blocks * rows, i % blocks * width
         sums[i, 0] = forward[m : m + rows, r : r + width]
         sums[i, 1] = backward[m : m + rows, r : r + width]
+    m, r = my_chunk(rows, blocks, width)
+    decay[...] = repeated(coeff[0, m, r], n)
     for copy in copies:
         copy.wait()
 
@@ -291,17 +305,13 @@
     spec[...] = split_dot(halves(value), (table_hi[...], table_lo[...])).reshape(planes.shape)
 
 
-def chunk_decay(rows, blocks, coeff, chunk, sem, sheets):
+def my_chunk(rows, blocks, width):
     n = lax.axis_index("yh")
     for name in GROUP_ALL[1:]:
         n = n * lax.axis_size(name) + lax.axis_index(name)
-    width = chunk.shape[1]
     m = pl.multiple_of(n // blocks * rows, rows)
     r = pl.multiple_of(n % blocks * width, width)
-    copy = pltpu.make_async_copy(coeff.at[0, pl.ds(m, rows), pl.ds(r, width)], chunk, sem)
-    copy.start()
-    copy.wait()
-    return repeated(chunk[...], sheets)
+    return pl.ds(m, rows), pl.ds(r, width)
 
 
 def repeated(value, times):
@@ -313,8 +323,8 @@
     return result
 
 
-def group_kernel(rows, blocks, sheets, got, coeff, out, chunk, sem):
-    decay = chunk_decay(rows, blocks, coeff, chunk, sem, sheets)
+def group_kernel(got, decay, out):
+    decay = decay[...]
     places, rings = got.shape[0], out.shape[0]
     forward, backward = None, None
     for p in range(places):
@@ -329,8 +339,8 @@
         forward, backward = forward * factor, backward * factor
 
 
-def carry_kernel(rows, blocks, sheets, got, rings, coeff, out, chunk, sem):
-    decay = chunk_decay(rows, blocks, coeff, chunk, sem, sheets)
+def carry_kernel(got, rings, decay, out):
+    decay = decay[...]
     places, around = got.shape[0], rings.shape[0]
     closing = 1.0 / (1.0 - repeated(decay, places * around))
     left, right = rings[0, 0], rings[0, 1]
@@ -346,31 +356,61 @@
         right = right * decay + (got[q, 0, 1] + got[q, 1, 1])
 
 
-def source_kernel(own, edge, own_other, edge_other, depth, out):
+def source_kernel(own_at, edge_at, own_other_at, edge_other_at, depth_at, out_at, own, edge, own_other, edge_other, depth, out, sems):
+    pairs = (
+        (depth_at, depth),
+        (own_at, own),
+        (own_other_at, own_other),
+        (edge_at, edge),
+        (edge_other_at, edge_other),
+    )
+    copies = [pltpu.make_async_copy(p, q, sems.at[k]) for k, (p, q) in enumerate(pairs)]
+    for copy in copies:
+        copy.start()
     half = own.shape[1]
     n = own.shape[0]
+    copies[0].wait()
     first = lax.axis_index("gz") == 0
     matrix = depth[...] * (-1.0 / own.shape[2])
     here = jnp.where(first, matrix[:, :half], matrix[:, half:])
     there = jnp.where(first, matrix[:, half:], matrix[:, :half])
-    matrix = thrice_left(halves(jnp.concatenate([here, there], axis=1)))
+    matrix = stacked_left(halves(jnp.concatenate([here, there], axis=1)))
 
     def product(mine, other):
-        full = halves(jnp.concatenate([mine, other], axis=0))
-        return jnp.dot(matrix, thrice_right(full), preferred_element_type=f32)
-
+        return stacked_dot(matrix, halves(jnp.concatenate([mine, other], axis=0)))
+
+    copies[1].wait()
+    copies[2].wait()
     for j in range(n):
         out[3 + j] = product(own[j], own_other[j])
+    copies.append(pltpu.make_async_copy(out.at[3 : 3 + n], out_at.at[3 : 3 + n], sems.at[5]))
+    copies[5].start()
+    copies[3].wait()
+    copies[4].wait()
     for j in range(5):
         out[j if j < 3 else j + n] = product(edge[j], edge_other[j])
-
-
-def solve_kernel(rows, blocks, source, carries, coeff_at, basis_at, hi_at, lo_at, phi, phi_edge, solved, levels_hi, levels_lo, coeff, basis, table_hi, table_lo, sems):
-    pairs = ((coeff_at, coeff), (basis_at, basis), (hi_at, table_hi), (lo_at, table_lo))
+    for k, (first, count) in enumerate(((0, 3), (3 + n, 2))):
+        part = pl.ds(first, count)
+        copies.append(pltpu.make_async_copy(out.at[part], out_at.at[part], sems.at[6 + k]))
+        copies[6 + k].start()
+    for copy in copies[5:]:
+        copy.wait()
+
+
+def solve_kernel(rows, blocks, source_at, carries_at, coeff_at, basis_at, hi_at, lo_at, phi, phi_edge, solved, levels_hi, levels_lo, source, carries, coeff, basis, table_hi, table_lo, heads, sems):
+    pairs = (
+        (carries_at, carries),
+        (coeff_at, coeff),
+        (source_at, source),
+        (basis_at, basis),
+        (hi_at, table_hi),
+        (lo_at, table_lo),
+    )
     copies = [pltpu.make_async_copy(p, q, sems.at[k]) for k, (p, q) in enumerate(pairs)]
     for copy in copies:
         copy.start()
-    copies[0].wait()
+    for copy in copies[:3]:
+        copy.wait()
     count = source.shape[0]
     n = count - 5
     columns = source.shape[2]
@@ -401,26 +441,33 @@
         return carry
 
     lax.fori_loop(0, carries.shape[0], chunk, 0)
-    for copy in copies[1:]:
+    for copy in copies[3:]:
         copy.wait()
     first = lax.axis_index("gz") == 0
-    share = thrice_left(halves(jnp.where(first, basis[:half, :], basis[half:, :])))
+    share = stacked_left(halves(jnp.where(first, basis[:half, :], basis[half:, :])))
 
     def plane(j, carry):
-        value = jnp.dot(share, thrice_right(halves(solved[j])), preferred_element_type=f32)
+        value = stacked_dot(share, halves(solved[j]))
         here = pl.ds(pl.multiple_of(j * half, half), half)
         levels_hi[here, :], levels_lo[here, :] = halves(value)
         return carry
 
     lax.fori_loop(0, count + 2, plane, 0)
     result = split_dot((levels_hi[...], levels_lo[...]), (table_hi[...], table_lo[...]))
-    result = result.reshape(count + 2, half, columns)
-    phi[...] = result[3 : 3 + n]
-    phi_edge[0:3] = result[0:3]
-    phi_edge[3:7] = result[3 + n :]
-
-
-AWAY = pl.BlockSpec(memory_space=pl.ANY)
+    heads[...] = result.reshape(count + 2, half, columns)
+    pairs = (
+        (heads.at[3 : 3 + n], phi),
+        (heads.at[0:3], phi_edge.at[0:3]),
+        (heads.at[3 + n : count + 2], phi_edge.at[3:7]),
+    )
+    copies = [pltpu.make_async_copy(p, q, sems.at[6 + k]) for k, (p, q) in enumerate(pairs)]
+    for copy in copies:
+        copy.start()
+    for copy in copies:
+        copy.wait()
+
+
+AWAY = pl.BlockSpec(memory_space=pltpu.HBM)
 
 
 def params():
@@ -447,6 +494,22 @@
         else whole(outs),
         scratch_shapes=list(scratch),
         compiler_params=params(),
+        cost_estimate=cost(us),
+        name=name,
+    )(*args)
+
+
+def near(kernel, outs, *args, us, name, scratch=(), away=(), out_away=(), limit=48):
+    where = pl.BlockSpec(memory_space=pltpu.VMEM)
+    return pl.pallas_call(
+        kernel,
+        out_shape=outs,
+        in_specs=[AWAY if k in away else where for k in range(len(args))],
+        out_specs=[AWAY if k in out_away else where for k in range(len(outs))]
+        if isinstance(outs, list)
+        else where,
+        scratch_shapes=list(scratch),
+        compiler_params=pltpu.CompilerParams(vmem_limit_bytes=limit * 1024 * 1024),
         cost_estimate=cost(us),
         name=name,
     )(*args)
@@ -537,12 +600,13 @@
     )
     before, after = to_right(right), to_left(left)
 
-    spec, coeff, sums, flow_right, flow_left = call(
+    spec, coeff, sums, decay, flow_right, flow_left = call(
         lambda *refs: moments_kernel(rows, blocks, *refs),
         [
             like(n, levels, columns),
             like(3, modes, columns),
             like(chunks, 2, rows, width),
+            like(rows, width),
             like(10, levels, columns),
             like(11, levels, columns),
         ],
@@ -554,10 +618,20 @@
         name="block_moments",
     )
     gathered = lax.all_to_all(sums, GROUP_ALL, 0, 0, tiled=True)
-    gathered, late, flow_right, flow_left = lax.optimization_barrier(
-        (gathered, spec, flow_right, flow_left)
+    t_base, s_base, c_base, to_left_part, to_right_part = by_rows(
+        tracer_kernel,
+        [like(n, levels, columns)] * 3 + [like(6, levels, columns), like(4, levels, columns)],
+        t, s, c, lt, ls, before, after,
+        us=9.0,
+        name="tracers",
+        counts={5: 8, 6: 4},
+    )
+    gathered, late, flow_right, flow_left, t_base = lax.optimization_barrier(
+        (gathered, spec, flow_right, flow_left, t_base)
     )
     gathered = gathered.reshape(places, chunks // places, 2, rows, width)
+    spec_other = other_half(late)
+    flow_before, flow_after = to_right(flow_right), to_left(flow_left)
     edge = call(
         halo_kernel,
         like(5, levels, columns),
@@ -567,66 +641,69 @@
         us=2.0,
         name="edge_spectrum",
     )
-    spec_other = other_half(late)
     edge_other = other_half(edge)
-    flow_before, flow_after = to_right(flow_right), to_left(flow_left)
-
-    t_base, s_base, c_base, to_left_part, to_right_part = by_rows(
-        tracer_kernel,
-        [like(n, levels, columns)] * 3 + [like(6, levels, columns), like(4, levels, columns)],
-        t, s, c, lt, ls, before, after,
-        us=9.0,
-        name="tracers",
-        counts={5: 8, 6: 4},
-    )
+
+    ring = near(
+        group_kernel,
+        like(rings, 2, rows, width),
+        gathered, decay,
+        us=1.0,
+        name="group_moments",
+    )
+    ring = lax.all_to_all(ring, "z", 0, 0, tiled=True)
+    carries = near(
+        carry_kernel,
+        like(places, chunks // places, 2, rows, width),
+        gathered, ring, decay,
+        us=1.0,
+        name="group_carries",
+    )
+    carries, to_left_part, to_right_part = lax.optimization_barrier(
+        (carries, to_left_part, to_right_part)
+    )
+    carries = lax.all_to_all(carries.reshape(chunks, 2, rows, width), GROUP_ALL, 0, 0, tiled=True)
     from_right = to_left(to_left_part)
     from_left = to_right(to_right_part)
 
-    decay_scratch = [pltpu.VMEM((rows, width), f32), pltpu.SemaphoreType.DMA]
-    ring = call(
-        lambda *refs: group_kernel(rows, blocks, n, *refs),
-        like(rings, 2, rows, width),
-        gathered, coeff,
-        scratch=decay_scratch,
-        away=(1,),
-        us=1.0,
-        name="group_moments",
-    )
-    ring = lax.all_to_all(ring, "z", 0, 0, tiled=True)
-    ring, t_base = lax.optimization_barrier((ring, t_base))
-    carries = call(
-        lambda *refs: carry_kernel(rows, blocks, n, *refs),
-        like(places, chunks // places, 2, rows, width),
-        gathered, ring, coeff,
-        scratch=decay_scratch,
-        away=(2,),
-        us=1.0,
-        name="group_carries",
-    )
-    carries = lax.all_to_all(carries.reshape(chunks, 2, rows, width), GROUP_ALL, 0, 0, tiled=True)
-
-    source = call(
+    (source,) = near(
         source_kernel,
-        like(n + 5, modes, columns),
+        [like(n + 5, modes, columns)],
         spec, edge, spec_other, edge_other, depth_into_eigenbasis,
+        scratch=[
+            pltpu.VMEM((n, levels, columns), f32),
+            pltpu.VMEM((5, levels, columns), f32),
+            pltpu.VMEM((n, levels, columns), f32),
+            pltpu.VMEM((5, levels, columns), f32),
+            pltpu.VMEM((modes, modes), f32),
+            pltpu.VMEM((n + 5, modes, columns), f32),
+            pltpu.SemaphoreType.DMA((8,)),
+        ],
+        away=range(5),
+        out_away=(0,),
         us=4.0,
+        limit=63,
         name="mode_source",
     )
-    phi, phi_edge = call(
+    phi, phi_edge = near(
         lambda *refs: solve_kernel(rows, blocks, *refs),
         [like(n, levels, columns), like(7, levels, columns)],
         source, carries, coeff, eigenbasis_into_depth, table_hi, table_lo,
         scratch=[pltpu.VMEM((n + 7, modes, columns), f32)]
         + [pltpu.VMEM(((n + 7) * levels, columns), bf16)] * 2
         + [
+            pltpu.VMEM((n + 5, modes, columns), f32),
+            pltpu.VMEM((chunks, 2, rows, width), f32),
             pltpu.VMEM((3, modes, columns), f32),
             pltpu.VMEM((modes, modes), f32),
             pltpu.VMEM((columns, columns), bf16),
             pltpu.VMEM((columns, columns), bf16),
-            pltpu.SemaphoreType.DMA((4,)),
+            pltpu.VMEM((n + 7, levels, columns), f32),
+            pltpu.SemaphoreType.DMA((9,)),
         ],
-        away=(2, 3, 4, 5),
+        away=range(6),
+        out_away=(0, 1),
         us=7.0,
+        limit=63,
         name="pressure",
     )
     t_bar, s_bar, u_bar, c_bar = by_rows(

time: 124 us -> 130 us (1.048)
  waiting for transfers between devices: 39 us -> 48.9 us
  Pallas kernels: 52.3 us -> 47.7 us
    pallas_call x7 -> x3, Pallas kernels: 31.5 us -> 12.9 us  [call(): pl.pallas_call(kernel, grid=(1,), out_shape=outs, in_specs=[AWAY if k in...]
    pallas_call x0 -> x4, Pallas kernels: none -> 14 us  [near(): pl.pallas_call(kernel, out_shape=outs, in_specs=[AWAY if k in away else w...]
    ppermute x2, waiting for transfers between devices: 26.6 us -> 38.8 us  [other_half(): return lax.ppermute(block, 'gz', [(0, 1), (1, 0)])]
    all_to_all x1, waiting for transfers between devices: 10.1 us -> 0.01 us  [shards(): gathered = lax.all_to_all(sums, GROUP_ALL, 0, 0, tiled=True)]
    ppermute x3, waiting for transfers between devices: 0.01 us -> 5.02 us  [to_right(): lax.ppermute(block, ALONG, [(i, (i + 1) % across) for i in range(across)])]
    all_to_all x1, waiting for transfers between devices: 0.01 us -> 3.34 us  [shards(): ring = lax.all_to_all(ring, 'z', 0, 0, tiled=True)]
    all_to_all x1, starting transfers between devices: 6.06 us -> 4.43 us  [shards(): lax.all_to_all(carries.reshape(chunks, 2, rows, width), GROUP_ALL, 0, 0,...]
  transfers between devices with their start and end apart: 11 -> 11, of which waited for: 4 -> 5; matrix products, arithmetic and copies ran while one was open for 0% -> 0% of each run, Pallas kernels for 32% -> 26%
where the time goes in v4:
time: 130 us; the launch traced here: 129 us
  waiting for transfers between devices  48.9 us (38%)
  Pallas kernels  47.7 us (37%)
  starting transfers between devices  30.2 us (23%)
  local copies, waits for them, and re-layouts  1.63 us (1%)
    ppermute x2, waiting for transfers between devices, other_half(): return lax.ppermute(block, 'gz', [(0, 1), (1, 0)])  38.8 us
    pallas_call x2, Pallas kernels, by_rows(): pl.pallas_call(kernel, grid=(levels // ROWS,), out_shape=outs, in_specs=[...  20.7 us
    pallas_call x4, Pallas kernels, near(): pl.pallas_call(kernel, out_shape=outs, in_specs=[AWAY if k in away else w...  14 us
    pallas_call x3, Pallas kernels, call(): pl.pallas_call(kernel, grid=(1,), out_shape=outs, in_specs=[AWAY if k in...  12.9 us
    ppermute x3, starting transfers between devices, to_right(): lax.ppermute(block, ALONG, [(i, (i + 1) % across) for i in range(across)])  9.91 us
    all_to_all x1, starting transfers between devices, shards(): gathered = lax.all_to_all(sums, GROUP_ALL, 0, 0, tiled=True)  7.49 us
    all_to_all x1, starting transfers between devices, shards(): ring = lax.all_to_all(ring, 'z', 0, 0, tiled=True)  6.73 us
    ppermute x3, waiting for transfers between devices, to_right(): lax.ppermute(block, ALONG, [(i, (i + 1) % across) for i in range(across)])  5.02 us
  transfers between devices with their start and end apart: 11, of which 5 were waited for; matrix products, arithmetic and copies ran while one was open for 0% of the time, Pallas kernels for 26%

profile of v4, /device:TPU:103, one launch (start us, length us, event | category | flops | bytes accessed | tf_op | source)
XLA Modules:
  0.0 129.1 jit_solution(97978351807580704)
XLA Ops:
  0.6 3.0 %pack.1 = (f32[11,64,512]{2,1,0:T(8,128)}, f32[6,64,512]{2,1,0:T(8,128)}) custom-call(f32[6,64,512]{2,1,0:T(8,128)} %bitcast.33, f32[6,64,512]{2,1,0:T(8,128)} %bitcast.21, f32[6,64,512]{2,1,0:T(8,128)} %bitcast.23, f32[6,64,512]{2,1,0:T(8,128)} %bitcast.25, f32[6,64,512]{2,1,0:T(8,128)} %bitcast.27), custom_call_target="tpu_custom_call" | custom-call | flops 2000000 | bytes 6000000 | tf_op jit(solution)/shard_map/pack/pallas_call | solution.py:487
  3.6 3.5 %collective-permute-start = (f32[11,64,512]{2,1,0:T(8,128)}, f32[11,64,512]{2,1,0:T(8,128)}, u32[]{:S(2)}, u32[]{:S(2)}) collective-permute-start(f32[11,64,512]{2,1,0:T(8,128)} %get-tuple-element.36), channel_id=1, source_target_pairs={{0,2},{2,4},{4,6},{6,8},{8,10},{10,12},{12,14},{14,16},{16,18},{18... | collective-permute-start | bytes 4325384 | tf_op jit(solution)/shard_map/ppermute | solution.py:573
  7.1 0.0 collective-permute-start.1
  7.1 6.2 %block_moments.1 = (f32[6,64,512]{2,1,0:T(8,128)}, f32[3,128,512]{2,1,0:T(8,128)}, f32[32,2,8,256]{3,2,1,0:T(8,128)}, f32[8,256]{1,0:T(8,128)}, f32[10,64,512]{2,1,0:T(8,128)}, /*index=5*/f32[11,64,512]{2,1,0:T(8,128)}) custom-call(f32[6,64,512]{2,1,0:T(8,128)} %bitcast.34, bf16[512,512]{1,0:T(8,128)(2,1)} %constant.6.clone.refs_1_.table_hi.refs_4_, ...), custom_call_target="tpu_custom_call" | custom-call | flops 5000000 | bytes 15000000 | tf_op jit(solution)/shard_map/block_moments/pallas_call | solution.py:487
  13.3 7.5 %all-to-all-start = ((f32[32,2,8,256]{3,2,1,0:T(8,128)}), f32[32,2,8,256]{3,2,1,0:T(8,128)S(1)}, u32[]{:S(2)}, u32[]{:S(2)}) async-start(f32[32,2,8,256]{3,2,1,0:T(8,128)} %get-tuple-element.32), calls=%async_computation | async-start | bytes 1048576 | tf_op jit(solution)/shard_map/all_to_all | solution.py:620
  20.8 1.7 %collective-permute-done.1.after = f32[6,64,512]{2,1,0:T(8,128)} collective-permute-done((f32[6,64,512]{2,1,0:T(8,128)}, f32[6,64,512]{2,1,0:T(8,128)}, u32[]{:S(2)}, u32[]{:S(2)}) %collective-permute-start.1) | collective-permute-done | bytes 786464 | tf_op jit(solution)/shard_map/ppermute | solution.py:576
  22.4 5.0 %collective-permute-done.before = f32[11,64,512]{2,1,0:T(8,128)} collective-permute-done((f32[11,64,512]{2,1,0:T(8,128)}, f32[11,64,512]{2,1,0:T(8,128)}, u32[]{:S(2)}, u32[]{:S(2)}) %collective-permute-start) | collective-permute-done | bytes 1441824 | tf_op jit(solution)/shard_map/ppermute | solution.py:573
  27.4 10.2 %tracers.1 = (f32[6,64,512]{2,1,0:T(8,128)}, f32[6,64,512]{2,1,0:T(8,128)}, f32[6,64,512]{2,1,0:T(8,128)}, f32[6,64,512]{2,1,0:T(8,128)}, f32[4,64,512]{2,1,0:T(8,128)}) custom-call(f32[6,64,512]{2,1,0:T(8,128)} %bitcast.22, f32[6,64,512]{2,1,0:T(8,128)} %bitcast.24, f32[6,64,512]{2,1,0:T(8,128)} %bitcast.19, f32[6,64,512]{2,1,0:T(8,128)} %bitcast.26, ...), custom_call_target="tpu_custom_call" | custom-call | flops 9000000 | bytes 27000000 | tf_op jit(solution)/shard_map/tracers/pallas_call | solution.py:524
  37.6 0.0 all-to-all-done
  37.7 0.0 copy-start
  37.7 0.1 collective-permute-start.3
  37.8 6.4 %collective-permute-start.2 = (f32[10,64,512]{2,1,0:T(8,128)}, f32[10,64,512]{2,1,0:T(8,128)}, u32[]{:S(2)}, u32[]{:S(2)}) collective-permute-start(f32[10,64,512]{2,1,0:T(8,128)} %get-tuple-element.39), channel_id=1, source_target_pairs={{0,2},{2,4},{4,6},{6,8},{8,10},{10,12},{12,14},{14,16},{16,18},{18... | collective-permute-start | bytes 3932168 | tf_op jit(solution)/shard_map/ppermute | solution.py:573
  44.2 3.8 %edge_spectrum.1.edge_at = f32[5,64,512]{2,1,0:T(8,128)} custom-call(f32[11,64,512]{2,1,0:T(8,128)} %collective-permute-done.before, f32[6,64,512]{2,1,0:T(8,128)} %collective-permute-done.1.after, bf16[512,512]{1,0:T(8,128)(2,1)} %constant.6.clone.refs_1_.table_hi.refs_4_, bf16[512,512]{1,0:T(8,128)(2,1)} %constant.7.clone.refs_2_.table_lo.refs_5_), custom_call_target="tpu_custom_call" | custom-call | flops 2000000 | bytes 6000000 | tf_op jit(solution)/shard_map/edge_spectrum/pallas_call | solution.py:487
  48.0 0.1 collective-permute-start.5
  48.1 0.0 copy-done
  48.1 0.7 group_moments.1
  48.8 6.7 %all-to-all-start.1 = ((f32[8,2,8,256]{3,2,1,0:T(8,128)}), f32[8,2,8,256]{3,2,1,0:T(8,128)S(1)}, u32[]{:S(2)}, u32[]{:S(2)}) async-start(f32[8,2,8,256]{3,2,1,0:T(8,128)} %group_moments.1), calls=%async_computation.1 | async-start | bytes 262144 | tf_op jit(solution)/shard_map/all_to_all | solution.py:653
  55.6 1.4 %collective-permute-start.4 = (f32[6,64,512]{2,1,0:T(8,128)}, f32[6,64,512]{2,1,0:T(8,128)}, u32[]{:S(2)}, u32[]{:S(2)}) collective-permute-start(f32[6,64,512]{2,1,0:T(8,128)} %get-tuple-element.41.own_at), channel_id=1, source_target_pairs={{0,1},{1,0},{2,3},{3,2},{4,5},{5,4},{6,7},{7,6},{8,9},{9,8},{10,11... | collective-permute-start | bytes 2359304 | tf_op jit(solution)/shard_map/ppermute | solution.py:579
  57.0 3.3 %all-to-all-done.1.rings = f32[8,2,8,256]{3,2,1,0:T(8,128)S(1)} async-done(((f32[8,2,8,256]{3,2,1,0:T(8,128)}), f32[8,2,8,256]{3,2,1,0:T(8,128)S(1)}, u32[]{:S(2)}, u32[]{:S(2)}) %all-to-all-start.1) | async-done | bytes 131104 | tf_op jit(solution)/shard_map/all_to_all | solution.py:653
  60.3 0.8 group_carries.1
  61.2 0.0 collective-permute-start.7
  61.2 23.4 %collective-permute-done.5.edge_other_at = f32[5,64,512]{2,1,0:T(8,128)S(1)} collective-permute-done((f32[5,64,512]{2,1,0:T(8,128)}, f32[5,64,512]{2,1,0:T(8,128)S(1)}, u32[]{:S(2)}, u32[]{:S(2)}) %collective-permute-start.5) | collective-permute-done | bytes 655392 | tf_op jit(solution)/shard_map/ppermute | solution.py:579
  84.6 0.0 copy-start.2
  84.6 0.0 collective-permute-start.6
  84.6 0.8 copy-done.2
  85.5 4.4 %all-to-all-start.2 = ((f32[32,2,8,256]{3,2,1,0:T(8,128)}), f32[32,2,8,256]{3,2,1,0:T(8,128)S(1)}, u32[]{:S(2)}, u32[]{:S(2)}) async-start(f32[32,2,8,256]{3,2,1,0:T(8,128)} %bitcast.10), calls=%async_computation.2 | async-start | bytes 1048576 | tf_op jit(solution)/shard_map/all_to_all | solution.py:664
  89.9 15.4 %collective-permute-done.4.own_other_at = f32[6,64,512]{2,1,0:T(8,128)} collective-permute-done((f32[6,64,512]{2,1,0:T(8,128)}, f32[6,64,512]{2,1,0:T(8,128)}, u32[]{:S(2)}, u32[]{:S(2)}) %collective-permute-start.4) | collective-permute-done | bytes 786464 | tf_op jit(solution)/shard_map/ppermute | solution.py:579
  105.3 3.7 %mode_source.1.refs_0_ = f32[11,128,512]{2,1,0:T(8,128)} custom-call(f32[6,64,512]{2,1,0:T(8,128)} %get-tuple-element.41.own_at, f32[5,64,512]{2,1,0:T(8,128)} %edge_spectrum.1.edge_at, f32[6,64,512]{2,1,0:T(8,128)} %collective-permute-done.4.own_other_at, f32[5,64,512]{2,1,0:T(8,128)} %copy-done.2, f32[128,128]{1,0:T(8,128)} %depth_at.1), custom_call_target="tpu_custom_call" | custom-call | flops 4000000 | bytes 12000000 | tf_op jit(solution)/shard_map/mode_source/pallas_call | solution.py:504
  109.0 0.0 all-to-all-done.2.refs_1_
  109.0 0.0 copy-start.1
  109.1 0.8 copy-done.1
  109.8 8.7 %pressure.1 = (f32[6,64,512]{2,1,0:T(8,128)}, f32[7,64,512]{2,1,0:T(8,128)}) custom-call(f32[11,128,512]{2,1,0:T(8,128)} %mode_source.1.refs_0_, f32[32,2,8,256]{3,2,1,0:T(8,128)} %copy-done.1, f32[3,128,512]{2,1,0:T(8,128)} %get-tuple-element.47.refs_2_, f32[128,128]{1,0:T(8,128)} %refs_3_.3, bf16[512,512]{1,0:T(8,128)(2,1)} %constant.6.clone.refs_1_.table_hi.refs_4_, ...), custom_call_target="tpu_custom_call" | custom-call | flops 7000000 | bytes 21000000 | tf_op jit(solution)/shard_map/pressure/pallas_call | solution.py:504
  118.6 0.0 collective-permute-done.6.from_left
  118.6 0.0 collective-permute-done.7.from_right
  118.6 0.0 collective-permute-done.2.before
  118.6 0.0 collective-permute-done.3.after
  118.6 10.5 %flow.1 = (f32[6,64,512]{2,1,0:T(8,128)}, f32[6,64,512]{2,1,0:T(8,128)}, f32[6,64,512]{2,1,0:T(8,128)}, f32[6,64,512]{2,1,0:T(8,128)}) custom-call(f32[6,64,512]{2,1,0:T(8,128)} %bitcast.30, f32[6,64,512]{2,1,0:T(8,128)} %bitcast.20, f32[6,64,512]{2,1,0:T(8,128)} %bitcast.32, f32[10,64,512]{2,1,0:T(8,128)} %collective-permute-done.2.before, ...), custom_call_target="tpu_custom_call" | custom-call | flops 7000000 | bytes 21000000 | tf_op jit(solution)/shard_map/flow/pallas_call | solution.py:524
Async XLA Ops:
  3.6 23.8 %collective-permute-start = (f32[11,64,512]{2,1,0:T(8,128)}, f32[11,64,512]{2,1,0:T(8,128)}, u32[]{:S(2)}, u32[]{:S(2)}) collective-permute-start(f32[11,64,512]{2,1,0:T(8,128)} %get-tuple-element.36), channel_id=1, source_target_pairs={{0,2},{2,4},{4,6},{6,8},{8,10},{10,12},{12,14},{14,16},{16,18},{18... | collective-permute-start | bytes 4325384 | tf_op jit(solution)/shard_map/ppermute | solution.py:573
  7.1 15.3 %collective-permute-start.1 = (f32[6,64,512]{2,1,0:T(8,128)}, f32[6,64,512]{2,1,0:T(8,128)}, u32[]{:S(2)}, u32[]{:S(2)}) collective-permute-start(f32[6,64,512]{2,1,0:T(8,128)} %get-tuple-element.37), channel_id=1, source_target_pairs={{2,0},{4,2},{6,4},{8,6},{10,8},{12,10},{14,12},{16,14},{18,16},{20... | collective-permute-start | bytes 2359304 | tf_op jit(solution)/shard_map/ppermute | solution.py:576
  13.3 24.4 %all-to-all-start = ((f32[32,2,8,256]{3,2,1,0:T(8,128)}), f32[32,2,8,256]{3,2,1,0:T(8,128)S(1)}, u32[]{:S(2)}, u32[]{:S(2)}) async-start(f32[32,2,8,256]{3,2,1,0:T(8,128)} %get-tuple-element.32), calls=%async_computation | async-start | bytes 1048576 | tf_op jit(solution)/shard_map/all_to_all | solution.py:620
  37.7 10.5 %copy-start = (f32[8,256]{1,0:T(8,128)S(1)}, f32[8,256]{1,0:T(8,128)}, u32[]{:S(2)}) copy-start(f32[8,256]{1,0:T(8,128)} %get-tuple-element.43.decay) | copy-start | bytes 24580
  37.7 80.9 %collective-permute-start.3 = (f32[11,64,512]{2,1,0:T(8,128)}, f32[11,64,512]{2,1,0:T(8,128)}, u32[]{:S(2)}, u32[]{:S(2)}) collective-permute-start(f32[11,64,512]{2,1,0:T(8,128)} %get-tuple-element.40), channel_id=1, source_target_pairs={{2,0},{4,2},{6,4},{8,6},{10,8},{12,10},{14,12},{16,14},{18,16},{20... | collective-permute-start | bytes 4325384 | tf_op jit(solution)/shard_map/ppermute | solution.py:576
  37.8 80.8 %collective-permute-start.2 = (f32[10,64,512]{2,1,0:T(8,128)}, f32[10,64,512]{2,1,0:T(8,128)}, u32[]{:S(2)}, u32[]{:S(2)}) collective-permute-start(f32[10,64,512]{2,1,0:T(8,128)} %get-tuple-element.39), channel_id=1, source_target_pairs={{0,2},{2,4},{4,6},{6,8},{8,10},{10,12},{12,14},{14,16},{16,18},{18... | collective-permute-start | bytes 3932168 | tf_op jit(solution)/shard_map/ppermute | solution.py:573
  48.0 36.6 %collective-permute-start.5 = (f32[5,64,512]{2,1,0:T(8,128)}, f32[5,64,512]{2,1,0:T(8,128)S(1)}, u32[]{:S(2)}, u32[]{:S(2)}) collective-permute-start(f32[5,64,512]{2,1,0:T(8,128)} %edge_spectrum.1.edge_at), channel_id=1, source_target_pairs={{0,1},{1,0},{2,3},{3,2},{4,5},{5,4},{6,7},{7,6},{8,9},{9,8},{10,11... | collective-permute-start | bytes 1966088 | tf_op jit(solution)/shard_map/ppermute | solution.py:579
  48.8 11.5 %all-to-all-start.1 = ((f32[8,2,8,256]{3,2,1,0:T(8,128)}), f32[8,2,8,256]{3,2,1,0:T(8,128)S(1)}, u32[]{:S(2)}, u32[]{:S(2)}) async-start(f32[8,2,8,256]{3,2,1,0:T(8,128)} %group_moments.1), calls=%async_computation.1 | async-start | bytes 262144 | tf_op jit(solution)/shard_map/all_to_all | solution.py:653
  55.6 49.7 %collective-permute-start.4 = (f32[6,64,512]{2,1,0:T(8,128)}, f32[6,64,512]{2,1,0:T(8,128)}, u32[]{:S(2)}, u32[]{:S(2)}) collective-permute-start(f32[6,64,512]{2,1,0:T(8,128)} %get-tuple-element.41.own_at), channel_id=1, source_target_pairs={{0,1},{1,0},{2,3},{3,2},{4,5},{5,4},{6,7},{7,6},{8,9},{9,8},{10,11... | collective-permute-start | bytes 2359304 | tf_op jit(solution)/shard_map/ppermute | solution.py:579
  61.2 57.4 %collective-permute-start.7 = (f32[6,64,512]{2,1,0:T(8,128)}, f32[6,64,512]{2,1,0:T(8,128)}, u32[]{:S(2)}, u32[]{:S(2)}) collective-permute-start(f32[6,64,512]{2,1,0:T(8,128)} %get-tuple-element.54), channel_id=1, source_target_pairs={{2,0},{4,2},{6,4},{8,6},{10,8},{12,10},{14,12},{16,14},{18,16},{20... | collective-permute-start | bytes 2359304 | tf_op jit(solution)/shard_map/ppermute | solution.py:576
  84.6 0.8 copy-start.2
  84.6 33.9 %collective-permute-start.6 = (f32[4,64,512]{2,1,0:T(8,128)}, f32[4,64,512]{2,1,0:T(8,128)}, u32[]{:S(2)}, u32[]{:S(2)}) collective-permute-start(f32[4,64,512]{2,1,0:T(8,128)} %get-tuple-element.53), channel_id=1, source_target_pairs={{0,2},{2,4},{4,6},{6,8},{8,10},{10,12},{12,14},{14,16},{16,18},{18... | collective-permute-start | bytes 1572872 | tf_op jit(solution)/shard_map/ppermute | solution.py:573
  85.5 23.6 %all-to-all-start.2 = ((f32[32,2,8,256]{3,2,1,0:T(8,128)}), f32[32,2,8,256]{3,2,1,0:T(8,128)S(1)}, u32[]{:S(2)}, u32[]{:S(2)}) async-start(f32[32,2,8,256]{3,2,1,0:T(8,128)} %bitcast.10), calls=%async_computation.2 | async-start | bytes 1048576 | tf_op jit(solution)/shard_map/all_to_all | solution.py:664
  109.0 0.8 copy-start.1

commit v5 on v4

--- a/solution.py
+++ b/solution.py
@@ -626,12 +626,9 @@
         name="tracers",
         counts={5: 8, 6: 4},
     )
-    gathered, late, flow_right, flow_left, t_base = lax.optimization_barrier(
-        (gathered, spec, flow_right, flow_left, t_base)
-    )
+    spec_other = other_half(spec)
+    gathered, t_base, spec_other = lax.optimization_barrier((gathered, t_base, spec_other))
     gathered = gathered.reshape(places, chunks // places, 2, rows, width)
-    spec_other = other_half(late)
-    flow_before, flow_after = to_right(flow_right), to_left(flow_left)
     edge = call(
         halo_kernel,
         like(5, levels, columns),
@@ -650,16 +647,15 @@
         us=1.0,
         name="group_moments",
     )
+    ring, flow_right, flow_left = lax.optimization_barrier((ring, flow_right, flow_left))
     ring = lax.all_to_all(ring, "z", 0, 0, tiled=True)
+    flow_before, flow_after = to_right(flow_right), to_left(flow_left)
     carries = near(
         carry_kernel,
         like(places, chunks // places, 2, rows, width),
         gathered, ring, decay,
         us=1.0,
         name="group_carries",
-    )
-    carries, to_left_part, to_right_part = lax.optimization_barrier(
-        (carries, to_left_part, to_right_part)
     )
     carries = lax.all_to_all(carries.reshape(chunks, 2, rows, width), GROUP_ALL, 0, 0, tiled=True)
     from_right = to_left(to_left_part)

time: 130 us -> 126 us (0.969); the launches traced: 129 us -> 124 us
  waiting for transfers between devices: 48.9 us -> 25.9 us
  starting transfers between devices: 30.2 us -> 48.7 us
    ppermute x2, waiting for transfers between devices: 38.8 us -> 12.1 us  [other_half(): return lax.ppermute(block, 'gz', [(0, 1), (1, 0)])]
    all_to_all x1, waiting for transfers between devices: 0.01 us -> 12.5 us  [shards(): gathered = lax.all_to_all(sums, GROUP_ALL, 0, 0, tiled=True)]
    all_to_all x1, starting transfers between devices: 4.43 us -> 16.3 us  [shards(): lax.all_to_all(carries.reshape(chunks, 2, rows, width), GROUP_ALL, 0, 0,...]
    ppermute x3, starting transfers between devices: 9.91 us -> 15.2 us  [to_right(): lax.ppermute(block, ALONG, [(i, (i + 1) % across) for i in range(across)])]
    ppermute x3, waiting for transfers between devices: 5.02 us -> 0.91 us  [to_right(): lax.ppermute(block, ALONG, [(i, (i + 1) % across) for i in range(across)])]
    all_to_all x1, waiting for transfers between devices: 3.34 us -> 0.01 us  [shards(): ring = lax.all_to_all(ring, 'z', 0, 0, tiled=True)]
    ppermute x3, waiting for transfers between devices: 1.67 us -> 0.31 us  [to_left(): lax.ppermute(block, ALONG, [((i + 1) % across, i) for i in range(across)])]
  transfers between devices with their start and end apart: 11 -> 11, of which waited for: 5 -> 4; matrix products, arithmetic and copies ran while one was open for 0% -> 0% of each run, Pallas kernels for 26% -> 27%
where the time goes in v5:
time: 126 us; the launch traced here: 124 us
  starting transfers between devices  48.7 us (39%)
  Pallas kernels  47.7 us (38%)
  waiting for transfers between devices  25.9 us (21%)
    pallas_call x2, Pallas kernels, by_rows(): pl.pallas_call(kernel, grid=(levels // ROWS,), out_shape=outs, in_specs=[...  20.7 us
    all_to_all x1, starting transfers between devices, shards(): lax.all_to_all(carries.reshape(chunks, 2, rows, width), GROUP_ALL, 0, 0,...  16.3 us
    ppermute x3, starting transfers between devices, to_right(): lax.ppermute(block, ALONG, [(i, (i + 1) % across) for i in range(across)])  15.2 us
    pallas_call x4, Pallas kernels, near(): pl.pallas_call(kernel, out_shape=outs, in_specs=[AWAY if k in away else w...  14 us
    pallas_call x3, Pallas kernels, call(): pl.pallas_call(kernel, grid=(1,), out_shape=outs, in_specs=[AWAY if k in...  12.9 us
    all_to_all x1, waiting for transfers between devices, shards(): gathered = lax.all_to_all(sums, GROUP_ALL, 0, 0, tiled=True)  12.5 us
    ppermute x2, waiting for transfers between devices, other_half(): return lax.ppermute(block, 'gz', [(0, 1), (1, 0)])  12.1 us
    all_to_all x1, starting transfers between devices, shards(): gathered = lax.all_to_all(sums, GROUP_ALL, 0, 0, tiled=True)  8.46 us
  transfers between devices with their start and end apart: 11, of which 4 were waited for; matrix products, arithmetic and copies ran while one was open for 0% of the time, Pallas kernels for 27%

profile of v5, /device:TPU:103, one launch (start us, length us, event | category | flops | bytes accessed | tf_op | source)
XLA Modules:
  0.0 123.8 jit_solution(12508030271869926077)
XLA Ops:
  0.6 3.0 %pack.1 = (f32[11,64,512]{2,1,0:T(8,128)}, f32[6,64,512]{2,1,0:T(8,128)}) custom-call(f32[6,64,512]{2,1,0:T(8,128)} %bitcast.33, f32[6,64,512]{2,1,0:T(8,128)} %bitcast.21, f32[6,64,512]{2,1,0:T(8,128)} %bitcast.23, f32[6,64,512]{2,1,0:T(8,128)} %bitcast.25, f32[6,64,512]{2,1,0:T(8,128)} %bitcast.27), custom_call_target="tpu_custom_call" | custom-call | flops 2000000 | bytes 6000000 | tf_op jit(solution)/shard_map/pack/pallas_call | solution.py:487
  3.6 3.5 %collective-permute-start = (f32[11,64,512]{2,1,0:T(8,128)}, f32[11,64,512]{2,1,0:T(8,128)}, u32[]{:S(2)}, u32[]{:S(2)}) collective-permute-start(f32[11,64,512]{2,1,0:T(8,128)} %get-tuple-element.31), channel_id=1, source_target_pairs={{0,2},{2,4},{4,6},{6,8},{8,10},{10,12},{12,14},{14,16},{16,18},{18... | collective-permute-start | bytes 4325384 | tf_op jit(solution)/shard_map/ppermute | solution.py:573
  7.1 0.0 collective-permute-start.1
  7.1 6.2 %block_moments.1 = (f32[6,64,512]{2,1,0:T(8,128)}, f32[3,128,512]{2,1,0:T(8,128)}, f32[32,2,8,256]{3,2,1,0:T(8,128)}, f32[8,256]{1,0:T(8,128)}, f32[10,64,512]{2,1,0:T(8,128)}, /*index=5*/f32[11,64,512]{2,1,0:T(8,128)}) custom-call(f32[6,64,512]{2,1,0:T(8,128)} %bitcast.34, bf16[512,512]{1,0:T(8,128)(2,1)} %constant.6.clone.refs_1_.table_hi.refs_4_, ...), custom_call_target="tpu_custom_call" | custom-call | flops 5000000 | bytes 15000000 | tf_op jit(solution)/shard_map/block_moments/pallas_call | solution.py:487
  13.3 0.5 collective-permute-start.2
  13.7 8.5 %all-to-all-start = ((f32[32,2,8,256]{3,2,1,0:T(8,128)}), f32[32,2,8,256]{3,2,1,0:T(8,128)S(1)}, u32[]{:S(2)}, u32[]{:S(2)}) async-start(f32[32,2,8,256]{3,2,1,0:T(8,128)} %get-tuple-element.30), calls=%async_computation | async-start | bytes 1048576 | tf_op jit(solution)/shard_map/all_to_all | solution.py:620
  22.2 0.0 copy-start
  22.2 0.3 collective-permute-done.1.after
  22.5 0.9 collective-permute-done.before
  23.4 10.2 %tracers.1 = (f32[6,64,512]{2,1,0:T(8,128)}, f32[6,64,512]{2,1,0:T(8,128)}, f32[6,64,512]{2,1,0:T(8,128)}, f32[6,64,512]{2,1,0:T(8,128)}, f32[4,64,512]{2,1,0:T(8,128)}) custom-call(f32[6,64,512]{2,1,0:T(8,128)} %bitcast.22, f32[6,64,512]{2,1,0:T(8,128)} %bitcast.24, f32[6,64,512]{2,1,0:T(8,128)} %bitcast.19, f32[6,64,512]{2,1,0:T(8,128)} %bitcast.26, ...), custom_call_target="tpu_custom_call" | custom-call | flops 9000000 | bytes 27000000 | tf_op jit(solution)/shard_map/tracers/pallas_call | solution.py:524
  33.7 12.5 %all-to-all-done = f32[32,2,8,256]{3,2,1,0:T(8,128)S(1)} async-done(((f32[32,2,8,256]{3,2,1,0:T(8,128)}), f32[32,2,8,256]{3,2,1,0:T(8,128)S(1)}, u32[]{:S(2)}, u32[]{:S(2)}) %all-to-all-start) | async-done | bytes 524320 | tf_op jit(solution)/shard_map/all_to_all | solution.py:620
  46.2 0.0 collective-permute-done.2.own_other_at
  46.2 0.0 copy-done
  46.2 0.7 group_moments.1
  46.9 0.2 collective-permute-start.4
  47.1 5.4 %collective-permute-start.3 = (f32[10,64,512]{2,1,0:T(8,128)}, f32[10,64,512]{2,1,0:T(8,128)}, u32[]{:S(2)}, u32[]{:S(2)}) collective-permute-start(f32[10,64,512]{2,1,0:T(8,128)} %get-tuple-element.39), channel_id=1, source_target_pairs={{0,2},{2,4},{4,6},{6,8},{8,10},{10,12},{12,14},{14,16},{16,18},{18... | collective-permute-start | bytes 3932168 | tf_op jit(solution)/shard_map/ppermute | solution.py:573
  52.5 0.0 collective-permute-start.7
  52.5 7.9 %all-to-all-start.1 = ((f32[8,2,8,256]{3,2,1,0:T(8,128)}), f32[8,2,8,256]{3,2,1,0:T(8,128)S(1)}, u32[]{:S(2)}, u32[]{:S(2)}) async-start(f32[8,2,8,256]{3,2,1,0:T(8,128)} %group_moments.1), calls=%async_computation.1 | async-start | bytes 262144 | tf_op jit(solution)/shard_map/all_to_all | solution.py:651
  60.5 3.8 %edge_spectrum.1.edge_at = f32[5,64,512]{2,1,0:T(8,128)} custom-call(f32[11,64,512]{2,1,0:T(8,128)} %collective-permute-done.before, f32[6,64,512]{2,1,0:T(8,128)} %collective-permute-done.1.after, bf16[512,512]{1,0:T(8,128)(2,1)} %constant.6.clone.refs_1_.table_hi.refs_4_, bf16[512,512]{1,0:T(8,128)(2,1)} %constant.7.clone.refs_2_.table_lo.refs_5_), custom_call_target="tpu_custom_call" | custom-call | flops 2000000 | bytes 6000000 | tf_op jit(solution)/shard_map/edge_spectrum/pallas_call | solution.py:487
  64.3 0.1 collective-permute-start.5
  64.4 6.3 %collective-permute-start.6 = (f32[4,64,512]{2,1,0:T(8,128)}, f32[4,64,512]{2,1,0:T(8,128)}, u32[]{:S(2)}, u32[]{:S(2)}) collective-permute-start(f32[4,64,512]{2,1,0:T(8,128)} %get-tuple-element.49), channel_id=1, source_target_pairs={{0,2},{2,4},{4,6},{6,8},{8,10},{10,12},{12,14},{14,16},{16,18},{18... | collective-permute-start | bytes 1572872 | tf_op jit(solution)/shard_map/ppermute | solution.py:573
  70.7 0.0 all-to-all-done.1.rings
  70.7 0.8 group_carries.1
  71.6 16.3 %all-to-all-start.2 = ((f32[32,2,8,256]{3,2,1,0:T(8,128)}), f32[32,2,8,256]{3,2,1,0:T(8,128)S(1)}, u32[]{:S(2)}, u32[]{:S(2)}) async-start(f32[32,2,8,256]{3,2,1,0:T(8,128)} %bitcast.10), calls=%async_computation.2 | async-start | bytes 1048576 | tf_op jit(solution)/shard_map/all_to_all | solution.py:660
  87.9 12.1 %collective-permute-done.5.edge_other_at = f32[5,64,512]{2,1,0:T(8,128)} collective-permute-done((f32[5,64,512]{2,1,0:T(8,128)}, f32[5,64,512]{2,1,0:T(8,128)}, u32[]{:S(2)}, u32[]{:S(2)}) %collective-permute-start.5) | collective-permute-done | bytes 655392 | tf_op jit(solution)/shard_map/ppermute | solution.py:579
  100.0 3.7 %mode_source.1.refs_0_ = f32[11,128,512]{2,1,0:T(8,128)} custom-call(f32[6,64,512]{2,1,0:T(8,128)} %get-tuple-element.34.own_at, f32[5,64,512]{2,1,0:T(8,128)} %edge_spectrum.1.edge_at, f32[6,64,512]{2,1,0:T(8,128)} %collective-permute-done.2.own_other_at, f32[5,64,512]{2,1,0:T(8,128)} %collective-permute-done.5.edge_other_at, f32[128,128]{1,0:T(8,128)} %depth_at.1), custom_call_target="tpu_custom_call" | custom-call | flops 4000000 | bytes 12000000 | tf_op jit(solution)/shard_map/mode_source/pallas_call | solution.py:504
  103.7 0.0 all-to-all-done.2.refs_1_
  103.7 0.0 copy-start.1
  103.7 0.8 copy-done.1
  104.5 8.7 %pressure.1 = (f32[6,64,512]{2,1,0:T(8,128)}, f32[7,64,512]{2,1,0:T(8,128)}) custom-call(f32[11,128,512]{2,1,0:T(8,128)} %mode_source.1.refs_0_, f32[32,2,8,256]{3,2,1,0:T(8,128)} %copy-done.1, f32[3,128,512]{2,1,0:T(8,128)} %get-tuple-element.43.refs_2_, f32[128,128]{1,0:T(8,128)} %refs_3_.3, bf16[512,512]{1,0:T(8,128)(2,1)} %constant.6.clone.refs_1_.table_hi.refs_4_, ...), custom_call_target="tpu_custom_call" | custom-call | flops 7000000 | bytes 21000000 | tf_op jit(solution)/shard_map/pressure/pallas_call | solution.py:504
  113.3 0.0 collective-permute-done.6.from_left
  113.3 0.0 collective-permute-done.7.from_right
  113.3 0.0 collective-permute-done.3.before
  113.3 0.0 collective-permute-done.4.after
  113.3 10.5 %flow.1 = (f32[6,64,512]{2,1,0:T(8,128)}, f32[6,64,512]{2,1,0:T(8,128)}, f32[6,64,512]{2,1,0:T(8,128)}, f32[6,64,512]{2,1,0:T(8,128)}) custom-call(f32[6,64,512]{2,1,0:T(8,128)} %bitcast.30, f32[6,64,512]{2,1,0:T(8,128)} %bitcast.20, f32[6,64,512]{2,1,0:T(8,128)} %bitcast.32, f32[10,64,512]{2,1,0:T(8,128)} %collective-permute-done.3.before, ...), custom_call_target="tpu_custom_call" | custom-call | flops 7000000 | bytes 21000000 | tf_op jit(solution)/shard_map/flow/pallas_call | solution.py:524
Async XLA Ops:
  3.6 19.8 %collective-permute-start = (f32[11,64,512]{2,1,0:T(8,128)}, f32[11,64,512]{2,1,0:T(8,128)}, u32[]{:S(2)}, u32[]{:S(2)}) collective-permute-start(f32[11,64,512]{2,1,0:T(8,128)} %get-tuple-element.31), channel_id=1, source_target_pairs={{0,2},{2,4},{4,6},{6,8},{8,10},{10,12},{12,14},{14,16},{16,18},{18... | collective-permute-start | bytes 4325384 | tf_op jit(solution)/shard_map/ppermute | solution.py:573
  7.1 15.4 %collective-permute-start.1 = (f32[6,64,512]{2,1,0:T(8,128)}, f32[6,64,512]{2,1,0:T(8,128)}, u32[]{:S(2)}, u32[]{:S(2)}) collective-permute-start(f32[6,64,512]{2,1,0:T(8,128)} %get-tuple-element.32), channel_id=1, source_target_pairs={{2,0},{4,2},{6,4},{8,6},{10,8},{12,10},{14,12},{16,14},{18,16},{20... | collective-permute-start | bytes 2359304 | tf_op jit(solution)/shard_map/ppermute | solution.py:576
  13.3 32.9 %collective-permute-start.2 = (f32[6,64,512]{2,1,0:T(8,128)}, f32[6,64,512]{2,1,0:T(8,128)}, u32[]{:S(2)}, u32[]{:S(2)}) collective-permute-start(f32[6,64,512]{2,1,0:T(8,128)} %get-tuple-element.34.own_at), channel_id=1, source_target_pairs={{0,1},{1,0},{2,3},{3,2},{4,5},{5,4},{6,7},{7,6},{8,9},{9,8},{10,11... | collective-permute-start | bytes 2359304 | tf_op jit(solution)/shard_map/ppermute | solution.py:579
  13.7 32.4 %all-to-all-start = ((f32[32,2,8,256]{3,2,1,0:T(8,128)}), f32[32,2,8,256]{3,2,1,0:T(8,128)S(1)}, u32[]{:S(2)}, u32[]{:S(2)}) async-start(f32[32,2,8,256]{3,2,1,0:T(8,128)} %get-tuple-element.30), calls=%async_computation | async-start | bytes 1048576 | tf_op jit(solution)/shard_map/all_to_all | solution.py:620
  22.2 24.0 %copy-start = (f32[8,256]{1,0:T(8,128)S(1)}, f32[8,256]{1,0:T(8,128)}, u32[]{:S(2)}) copy-start(f32[8,256]{1,0:T(8,128)} %get-tuple-element.36.decay) | copy-start | bytes 24580
  46.9 66.4 %collective-permute-start.4 = (f32[11,64,512]{2,1,0:T(8,128)}, f32[11,64,512]{2,1,0:T(8,128)}, u32[]{:S(2)}, u32[]{:S(2)}) collective-permute-start(f32[11,64,512]{2,1,0:T(8,128)} %get-tuple-element.40), channel_id=1, source_target_pairs={{2,0},{4,2},{6,4},{8,6},{10,8},{12,10},{14,12},{16,14},{18,16},{20... | collective-permute-start | bytes 4325384 | tf_op jit(solution)/shard_map/ppermute | solution.py:576
  47.1 66.1 %collective-permute-start.3 = (f32[10,64,512]{2,1,0:T(8,128)}, f32[10,64,512]{2,1,0:T(8,128)}, u32[]{:S(2)}, u32[]{:S(2)}) collective-permute-start(f32[10,64,512]{2,1,0:T(8,128)} %get-tuple-element.39), channel_id=1, source_target_pairs={{0,2},{2,4},{4,6},{6,8},{8,10},{10,12},{12,14},{14,16},{16,18},{18... | collective-permute-start | bytes 3932168 | tf_op jit(solution)/shard_map/ppermute | solution.py:573
  52.5 60.7 %collective-permute-start.7 = (f32[6,64,512]{2,1,0:T(8,128)}, f32[6,64,512]{2,1,0:T(8,128)}, u32[]{:S(2)}, u32[]{:S(2)}) collective-permute-start(f32[6,64,512]{2,1,0:T(8,128)} %get-tuple-element.50), channel_id=1, source_target_pairs={{2,0},{4,2},{6,4},{8,6},{10,8},{12,10},{14,12},{16,14},{18,16},{20... | collective-permute-start | bytes 2359304 | tf_op jit(solution)/shard_map/ppermute | solution.py:576
  52.5 18.2 %all-to-all-start.1 = ((f32[8,2,8,256]{3,2,1,0:T(8,128)}), f32[8,2,8,256]{3,2,1,0:T(8,128)S(1)}, u32[]{:S(2)}, u32[]{:S(2)}) async-start(f32[8,2,8,256]{3,2,1,0:T(8,128)} %group_moments.1), calls=%async_computation.1 | async-start | bytes 262144 | tf_op jit(solution)/shard_map/all_to_all | solution.py:651
  64.3 35.7 %collective-permute-start.5 = (f32[5,64,512]{2,1,0:T(8,128)}, f32[5,64,512]{2,1,0:T(8,128)}, u32[]{:S(2)}, u32[]{:S(2)}) collective-permute-start(f32[5,64,512]{2,1,0:T(8,128)} %edge_spectrum.1.edge_at), channel_id=1, source_target_pairs={{0,1},{1,0},{2,3},{3,2},{4,5},{5,4},{6,7},{7,6},{8,9},{9,8},{10,11... | collective-permute-start | bytes 1966088 | tf_op jit(solution)/shard_map/ppermute | solution.py:579
  64.4 48.9 %collective-permute-start.6 = (f32[4,64,512]{2,1,0:T(8,128)}, f32[4,64,512]{2,1,0:T(8,128)}, u32[]{:S(2)}, u32[]{:S(2)}) collective-permute-start(f32[4,64,512]{2,1,0:T(8,128)} %get-tuple-element.49), channel_id=1, source_target_pairs={{0,2},{2,4},{4,6},{6,8},{8,10},{10,12},{12,14},{14,16},{16,18},{18... | collective-permute-start | bytes 1572872 | tf_op jit(solution)/shard_map/ppermute | solution.py:573
  71.6 32.2 %all-to-all-start.2 = ((f32[32,2,8,256]{3,2,1,0:T(8,128)}), f32[32,2,8,256]{3,2,1,0:T(8,128)S(1)}, u32[]{:S(2)}, u32[]{:S(2)}) async-start(f32[32,2,8,256]{3,2,1,0:T(8,128)} %bitcast.10), calls=%async_computation.2 | async-start | bytes 1048576 | tf_op jit(solution)/shard_map/all_to_all | solution.py:660
  103.7 0.8 copy-start.1

commit v6 on v5

--- a/solution.py
+++ b/solution.py
@@ -58,12 +58,17 @@
     return dot(a_hi, b_hi) + (dot(a_hi, b_lo) + dot(a_lo, b_hi))
 
 
-def face_terms(edges, ratio):
+def face_terms(edges, ratio, side=None):
     positive = ratio >= 0.0
-    d1 = jnp.where(positive, edges[0], edges[4])
-    d2 = jnp.where(positive, edges[1], edges[3])
-    d3 = edges[2]
-    d4 = jnp.where(positive, edges[3], edges[1])
+    if side == "left":
+        d1, d2, d3, d4 = edges[0], edges[1], edges[2], edges[3]
+    elif side == "right":
+        d1, d2, d3, d4 = edges[4], edges[3], edges[2], edges[1]
+    else:
+        d1 = jnp.where(positive, edges[0], edges[4])
+        d2 = jnp.where(positive, edges[1], edges[3])
+        d3 = edges[2]
+        d4 = jnp.where(positive, edges[3], edges[1])
     s1, s2, s3 = d2 - d1, d3 - d2, d4 - d3
     e0, e1, e2 = (d2 + d2) + s1, d2 + d3, (d3 + d3) - s3
     t0, t1, t2 = (13.0 / 3.0) * s1, (13.0 / 3.0) * s2, (13.0 / 3.0) * s3
@@ -89,7 +94,7 @@
     return positive, total, (m1, g2, g3, m4)
 
 
-def weno_tile(field, ratio, cotangent, faces, cells, owned):
+def weno_tile(field, ratio, cotangent, faces, cells, owned, ends=()):
     edge_of, edge_bar, cell_bar, ratio_bar = {}, {}, {}, {}
 
     def edge(x):
@@ -105,7 +110,10 @@
 
     for f in faces:
         c, e = ratio(f), cotangent(f)
-        positive, total, (m1, g2, g3, m4) = face_terms([edge(f - 3 + k) for k in range(5)], c)
+        side = ("right" if f == ends[0] else "left" if f == ends[1] else None) if ends else None
+        skip = {"right": 0, "left": 4}.get(side)
+        five = [None if k == skip else edge(f - 3 + k) for k in range(5)]
+        positive, total, (m1, g2, g3, m4) = face_terms(five, c, side)
         gain = (2.0 / 3.0) * (jnp.abs(c) * e)
         m1, g2, g3, m4 = gain * m1, gain * g2, gain * g3, gain * m4
         zero = jnp.zeros_like(m1)
@@ -183,9 +191,9 @@
 
     def tile(l, carry):
         lanes = pl.ds(pl.multiple_of(l * LANES, LANES), LANES)
-        field = planes(u, before, after, n, 0, 5, 0, lanes)
-        ratio = planes(c, before, after, n, 5, 2, 5, lanes)
-        dual = planes(df, before, after, n, 7, 3, 8, lanes)
+        field = planes(u, before, after, n, 0, 4, 0, lanes)
+        ratio = planes(c, before, after, n, 4, 2, 4, lanes)
+        dual = planes(df, before, after, n, 6, 3, 7, lanes)
         head = planes(phi, phi_edge, phi_edge, n, 0, 3, 3, lanes)
         step = {x: head(x) - head(x - 1) for x in range(-2, n + 2)}
 
@@ -203,6 +211,7 @@
             range(-2, n + 3),
             range(n),
             range(n),
+            (-2, n + 2),
         )
         for x in range(n):
             u_out[x, :, lanes] = (df[x, :, lanes] - step[x]) + bars[x]
@@ -227,12 +236,12 @@
         pltpu.make_async_copy(source, target, sems.at[k])
         for k, (source, target) in enumerate(
             (
-                (u.at[n - 5 : n], flow_right.at[0:5]),
-                (c.at[n - 2 : n], flow_right.at[5:7]),
-                (df.at[n - 3 : n], flow_right.at[7:10]),
-                (u.at[0:5], flow_left.at[0:5]),
-                (c.at[0:3], flow_left.at[5:8]),
-                (df.at[0:3], flow_left.at[8:11]),
+                (u.at[n - 4 : n], flow_right.at[0:4]),
+                (c.at[n - 2 : n], flow_right.at[4:6]),
+                (df.at[n - 3 : n], flow_right.at[6:9]),
+                (u.at[0:4], flow_left.at[0:4]),
+                (c.at[0:3], flow_left.at[4:7]),
+                (df.at[0:3], flow_left.at[7:10]),
             )
         )
     ]
@@ -607,8 +616,8 @@
             like(3, modes, columns),
             like(chunks, 2, rows, width),
             like(rows, width),
+            like(9, levels, columns),
             like(10, levels, columns),
-            like(11, levels, columns),
         ],
         head, table_hi, table_lo, depth_into_eigenbasis,
         spectral_magnitudes.reshape(1, modes), waves, u, c, df,
@@ -626,13 +635,15 @@
         name="tracers",
         counts={5: 8, 6: 4},
     )
-    spec_other = other_half(spec)
-    gathered, t_base, spec_other = lax.optimization_barrier((gathered, t_base, spec_other))
+    gathered, t_base, late, edge_before, edge_after = lax.optimization_barrier(
+        (gathered, t_base, spec, before, after)
+    )
+    spec_other = other_half(late)
     gathered = gathered.reshape(places, chunks // places, 2, rows, width)
     edge = call(
         halo_kernel,
         like(5, levels, columns),
-        before, after, table_hi, table_lo,
+        edge_before, edge_after, table_hi, table_lo,
         scratch=[pltpu.VMEM((5, levels, columns), f32), pltpu.SemaphoreType.DMA((2,))],
         away=(0, 1),
         us=2.0,
@@ -650,6 +661,7 @@
     ring, flow_right, flow_left = lax.optimization_barrier((ring, flow_right, flow_left))
     ring = lax.all_to_all(ring, "z", 0, 0, tiled=True)
     flow_before, flow_after = to_right(flow_right), to_left(flow_left)
+    ring, spec_other = lax.optimization_barrier((ring, spec_other))
     carries = near(
         carry_kernel,
         like(places, chunks // places, 2, rows, width),

time: 126 us -> 120 us (0.952)
  starting transfers between devices: 48.7 us -> 31.8 us
  waiting for transfers between devices: 25.9 us -> 37.2 us
    ppermute x2, waiting for transfers between devices: 12.1 us -> 30 us  [other_half(): return lax.ppermute(block, 'gz', [(0, 1), (1, 0)])]
    all_to_all x1, waiting for transfers between devices: 12.5 us -> 0.01 us  [shards(): gathered = lax.all_to_all(sums, GROUP_ALL, 0, 0, tiled=True)]
    all_to_all x1, starting transfers between devices: 16.3 us -> 6.47 us  [shards(): lax.all_to_all(carries.reshape(chunks, 2, rows, width), GROUP_ALL, 0, 0,...]
    ppermute x3, starting transfers between devices: 15.2 us -> 9.85 us  [to_right(): lax.ppermute(block, ALONG, [(i, (i + 1) % across) for i in range(across)])]
    ppermute x3, waiting for transfers between devices: 0.91 us -> 5.07 us  [to_right(): lax.ppermute(block, ALONG, [(i, (i + 1) % across) for i in range(across)])]
    ppermute x3, waiting for transfers between devices: 0.31 us -> 1.79 us  [to_left(): lax.ppermute(block, ALONG, [((i + 1) % across, i) for i in range(across)])]
  transfers between devices with their start and end apart: 11 -> 11, of which waited for: 4 -> 5; matrix products, arithmetic and copies ran while one was open for 0% -> 0% of each run, Pallas kernels for 27% -> 29%
where the time goes in v6:
time: 120 us; the launch traced here: 118 us
  Pallas kernels  47.3 us (39%)
  waiting for transfers between devices  37.2 us (31%)
  starting transfers between devices  31.8 us (26%)
    ppermute x2, waiting for transfers between devices, other_half(): return lax.ppermute(block, 'gz', [(0, 1), (1, 0)])  30 us
    pallas_call x2, Pallas kernels, by_rows(): pl.pallas_call(kernel, grid=(levels // ROWS,), out_shape=outs, in_specs=[...  20.6 us
    pallas_call x4, Pallas kernels, near(): pl.pallas_call(kernel, out_shape=outs, in_specs=[AWAY if k in away else w...  13.9 us
    pallas_call x3, Pallas kernels, call(): pl.pallas_call(kernel, grid=(1,), out_shape=outs, in_specs=[AWAY if k in...  12.8 us
    ppermute x3, starting transfers between devices, to_right(): lax.ppermute(block, ALONG, [(i, (i + 1) % across) for i in range(across)])  9.85 us
    all_to_all x1, starting transfers between devices, shards(): gathered = lax.all_to_all(sums, GROUP_ALL, 0, 0, tiled=True)  7.49 us
    all_to_all x1, starting transfers between devices, shards(): ring = lax.all_to_all(ring, 'z', 0, 0, tiled=True)  6.69 us
    all_to_all x1, starting transfers between devices, shards(): lax.all_to_all(carries.reshape(chunks, 2, rows, width), GROUP_ALL, 0, 0,...  6.47 us
  transfers between devices with their start and end apart: 11, of which 5 were waited for; matrix products, arithmetic and copies ran while one was open for 0% of the time, Pallas kernels for 29%

profile of v6, /device:TPU:103, one launch (start us, length us, event | category | flops | bytes accessed | tf_op | source)
XLA Modules:
  0.0 117.9 jit_solution(536791107098768917)
XLA Ops:
  0.6 3.0 %pack.1 = (f32[11,64,512]{2,1,0:T(8,128)}, f32[6,64,512]{2,1,0:T(8,128)}) custom-call(f32[6,64,512]{2,1,0:T(8,128)} %bitcast.33, f32[6,64,512]{2,1,0:T(8,128)} %bitcast.21, f32[6,64,512]{2,1,0:T(8,128)} %bitcast.23, f32[6,64,512]{2,1,0:T(8,128)} %bitcast.25, f32[6,64,512]{2,1,0:T(8,128)} %bitcast.27), custom_call_target="tpu_custom_call" | custom-call | flops 2000000 | bytes 6000000 | tf_op jit(solution)/shard_map/pack/pallas_call | solution.py:496
  3.6 3.5 %collective-permute-start = (f32[11,64,512]{2,1,0:T(8,128)}, f32[11,64,512]{2,1,0:T(8,128)}, u32[]{:S(2)}, u32[]{:S(2)}) collective-permute-start(f32[11,64,512]{2,1,0:T(8,128)} %get-tuple-element.35), channel_id=1, source_target_pairs={{0,2},{2,4},{4,6},{6,8},{8,10},{10,12},{12,14},{14,16},{16,18},{18... | collective-permute-start | bytes 4325384 | tf_op jit(solution)/shard_map/ppermute | solution.py:582
  7.1 0.0 collective-permute-start.1
  7.1 6.0 %block_moments.1 = (f32[6,64,512]{2,1,0:T(8,128)}, f32[3,128,512]{2,1,0:T(8,128)}, f32[32,2,8,256]{3,2,1,0:T(8,128)}, f32[8,256]{1,0:T(8,128)}, f32[9,64,512]{2,1,0:T(8,128)}, /*index=5*/f32[10,64,512]{2,1,0:T(8,128)}) custom-call(f32[6,64,512]{2,1,0:T(8,128)} %bitcast.34, bf16[512,512]{1,0:T(8,128)(2,1)} %constant.6.clone.refs_1_.table_hi.refs_4_, ...), custom_call_target="tpu_custom_call" | custom-call | flops 5000000 | bytes 15000000 | tf_op jit(solution)/shard_map/block_moments/pallas_call | solution.py:496
  13.1 7.5 %all-to-all-start = ((f32[32,2,8,256]{3,2,1,0:T(8,128)}), f32[32,2,8,256]{3,2,1,0:T(8,128)S(1)}, u32[]{:S(2)}, u32[]{:S(2)}) async-start(f32[32,2,8,256]{3,2,1,0:T(8,128)} %get-tuple-element.34), calls=%async_computation | async-start | bytes 1048576 | tf_op jit(solution)/shard_map/all_to_all | solution.py:629
  20.6 0.0 copy-start
  20.6 1.8 %collective-permute-done.1.after = f32[6,64,512]{2,1,0:T(8,128)} collective-permute-done((f32[6,64,512]{2,1,0:T(8,128)}, f32[6,64,512]{2,1,0:T(8,128)}, u32[]{:S(2)}, u32[]{:S(2)}) %collective-permute-start.1) | collective-permute-done | bytes 786464 | tf_op jit(solution)/shard_map/ppermute | solution.py:585
  22.4 5.1 %collective-permute-done.before = f32[11,64,512]{2,1,0:T(8,128)} collective-permute-done((f32[11,64,512]{2,1,0:T(8,128)}, f32[11,64,512]{2,1,0:T(8,128)}, u32[]{:S(2)}, u32[]{:S(2)}) %collective-permute-start) | collective-permute-done | bytes 1441824 | tf_op jit(solution)/shard_map/ppermute | solution.py:582
  27.5 10.2 %tracers.1 = (f32[6,64,512]{2,1,0:T(8,128)}, f32[6,64,512]{2,1,0:T(8,128)}, f32[6,64,512]{2,1,0:T(8,128)}, f32[6,64,512]{2,1,0:T(8,128)}, f32[4,64,512]{2,1,0:T(8,128)}) custom-call(f32[6,64,512]{2,1,0:T(8,128)} %bitcast.22, f32[6,64,512]{2,1,0:T(8,128)} %bitcast.24, f32[6,64,512]{2,1,0:T(8,128)} %bitcast.19, f32[6,64,512]{2,1,0:T(8,128)} %bitcast.26, ...), custom_call_target="tpu_custom_call" | custom-call | flops 9000000 | bytes 27000000 | tf_op jit(solution)/shard_map/tracers/pallas_call | solution.py:533
  37.7 0.0 all-to-all-done
  37.7 0.1 collective-permute-start.4
  37.8 0.0 copy-done
  37.8 0.7 group_moments.1
  38.5 0.0 collective-permute-start.3
  38.6 6.4 %collective-permute-start.2 = (f32[9,64,512]{2,1,0:T(8,128)}, f32[9,64,512]{2,1,0:T(8,128)}, u32[]{:S(2)}, u32[]{:S(2)}) collective-permute-start(f32[9,64,512]{2,1,0:T(8,128)} %get-tuple-element.43), channel_id=1, source_target_pairs={{0,2},{2,4},{4,6},{6,8},{8,10},{10,12},{12,14},{14,16},{16,18},{18... | collective-permute-start | bytes 3538952 | tf_op jit(solution)/shard_map/ppermute | solution.py:582
  44.9 0.0 collective-permute-start.7
  44.9 6.7 %all-to-all-start.1 = ((f32[8,2,8,256]{3,2,1,0:T(8,128)}), f32[8,2,8,256]{3,2,1,0:T(8,128)S(1)}, u32[]{:S(2)}, u32[]{:S(2)}) async-start(f32[8,2,8,256]{3,2,1,0:T(8,128)} %group_moments.1), calls=%async_computation.1 | async-start | bytes 262144 | tf_op jit(solution)/shard_map/all_to_all | solution.py:662
  51.6 3.8 %edge_spectrum.1.edge_at = f32[5,64,512]{2,1,0:T(8,128)} custom-call(f32[11,64,512]{2,1,0:T(8,128)} %collective-permute-done.before, f32[6,64,512]{2,1,0:T(8,128)} %collective-permute-done.1.after, bf16[512,512]{1,0:T(8,128)(2,1)} %constant.6.clone.refs_1_.table_hi.refs_4_, bf16[512,512]{1,0:T(8,128)(2,1)} %constant.7.clone.refs_2_.table_lo.refs_5_), custom_call_target="tpu_custom_call" | custom-call | flops 2000000 | bytes 6000000 | tf_op jit(solution)/shard_map/edge_spectrum/pallas_call | solution.py:496
  55.4 1.2 %collective-permute-start.5 = (f32[5,64,512]{2,1,0:T(8,128)}, f32[5,64,512]{2,1,0:T(8,128)}, u32[]{:S(2)}, u32[]{:S(2)}) collective-permute-start(f32[5,64,512]{2,1,0:T(8,128)} %edge_spectrum.1.edge_at), channel_id=1, source_target_pairs={{0,1},{1,0},{2,3},{3,2},{4,5},{5,4},{6,7},{7,6},{8,9},{9,8},{10,11... | collective-permute-start | bytes 1966088 | tf_op jit(solution)/shard_map/ppermute | solution.py:588
  56.6 23.6 %collective-permute-done.4.own_other_at = f32[6,64,512]{2,1,0:T(8,128)} collective-permute-done((f32[6,64,512]{2,1,0:T(8,128)}, f32[6,64,512]{2,1,0:T(8,128)}, u32[]{:S(2)}, u32[]{:S(2)}) %collective-permute-start.4) | collective-permute-done | bytes 786464 | tf_op jit(solution)/shard_map/ppermute | solution.py:588
  80.2 0.0 collective-permute-start.6
  80.2 0.0 all-to-all-done.1.rings
  80.2 0.8 group_carries.1
  81.1 6.5 %all-to-all-start.2 = ((f32[32,2,8,256]{3,2,1,0:T(8,128)}), f32[32,2,8,256]{3,2,1,0:T(8,128)S(1)}, u32[]{:S(2)}, u32[]{:S(2)}) async-start(f32[32,2,8,256]{3,2,1,0:T(8,128)} %bitcast.10), calls=%async_computation.2 | async-start | bytes 1048576 | tf_op jit(solution)/shard_map/all_to_all | solution.py:672
  87.6 6.4 %collective-permute-done.5.edge_other_at = f32[5,64,512]{2,1,0:T(8,128)} collective-permute-done((f32[5,64,512]{2,1,0:T(8,128)}, f32[5,64,512]{2,1,0:T(8,128)}, u32[]{:S(2)}, u32[]{:S(2)}) %collective-permute-start.5) | collective-permute-done | bytes 655392 | tf_op jit(solution)/shard_map/ppermute | solution.py:588
  94.0 3.6 %mode_source.1.refs_0_ = f32[11,128,512]{2,1,0:T(8,128)} custom-call(f32[6,64,512]{2,1,0:T(8,128)} %get-tuple-element.48.own_at, f32[5,64,512]{2,1,0:T(8,128)} %edge_spectrum.1.edge_at, f32[6,64,512]{2,1,0:T(8,128)} %collective-permute-done.4.own_other_at, f32[5,64,512]{2,1,0:T(8,128)} %collective-permute-done.5.edge_other_at, f32[128,128]{1,0:T(8,128)} %depth_at.1), custom_call_target="tpu_custom_call" | custom-call | flops 4000000 | bytes 12000000 | tf_op jit(solution)/shard_map/mode_source/pallas_call | solution.py:513
  97.6 0.3 all-to-all-done.2.refs_1_
  98.0 0.0 copy-start.1
  98.0 0.8 copy-done.1
  98.8 8.7 %pressure.1 = (f32[6,64,512]{2,1,0:T(8,128)}, f32[7,64,512]{2,1,0:T(8,128)}) custom-call(f32[11,128,512]{2,1,0:T(8,128)} %mode_source.1.refs_0_, f32[32,2,8,256]{3,2,1,0:T(8,128)} %copy-done.1, f32[3,128,512]{2,1,0:T(8,128)} %get-tuple-element.51.refs_2_, f32[128,128]{1,0:T(8,128)} %refs_3_.3, bf16[512,512]{1,0:T(8,128)(2,1)} %constant.6.clone.refs_1_.table_hi.refs_4_, ...), custom_call_target="tpu_custom_call" | custom-call | flops 7000000 | bytes 21000000 | tf_op jit(solution)/shard_map/pressure/pallas_call | solution.py:513
  107.5 0.0 collective-permute-done.6.from_left
  107.5 0.0 collective-permute-done.7.from_right
  107.5 0.0 collective-permute-done.2.before
  107.5 0.0 collective-permute-done.3.after
  107.5 10.4 %flow.1 = (f32[6,64,512]{2,1,0:T(8,128)}, f32[6,64,512]{2,1,0:T(8,128)}, f32[6,64,512]{2,1,0:T(8,128)}, f32[6,64,512]{2,1,0:T(8,128)}) custom-call(f32[6,64,512]{2,1,0:T(8,128)} %bitcast.30, f32[6,64,512]{2,1,0:T(8,128)} %bitcast.20, f32[6,64,512]{2,1,0:T(8,128)} %bitcast.32, f32[9,64,512]{2,1,0:T(8,128)} %collective-permute-done.2.before, ...), custom_call_target="tpu_custom_call" | custom-call | flops 7000000 | bytes 21000000 | tf_op jit(solution)/shard_map/flow/pallas_call | solution.py:533
Async XLA Ops:
  3.6 23.9 %collective-permute-start = (f32[11,64,512]{2,1,0:T(8,128)}, f32[11,64,512]{2,1,0:T(8,128)}, u32[]{:S(2)}, u32[]{:S(2)}) collective-permute-start(f32[11,64,512]{2,1,0:T(8,128)} %get-tuple-element.35), channel_id=1, source_target_pairs={{0,2},{2,4},{4,6},{6,8},{8,10},{10,12},{12,14},{14,16},{16,18},{18... | collective-permute-start | bytes 4325384 | tf_op jit(solution)/shard_map/ppermute | solution.py:582
  7.1 15.3 %collective-permute-start.1 = (f32[6,64,512]{2,1,0:T(8,128)}, f32[6,64,512]{2,1,0:T(8,128)}, u32[]{:S(2)}, u32[]{:S(2)}) collective-permute-start(f32[6,64,512]{2,1,0:T(8,128)} %get-tuple-element.36), channel_id=1, source_target_pairs={{2,0},{4,2},{6,4},{8,6},{10,8},{12,10},{14,12},{16,14},{18,16},{20... | collective-permute-start | bytes 2359304 | tf_op jit(solution)/shard_map/ppermute | solution.py:585
  13.1 24.6 %all-to-all-start = ((f32[32,2,8,256]{3,2,1,0:T(8,128)}), f32[32,2,8,256]{3,2,1,0:T(8,128)S(1)}, u32[]{:S(2)}, u32[]{:S(2)}) async-start(f32[32,2,8,256]{3,2,1,0:T(8,128)} %get-tuple-element.34), calls=%async_computation | async-start | bytes 1048576 | tf_op jit(solution)/shard_map/all_to_all | solution.py:629
  20.6 17.2 %copy-start = (f32[8,256]{1,0:T(8,128)S(1)}, f32[8,256]{1,0:T(8,128)}, u32[]{:S(2)}) copy-start(f32[8,256]{1,0:T(8,128)} %get-tuple-element.40.decay) | copy-start | bytes 24580
  37.7 42.5 %collective-permute-start.4 = (f32[6,64,512]{2,1,0:T(8,128)}, f32[6,64,512]{2,1,0:T(8,128)}, u32[]{:S(2)}, u32[]{:S(2)}) collective-permute-start(f32[6,64,512]{2,1,0:T(8,128)} %get-tuple-element.48.own_at), channel_id=1, source_target_pairs={{0,1},{1,0},{2,3},{3,2},{4,5},{5,4},{6,7},{7,6},{8,9},{9,8},{10,11... | collective-permute-start | bytes 2359304 | tf_op jit(solution)/shard_map/ppermute | solution.py:588
  38.5 69.0 %collective-permute-start.3 = (f32[10,64,512]{2,1,0:T(8,128)}, f32[10,64,512]{2,1,0:T(8,128)}, u32[]{:S(2)}, u32[]{:S(2)}) collective-permute-start(f32[10,64,512]{2,1,0:T(8,128)} %get-tuple-element.44), channel_id=1, source_target_pairs={{2,0},{4,2},{6,4},{8,6},{10,8},{12,10},{14,12},{16,14},{18,16},{20... | collective-permute-start | bytes 3932168 | tf_op jit(solution)/shard_map/ppermute | solution.py:585
  38.6 69.0 %collective-permute-start.2 = (f32[9,64,512]{2,1,0:T(8,128)}, f32[9,64,512]{2,1,0:T(8,128)}, u32[]{:S(2)}, u32[]{:S(2)}) collective-permute-start(f32[9,64,512]{2,1,0:T(8,128)} %get-tuple-element.43), channel_id=1, source_target_pairs={{0,2},{2,4},{4,6},{6,8},{8,10},{10,12},{12,14},{14,16},{16,18},{18... | collective-permute-start | bytes 3538952 | tf_op jit(solution)/shard_map/ppermute | solution.py:582
  44.9 62.6 %collective-permute-start.7 = (f32[6,64,512]{2,1,0:T(8,128)}, f32[6,64,512]{2,1,0:T(8,128)}, u32[]{:S(2)}, u32[]{:S(2)}) collective-permute-start(f32[6,64,512]{2,1,0:T(8,128)} %get-tuple-element.58), channel_id=1, source_target_pairs={{2,0},{4,2},{6,4},{8,6},{10,8},{12,10},{14,12},{16,14},{18,16},{20... | collective-permute-start | bytes 2359304 | tf_op jit(solution)/shard_map/ppermute | solution.py:585
  44.9 35.3 %all-to-all-start.1 = ((f32[8,2,8,256]{3,2,1,0:T(8,128)}), f32[8,2,8,256]{3,2,1,0:T(8,128)S(1)}, u32[]{:S(2)}, u32[]{:S(2)}) async-start(f32[8,2,8,256]{3,2,1,0:T(8,128)} %group_moments.1), calls=%async_computation.1 | async-start | bytes 262144 | tf_op jit(solution)/shard_map/all_to_all | solution.py:662
  55.4 38.5 %collective-permute-start.5 = (f32[5,64,512]{2,1,0:T(8,128)}, f32[5,64,512]{2,1,0:T(8,128)}, u32[]{:S(2)}, u32[]{:S(2)}) collective-permute-start(f32[5,64,512]{2,1,0:T(8,128)} %edge_spectrum.1.edge_at), channel_id=1, source_target_pairs={{0,1},{1,0},{2,3},{3,2},{4,5},{5,4},{6,7},{7,6},{8,9},{9,8},{10,11... | collective-permute-start | bytes 1966088 | tf_op jit(solution)/shard_map/ppermute | solution.py:588
  80.2 27.3 %collective-permute-start.6 = (f32[4,64,512]{2,1,0:T(8,128)}, f32[4,64,512]{2,1,0:T(8,128)}, u32[]{:S(2)}, u32[]{:S(2)}) collective-permute-start(f32[4,64,512]{2,1,0:T(8,128)} %get-tuple-element.57), channel_id=1, source_target_pairs={{0,2},{2,4},{4,6},{6,8},{8,10},{10,12},{12,14},{14,16},{16,18},{18... | collective-permute-start | bytes 1572872 | tf_op jit(solution)/shard_map/ppermute | solution.py:582
  81.1 16.9 %all-to-all-start.2 = ((f32[32,2,8,256]{3,2,1,0:T(8,128)}), f32[32,2,8,256]{3,2,1,0:T(8,128)S(1)}, u32[]{:S(2)}, u32[]{:S(2)}) async-start(f32[32,2,8,256]{3,2,1,0:T(8,128)} %bitcast.10), calls=%async_computation.2 | async-start | bytes 1048576 | tf_op jit(solution)/shard_map/all_to_all | solution.py:672
  98.0 0.8 copy-start.1

commit v7 on v6

--- a/solution.py
+++ b/solution.py
@@ -658,10 +658,13 @@
         us=1.0,
         name="group_moments",
     )
-    ring, flow_right, flow_left = lax.optimization_barrier((ring, flow_right, flow_left))
     ring = lax.all_to_all(ring, "z", 0, 0, tiled=True)
+    from_right = to_left(to_left_part)
+    from_left = to_right(to_right_part)
+    ring, spec_other, flow_right, flow_left, from_right, from_left = lax.optimization_barrier(
+        (ring, spec_other, flow_right, flow_left, from_right, from_left)
+    )
     flow_before, flow_after = to_right(flow_right), to_left(flow_left)
-    ring, spec_other = lax.optimization_barrier((ring, spec_other))
     carries = near(
         carry_kernel,
         like(places, chunks // places, 2, rows, width),
@@ -670,8 +673,6 @@
         name="group_carries",
     )
     carries = lax.all_to_all(carries.reshape(chunks, 2, rows, width), GROUP_ALL, 0, 0, tiled=True)
-    from_right = to_left(to_left_part)
-    from_left = to_right(to_right_part)
 
     (source,) = near(
         source_kernel,

time: 120 us -> 129 us (1.075)
  blocking collectives: 0 us -> 11.3 us
  waiting for transfers between devices: 37.2 us -> 33.2 us
  starting transfers between devices: 31.8 us -> 33.8 us
    all_to_all x0 -> x1, blocking collectives: none -> 11.3 us  [shards(): ring = lax.all_to_all(ring, 'z', 0, 0, tiled=True)]
    ppermute x3, starting transfers between devices: 9.85 us -> 17.7 us  [to_right(): lax.ppermute(block, ALONG, [(i, (i + 1) % across) for i in range(across)])]
    all_to_all x1 -> x0, starting transfers between devices: 6.69 us -> none  [shards(): ring = lax.all_to_all(ring, 'z', 0, 0, tiled=True)]
    ppermute x2, waiting for transfers between devices: 30 us -> 26.3 us  [other_half(): return lax.ppermute(block, 'gz', [(0, 1), (1, 0)])]
    all_to_all x1, starting transfers between devices: 6.47 us -> 8.31 us  [shards(): lax.all_to_all(carries.reshape(chunks, 2, rows, width), GROUP_ALL, 0, 0,...]
  transfers between devices with their start and end apart: 11 -> 10, of which waited for: 5 -> 4; matrix products, arithmetic and copies ran while one was open for 0% -> 0% of each run, Pallas kernels for 29% -> 26%
where the time goes in v7:
time: 129 us; the launch traced here: 126 us
  Pallas kernels  46.7 us (36%)
  starting transfers between devices  33.8 us (26%)
  waiting for transfers between devices  33.2 us (26%)
  blocking collectives  11.3 us (9%)
    ppermute x2, waiting for transfers between devices, other_half(): return lax.ppermute(block, 'gz', [(0, 1), (1, 0)])  26.3 us
    pallas_call x2, Pallas kernels, by_rows(): pl.pallas_call(kernel, grid=(levels // ROWS,), out_shape=outs, in_specs=[...  20.6 us
    ppermute x3, starting transfers between devices, to_right(): lax.ppermute(block, ALONG, [(i, (i + 1) % across) for i in range(across)])  17.7 us
    pallas_call x4, Pallas kernels, near(): pl.pallas_call(kernel, out_shape=outs, in_specs=[AWAY if k in away else w...  13.3 us
    pallas_call x3, Pallas kernels, call(): pl.pallas_call(kernel, grid=(1,), out_shape=outs, in_specs=[AWAY if k in...  12.8 us
    all_to_all x1, blocking collectives, shards(): ring = lax.all_to_all(ring, 'z', 0, 0, tiled=True)  11.3 us
    all_to_all x1, starting transfers between devices, shards(): lax.all_to_all(carries.reshape(chunks, 2, rows, width), GROUP_ALL, 0, 0,...  8.31 us
    all_to_all x1, starting transfers between devices, shards(): gathered = lax.all_to_all(sums, GROUP_ALL, 0, 0, tiled=True)  7.5 us
  transfers between devices with their start and end apart: 10, of which 4 were waited for; matrix products, arithmetic and copies ran while one was open for 0% of the time, Pallas kernels for 26%

profile of v7, /device:TPU:103, one launch (start us, length us, event | category | flops | bytes accessed | tf_op | source)
XLA Modules:
  0.0 126.5 jit_solution(17063087020615068039)
XLA Ops:
  0.6 3.0 %pack.1 = (f32[11,64,512]{2,1,0:T(8,128)}, f32[6,64,512]{2,1,0:T(8,128)}) custom-call(f32[6,64,512]{2,1,0:T(8,128)} %bitcast.33, f32[6,64,512]{2,1,0:T(8,128)} %bitcast.21, f32[6,64,512]{2,1,0:T(8,128)} %bitcast.23, f32[6,64,512]{2,1,0:T(8,128)} %bitcast.25, f32[6,64,512]{2,1,0:T(8,128)} %bitcast.27), custom_call_target="tpu_custom_call" | custom-call | flops 2000000 | bytes 6000000 | tf_op jit(solution)/shard_map/pack/pallas_call | solution.py:496
  3.6 3.5 %collective-permute-start = (f32[11,64,512]{2,1,0:T(8,128)}, f32[11,64,512]{2,1,0:T(8,128)}, u32[]{:S(2)}, u32[]{:S(2)}) collective-permute-start(f32[11,64,512]{2,1,0:T(8,128)} %get-tuple-element.36), channel_id=1, source_target_pairs={{0,2},{2,4},{4,6},{6,8},{8,10},{10,12},{12,14},{14,16},{16,18},{18... | collective-permute-start | bytes 4325384 | tf_op jit(solution)/shard_map/ppermute | solution.py:582
  7.1 0.0 collective-permute-start.1
  7.1 6.0 %block_moments.1 = (f32[6,64,512]{2,1,0:T(8,128)}, f32[3,128,512]{2,1,0:T(8,128)}, f32[32,2,8,256]{3,2,1,0:T(8,128)}, f32[8,256]{1,0:T(8,128)}, f32[9,64,512]{2,1,0:T(8,128)}, /*index=5*/f32[10,64,512]{2,1,0:T(8,128)}) custom-call(f32[6,64,512]{2,1,0:T(8,128)} %bitcast.34, bf16[512,512]{1,0:T(8,128)(2,1)} %constant.6.clone.refs_1_.table_hi.refs_4_, ...), custom_call_target="tpu_custom_call" | custom-call | flops 5000000 | bytes 15000000 | tf_op jit(solution)/shard_map/block_moments/pallas_call | solution.py:496
  13.1 7.5 %all-to-all-start = ((f32[32,2,8,256]{3,2,1,0:T(8,128)}), f32[32,2,8,256]{3,2,1,0:T(8,128)S(1)}, u32[]{:S(2)}, u32[]{:S(2)}) async-start(f32[32,2,8,256]{3,2,1,0:T(8,128)} %get-tuple-element.35), calls=%async_computation | async-start | bytes 1048576 | tf_op jit(solution)/shard_map/all_to_all | solution.py:629
  20.6 0.0 copy-start
  20.6 1.8 %collective-permute-done.1.after = f32[6,64,512]{2,1,0:T(8,128)} collective-permute-done((f32[6,64,512]{2,1,0:T(8,128)}, f32[6,64,512]{2,1,0:T(8,128)}, u32[]{:S(2)}, u32[]{:S(2)}) %collective-permute-start.1) | collective-permute-done | bytes 786464 | tf_op jit(solution)/shard_map/ppermute | solution.py:585
  22.4 5.1 %collective-permute-done.before = f32[11,64,512]{2,1,0:T(8,128)} collective-permute-done((f32[11,64,512]{2,1,0:T(8,128)}, f32[11,64,512]{2,1,0:T(8,128)}, u32[]{:S(2)}, u32[]{:S(2)}) %collective-permute-start) | collective-permute-done | bytes 1441824 | tf_op jit(solution)/shard_map/ppermute | solution.py:582
  27.5 10.2 %tracers.1 = (f32[6,64,512]{2,1,0:T(8,128)}, f32[6,64,512]{2,1,0:T(8,128)}, f32[6,64,512]{2,1,0:T(8,128)}, f32[6,64,512]{2,1,0:T(8,128)}, f32[4,64,512]{2,1,0:T(8,128)}) custom-call(f32[6,64,512]{2,1,0:T(8,128)} %bitcast.22, f32[6,64,512]{2,1,0:T(8,128)} %bitcast.24, f32[6,64,512]{2,1,0:T(8,128)} %bitcast.19, f32[6,64,512]{2,1,0:T(8,128)} %bitcast.26, ...), custom_call_target="tpu_custom_call" | custom-call | flops 9000000 | bytes 27000000 | tf_op jit(solution)/shard_map/tracers/pallas_call | solution.py:533
  37.7 0.1 collective-permute-start.3
  37.8 0.0 all-to-all-done
  37.8 0.1 collective-permute-start.2
  37.9 6.4 %collective-permute-start.4 = (f32[4,64,512]{2,1,0:T(8,128)}, f32[4,64,512]{2,1,0:T(8,128)}, u32[]{:S(2)}, u32[]{:S(2)}) collective-permute-start(f32[4,64,512]{2,1,0:T(8,128)} %get-tuple-element.46), channel_id=1, source_target_pairs={{0,2},{2,4},{4,6},{6,8},{8,10},{10,12},{12,14},{14,16},{16,18},{18... | collective-permute-start | bytes 1572872 | tf_op jit(solution)/shard_map/ppermute | solution.py:582
  44.4 0.0 copy-done
  44.4 0.1 group_moments.1
  44.4 11.3 %all_to_all.15.rings = f32[8,2,8,256]{3,2,1,0:T(8,128)S(1)} all-to-all(f32[8,2,8,256]{3,2,1,0:T(8,128)S(1)} %group_moments.1), channel_id=1, replica_groups=mesh['z'=8,'yh'=2,'x'=4,'c'=2,'gz'=2] {'z'}, dimensions={0} | all-to-all | bytes 262144 | tf_op jit(solution)/shard_map/all_to_all | solution.py:661
  55.7 0.0 collective-permute-done.4.from_left
  55.7 0.0 collective-permute-done.3.from_right
  55.7 6.6 %collective-permute-done.2.own_other_at = f32[6,64,512]{2,1,0:T(8,128)} collective-permute-done((f32[6,64,512]{2,1,0:T(8,128)}, f32[6,64,512]{2,1,0:T(8,128)}, u32[]{:S(2)}, u32[]{:S(2)}) %collective-permute-start.2) | collective-permute-done | bytes 786464 | tf_op jit(solution)/shard_map/ppermute | solution.py:588
  62.3 0.0 collective-permute-start.6
  62.3 7.8 %collective-permute-start.5 = (f32[9,64,512]{2,1,0:T(8,128)}, f32[9,64,512]{2,1,0:T(8,128)}, u32[]{:S(2)}, u32[]{:S(2)}) collective-permute-start(f32[9,64,512]{2,1,0:T(8,128)} %get-tuple-element.47), channel_id=1, source_target_pairs={{0,2},{2,4},{4,6},{6,8},{8,10},{10,12},{12,14},{14,16},{16,18},{18... | collective-permute-start | bytes 3538952 | tf_op jit(solution)/shard_map/ppermute | solution.py:582
  70.1 3.8 %edge_spectrum.1.edge_at = f32[5,64,512]{2,1,0:T(8,128)} custom-call(f32[11,64,512]{2,1,0:T(8,128)} %collective-permute-done.before, f32[6,64,512]{2,1,0:T(8,128)} %collective-permute-done.1.after, bf16[512,512]{1,0:T(8,128)(2,1)} %constant.6.clone.refs_1_.table_hi.refs_4_, bf16[512,512]{1,0:T(8,128)(2,1)} %constant.7.clone.refs_2_.table_lo.refs_5_), custom_call_target="tpu_custom_call" | custom-call | flops 2000000 | bytes 6000000 | tf_op jit(solution)/shard_map/edge_spectrum/pallas_call | solution.py:496
  73.9 0.1 collective-permute-start.7
  74.0 0.8 group_carries.1
  74.8 8.3 %all-to-all-start.2 = ((f32[32,2,8,256]{3,2,1,0:T(8,128)}), f32[32,2,8,256]{3,2,1,0:T(8,128)S(1)}, u32[]{:S(2)}, u32[]{:S(2)}) async-start(f32[32,2,8,256]{3,2,1,0:T(8,128)} %bitcast.10), calls=%async_computation.2 | async-start | bytes 1048576 | tf_op jit(solution)/shard_map/all_to_all | solution.py:675
  83.1 19.7 %collective-permute-done.7.edge_other_at = f32[5,64,512]{2,1,0:T(8,128)} collective-permute-done((f32[5,64,512]{2,1,0:T(8,128)}, f32[5,64,512]{2,1,0:T(8,128)}, u32[]{:S(2)}, u32[]{:S(2)}) %collective-permute-start.7) | collective-permute-done | bytes 655392 | tf_op jit(solution)/shard_map/ppermute | solution.py:588
  102.9 3.7 %mode_source.1.refs_0_ = f32[11,128,512]{2,1,0:T(8,128)} custom-call(f32[6,64,512]{2,1,0:T(8,128)} %get-tuple-element.42.own_at, f32[5,64,512]{2,1,0:T(8,128)} %edge_spectrum.1.edge_at, f32[6,64,512]{2,1,0:T(8,128)} %collective-permute-done.2.own_other_at, f32[5,64,512]{2,1,0:T(8,128)} %collective-permute-done.7.edge_other_at, f32[128,128]{1,0:T(8,128)} %depth_at.1), custom_call_target="tpu_custom_call" | custom-call | flops 4000000 | bytes 12000000 | tf_op jit(solution)/shard_map/mode_source/pallas_call | solution.py:513
  106.6 0.0 all-to-all-done.2.refs_1_
  106.6 0.0 copy-start.1
  106.6 0.8 copy-done.1
  107.4 8.8 %pressure.1 = (f32[6,64,512]{2,1,0:T(8,128)}, f32[7,64,512]{2,1,0:T(8,128)}) custom-call(f32[11,128,512]{2,1,0:T(8,128)} %mode_source.1.refs_0_, f32[32,2,8,256]{3,2,1,0:T(8,128)} %copy-done.1, f32[3,128,512]{2,1,0:T(8,128)} %get-tuple-element.53.refs_2_, f32[128,128]{1,0:T(8,128)} %refs_3_.3, bf16[512,512]{1,0:T(8,128)(2,1)} %constant.6.clone.refs_1_.table_hi.refs_4_, ...), custom_call_target="tpu_custom_call" | custom-call | flops 7000000 | bytes 21000000 | tf_op jit(solution)/shard_map/pressure/pallas_call | solution.py:513
  116.1 0.0 collective-permute-done.5.before
  116.1 0.0 collective-permute-done.6.after
  116.1 10.4 %flow.1 = (f32[6,64,512]{2,1,0:T(8,128)}, f32[6,64,512]{2,1,0:T(8,128)}, f32[6,64,512]{2,1,0:T(8,128)}, f32[6,64,512]{2,1,0:T(8,128)}) custom-call(f32[6,64,512]{2,1,0:T(8,128)} %bitcast.30, f32[6,64,512]{2,1,0:T(8,128)} %bitcast.20, f32[6,64,512]{2,1,0:T(8,128)} %bitcast.32, f32[9,64,512]{2,1,0:T(8,128)} %collective-permute-done.5.before, ...), custom_call_target="tpu_custom_call" | custom-call | flops 7000000 | bytes 21000000 | tf_op jit(solution)/shard_map/flow/pallas_call | solution.py:533
Async XLA Ops:
  3.6 23.9 %collective-permute-start = (f32[11,64,512]{2,1,0:T(8,128)}, f32[11,64,512]{2,1,0:T(8,128)}, u32[]{:S(2)}, u32[]{:S(2)}) collective-permute-start(f32[11,64,512]{2,1,0:T(8,128)} %get-tuple-element.36), channel_id=1, source_target_pairs={{0,2},{2,4},{4,6},{6,8},{8,10},{10,12},{12,14},{14,16},{16,18},{18... | collective-permute-start | bytes 4325384 | tf_op jit(solution)/shard_map/ppermute | solution.py:582
  7.1 15.3 %collective-permute-start.1 = (f32[6,64,512]{2,1,0:T(8,128)}, f32[6,64,512]{2,1,0:T(8,128)}, u32[]{:S(2)}, u32[]{:S(2)}) collective-permute-start(f32[6,64,512]{2,1,0:T(8,128)} %get-tuple-element.37), channel_id=1, source_target_pairs={{2,0},{4,2},{6,4},{8,6},{10,8},{12,10},{14,12},{16,14},{18,16},{20... | collective-permute-start | bytes 2359304 | tf_op jit(solution)/shard_map/ppermute | solution.py:585
  13.1 24.7 %all-to-all-start = ((f32[32,2,8,256]{3,2,1,0:T(8,128)}), f32[32,2,8,256]{3,2,1,0:T(8,128)S(1)}, u32[]{:S(2)}, u32[]{:S(2)}) async-start(f32[32,2,8,256]{3,2,1,0:T(8,128)} %get-tuple-element.35), calls=%async_computation | async-start | bytes 1048576 | tf_op jit(solution)/shard_map/all_to_all | solution.py:629
  20.6 23.7 %copy-start = (f32[8,256]{1,0:T(8,128)S(1)}, f32[8,256]{1,0:T(8,128)}, u32[]{:S(2)}) copy-start(f32[8,256]{1,0:T(8,128)} %get-tuple-element.41.decay) | copy-start | bytes 24580
  37.7 18.0 %collective-permute-start.3 = (f32[6,64,512]{2,1,0:T(8,128)}, f32[6,64,512]{2,1,0:T(8,128)}, u32[]{:S(2)}, u32[]{:S(2)}) collective-permute-start(f32[6,64,512]{2,1,0:T(8,128)} %get-tuple-element.45), channel_id=1, source_target_pairs={{2,0},{4,2},{6,4},{8,6},{10,8},{12,10},{14,12},{16,14},{18,16},{20... | collective-permute-start | bytes 2359304 | tf_op jit(solution)/shard_map/ppermute | solution.py:585
  37.8 24.5 %collective-permute-start.2 = (f32[6,64,512]{2,1,0:T(8,128)}, f32[6,64,512]{2,1,0:T(8,128)}, u32[]{:S(2)}, u32[]{:S(2)}) collective-permute-start(f32[6,64,512]{2,1,0:T(8,128)} %get-tuple-element.42.own_at), channel_id=1, source_target_pairs={{0,1},{1,0},{2,3},{3,2},{4,5},{5,4},{6,7},{7,6},{8,9},{9,8},{10,11... | collective-permute-start | bytes 2359304 | tf_op jit(solution)/shard_map/ppermute | solution.py:588
  37.9 17.8 %collective-permute-start.4 = (f32[4,64,512]{2,1,0:T(8,128)}, f32[4,64,512]{2,1,0:T(8,128)}, u32[]{:S(2)}, u32[]{:S(2)}) collective-permute-start(f32[4,64,512]{2,1,0:T(8,128)} %get-tuple-element.46), channel_id=1, source_target_pairs={{0,2},{2,4},{4,6},{6,8},{8,10},{10,12},{12,14},{14,16},{16,18},{18... | collective-permute-start | bytes 1572872 | tf_op jit(solution)/shard_map/ppermute | solution.py:582
  62.3 53.8 %collective-permute-start.6 = (f32[10,64,512]{2,1,0:T(8,128)}, f32[10,64,512]{2,1,0:T(8,128)}, u32[]{:S(2)}, u32[]{:S(2)}) collective-permute-start(f32[10,64,512]{2,1,0:T(8,128)} %get-tuple-element.48), channel_id=1, source_target_pairs={{2,0},{4,2},{6,4},{8,6},{10,8},{12,10},{14,12},{16,14},{18,16},{20... | collective-permute-start | bytes 3932168 | tf_op jit(solution)/shard_map/ppermute | solution.py:585
  62.3 53.8 %collective-permute-start.5 = (f32[9,64,512]{2,1,0:T(8,128)}, f32[9,64,512]{2,1,0:T(8,128)}, u32[]{:S(2)}, u32[]{:S(2)}) collective-permute-start(f32[9,64,512]{2,1,0:T(8,128)} %get-tuple-element.47), channel_id=1, source_target_pairs={{0,2},{2,4},{4,6},{6,8},{8,10},{10,12},{12,14},{14,16},{16,18},{18... | collective-permute-start | bytes 3538952 | tf_op jit(solution)/shard_map/ppermute | solution.py:582
  73.9 29.0 %collective-permute-start.7 = (f32[5,64,512]{2,1,0:T(8,128)}, f32[5,64,512]{2,1,0:T(8,128)}, u32[]{:S(2)}, u32[]{:S(2)}) collective-permute-start(f32[5,64,512]{2,1,0:T(8,128)} %edge_spectrum.1.edge_at), channel_id=1, source_target_pairs={{0,1},{1,0},{2,3},{3,2},{4,5},{5,4},{6,7},{7,6},{8,9},{9,8},{10,11... | collective-permute-start | bytes 1966088 | tf_op jit(solution)/shard_map/ppermute | solution.py:588
  74.8 31.7 %all-to-all-start.2 = ((f32[32,2,8,256]{3,2,1,0:T(8,128)}), f32[32,2,8,256]{3,2,1,0:T(8,128)S(1)}, u32[]{:S(2)}, u32[]{:S(2)}) async-start(f32[32,2,8,256]{3,2,1,0:T(8,128)} %bitcast.10), calls=%async_computation.2 | async-start | bytes 1048576 | tf_op jit(solution)/shard_map/all_to_all | solution.py:675
  106.6 0.8 copy-start.1

commit v8 on v6

--- a/solution.py
+++ b/solution.py
@@ -627,6 +627,10 @@
         name="block_moments",
     )
     gathered = lax.all_to_all(sums, GROUP_ALL, 0, 0, tiled=True)
+    before, after, flow_right, flow_left = lax.optimization_barrier(
+        (before, after, flow_right, flow_left)
+    )
+    flow_before, flow_after = to_right(flow_right), to_left(flow_left)
     t_base, s_base, c_base, to_left_part, to_right_part = by_rows(
         tracer_kernel,
         [like(n, levels, columns)] * 3 + [like(6, levels, columns), like(4, levels, columns)],
@@ -658,9 +662,7 @@
         us=1.0,
         name="group_moments",
     )
-    ring, flow_right, flow_left = lax.optimization_barrier((ring, flow_right, flow_left))
     ring = lax.all_to_all(ring, "z", 0, 0, tiled=True)
-    flow_before, flow_after = to_right(flow_right), to_left(flow_left)
     ring, spec_other = lax.optimization_barrier((ring, spec_other))
     carries = near(
         carry_kernel,

time: 120 us -> 120 us (level)
  no operation moved by 1% of the time
where the time goes in v8:
time: 120 us; the launch traced here: 118 us
  Pallas kernels  47.3 us (39%)
  waiting for transfers between devices  37.2 us (31%)
  starting transfers between devices  31.8 us (26%)
    ppermute x2, waiting for transfers between devices, other_half(): return lax.ppermute(block, 'gz', [(0, 1), (1, 0)])  30 us
    pallas_call x2, Pallas kernels, by_rows(): pl.pallas_call(kernel, grid=(levels // ROWS,), out_shape=outs, in_specs=[...  20.6 us
    pallas_call x4, Pallas kernels, near(): pl.pallas_call(kernel, out_shape=outs, in_specs=[AWAY if k in away else w...  13.9 us
    pallas_call x3, Pallas kernels, call(): pl.pallas_call(kernel, grid=(1,), out_shape=outs, in_specs=[AWAY if k in...  12.8 us
    ppermute x3, starting transfers between devices, to_right(): lax.ppermute(block, ALONG, [(i, (i + 1) % across) for i in range(across)])  9.91 us
    all_to_all x1, starting transfers between devices, shards(): gathered = lax.all_to_all(sums, GROUP_ALL, 0, 0, tiled=True)  7.49 us
    all_to_all x1, starting transfers between devices, shards(): ring = lax.all_to_all(ring, 'z', 0, 0, tiled=True)  6.69 us
    all_to_all x1, starting transfers between devices, shards(): lax.all_to_all(carries.reshape(chunks, 2, rows, width), GROUP_ALL, 0, 0,...  6.47 us
  transfers between devices with their start and end apart: 11, of which 5 were waited for; matrix products, arithmetic and copies ran while one was open for 0% of the time, Pallas kernels for 29%

profile of v8, /device:TPU:103, one launch (start us, length us, event | category | flops | bytes accessed | tf_op | source)
XLA Modules:
  0.0 117.9 jit_solution(5263207107987276901)
XLA Ops:
  0.6 3.0 %pack.1 = (f32[11,64,512]{2,1,0:T(8,128)}, f32[6,64,512]{2,1,0:T(8,128)}) custom-call(f32[6,64,512]{2,1,0:T(8,128)} %bitcast.33, f32[6,64,512]{2,1,0:T(8,128)} %bitcast.21, f32[6,64,512]{2,1,0:T(8,128)} %bitcast.23, f32[6,64,512]{2,1,0:T(8,128)} %bitcast.25, f32[6,64,512]{2,1,0:T(8,128)} %bitcast.27), custom_call_target="tpu_custom_call" | custom-call | flops 2000000 | bytes 6000000 | tf_op jit(solution)/shard_map/pack/pallas_call | solution.py:496
  3.6 3.5 %collective-permute-start = (f32[11,64,512]{2,1,0:T(8,128)}, f32[11,64,512]{2,1,0:T(8,128)}, u32[]{:S(2)}, u32[]{:S(2)}) collective-permute-start(f32[11,64,512]{2,1,0:T(8,128)} %get-tuple-element.35), channel_id=1, source_target_pairs={{0,2},{2,4},{4,6},{6,8},{8,10},{10,12},{12,14},{14,16},{16,18},{18... | collective-permute-start | bytes 4325384 | tf_op jit(solution)/shard_map/ppermute | solution.py:582
  7.1 0.0 collective-permute-start.1
  7.1 6.0 %block_moments.1 = (f32[6,64,512]{2,1,0:T(8,128)}, f32[3,128,512]{2,1,0:T(8,128)}, f32[32,2,8,256]{3,2,1,0:T(8,128)}, f32[8,256]{1,0:T(8,128)}, f32[9,64,512]{2,1,0:T(8,128)}, /*index=5*/f32[10,64,512]{2,1,0:T(8,128)}) custom-call(f32[6,64,512]{2,1,0:T(8,128)} %bitcast.34, bf16[512,512]{1,0:T(8,128)(2,1)} %constant.6.clone.refs_1_.table_hi.refs_4_, ...), custom_call_target="tpu_custom_call" | custom-call | flops 5000000 | bytes 15000000 | tf_op jit(solution)/shard_map/block_moments/pallas_call | solution.py:496
  13.1 7.5 %all-to-all-start = ((f32[32,2,8,256]{3,2,1,0:T(8,128)}), f32[32,2,8,256]{3,2,1,0:T(8,128)S(1)}, u32[]{:S(2)}, u32[]{:S(2)}) async-start(f32[32,2,8,256]{3,2,1,0:T(8,128)} %get-tuple-element.42), calls=%async_computation | async-start | bytes 1048576 | tf_op jit(solution)/shard_map/all_to_all | solution.py:629
  20.6 1.8 %collective-permute-done.1.after = f32[6,64,512]{2,1,0:T(8,128)} collective-permute-done((f32[6,64,512]{2,1,0:T(8,128)}, f32[6,64,512]{2,1,0:T(8,128)}, u32[]{:S(2)}, u32[]{:S(2)}) %collective-permute-start.1) | collective-permute-done | bytes 786464 | tf_op jit(solution)/shard_map/ppermute | solution.py:585
  22.4 5.1 %collective-permute-done.before = f32[11,64,512]{2,1,0:T(8,128)} collective-permute-done((f32[11,64,512]{2,1,0:T(8,128)}, f32[11,64,512]{2,1,0:T(8,128)}, u32[]{:S(2)}, u32[]{:S(2)}) %collective-permute-start) | collective-permute-done | bytes 1441824 | tf_op jit(solution)/shard_map/ppermute | solution.py:582
  27.5 0.0 copy-start
  27.5 10.2 %tracers.1 = (f32[6,64,512]{2,1,0:T(8,128)}, f32[6,64,512]{2,1,0:T(8,128)}, f32[6,64,512]{2,1,0:T(8,128)}, f32[6,64,512]{2,1,0:T(8,128)}, f32[4,64,512]{2,1,0:T(8,128)}) custom-call(f32[6,64,512]{2,1,0:T(8,128)} %bitcast.22, f32[6,64,512]{2,1,0:T(8,128)} %bitcast.24, f32[6,64,512]{2,1,0:T(8,128)} %bitcast.19, f32[6,64,512]{2,1,0:T(8,128)} %bitcast.26, ...), custom_call_target="tpu_custom_call" | custom-call | flops 9000000 | bytes 27000000 | tf_op jit(solution)/shard_map/tracers/pallas_call | solution.py:533
  37.7 0.0 all-to-all-done
  37.7 0.1 collective-permute-start.4
  37.8 0.1 collective-permute-start.3
  37.9 6.4 %collective-permute-start.2 = (f32[9,64,512]{2,1,0:T(8,128)}, f32[9,64,512]{2,1,0:T(8,128)}, u32[]{:S(2)}, u32[]{:S(2)}) collective-permute-start(f32[9,64,512]{2,1,0:T(8,128)} %get-tuple-element.39), channel_id=1, source_target_pairs={{0,2},{2,4},{4,6},{6,8},{8,10},{10,12},{12,14},{14,16},{16,18},{18... | collective-permute-start | bytes 3538952 | tf_op jit(solution)/shard_map/ppermute | solution.py:582
  44.4 0.0 collective-permute-start.7
  44.4 0.0 copy-done
  44.4 0.7 group_moments.1
  45.1 6.7 %all-to-all-start.1 = ((f32[8,2,8,256]{3,2,1,0:T(8,128)}), f32[8,2,8,256]{3,2,1,0:T(8,128)S(1)}, u32[]{:S(2)}, u32[]{:S(2)}) async-start(f32[8,2,8,256]{3,2,1,0:T(8,128)} %group_moments.1), calls=%async_computation.1 | async-start | bytes 262144 | tf_op jit(solution)/shard_map/all_to_all | solution.py:665
  51.8 3.8 %edge_spectrum.1.edge_at = f32[5,64,512]{2,1,0:T(8,128)} custom-call(f32[11,64,512]{2,1,0:T(8,128)} %collective-permute-done.before, f32[6,64,512]{2,1,0:T(8,128)} %collective-permute-done.1.after, bf16[512,512]{1,0:T(8,128)(2,1)} %constant.6.clone.refs_1_.table_hi.refs_4_, bf16[512,512]{1,0:T(8,128)(2,1)} %constant.7.clone.refs_2_.table_lo.refs_5_), custom_call_target="tpu_custom_call" | custom-call | flops 2000000 | bytes 6000000 | tf_op jit(solution)/shard_map/edge_spectrum/pallas_call | solution.py:496
  55.6 1.0 collective-permute-start.5
  56.6 23.6 %collective-permute-done.4.own_other_at = f32[6,64,512]{2,1,0:T(8,128)} collective-permute-done((f32[6,64,512]{2,1,0:T(8,128)}, f32[6,64,512]{2,1,0:T(8,128)}, u32[]{:S(2)}, u32[]{:S(2)}) %collective-permute-start.4) | collective-permute-done | bytes 786464 | tf_op jit(solution)/shard_map/ppermute | solution.py:588
  80.2 0.0 collective-permute-start.6
  80.2 0.0 all-to-all-done.1.rings
  80.2 0.8 group_carries.1
  81.1 6.5 %all-to-all-start.2 = ((f32[32,2,8,256]{3,2,1,0:T(8,128)}), f32[32,2,8,256]{3,2,1,0:T(8,128)S(1)}, u32[]{:S(2)}, u32[]{:S(2)}) async-start(f32[32,2,8,256]{3,2,1,0:T(8,128)} %bitcast.10), calls=%async_computation.2 | async-start | bytes 1048576 | tf_op jit(solution)/shard_map/all_to_all | solution.py:674
  87.6 6.4 %collective-permute-done.5.edge_other_at = f32[5,64,512]{2,1,0:T(8,128)} collective-permute-done((f32[5,64,512]{2,1,0:T(8,128)}, f32[5,64,512]{2,1,0:T(8,128)}, u32[]{:S(2)}, u32[]{:S(2)}) %collective-permute-start.5) | collective-permute-done | bytes 655392 | tf_op jit(solution)/shard_map/ppermute | solution.py:588
  94.0 3.6 %mode_source.1.refs_0_ = f32[11,128,512]{2,1,0:T(8,128)} custom-call(f32[6,64,512]{2,1,0:T(8,128)} %get-tuple-element.50.own_at, f32[5,64,512]{2,1,0:T(8,128)} %edge_spectrum.1.edge_at, f32[6,64,512]{2,1,0:T(8,128)} %collective-permute-done.4.own_other_at, f32[5,64,512]{2,1,0:T(8,128)} %collective-permute-done.5.edge_other_at, f32[128,128]{1,0:T(8,128)} %depth_at.1), custom_call_target="tpu_custom_call" | custom-call | flops 4000000 | bytes 12000000 | tf_op jit(solution)/shard_map/mode_source/pallas_call | solution.py:513
  97.6 0.3 all-to-all-done.2.refs_1_
  98.0 0.0 copy-start.1
  98.0 0.8 copy-done.1
  98.8 8.7 %pressure.1 = (f32[6,64,512]{2,1,0:T(8,128)}, f32[7,64,512]{2,1,0:T(8,128)}) custom-call(f32[11,128,512]{2,1,0:T(8,128)} %mode_source.1.refs_0_, f32[32,2,8,256]{3,2,1,0:T(8,128)} %copy-done.1, f32[3,128,512]{2,1,0:T(8,128)} %get-tuple-element.53.refs_2_, f32[128,128]{1,0:T(8,128)} %refs_3_.3, bf16[512,512]{1,0:T(8,128)(2,1)} %constant.6.clone.refs_1_.table_hi.refs_4_, ...), custom_call_target="tpu_custom_call" | custom-call | flops 7000000 | bytes 21000000 | tf_op jit(solution)/shard_map/pressure/pallas_call | solution.py:513
  107.5 0.0 collective-permute-done.6.from_left
  107.5 0.0 collective-permute-done.7.from_right
  107.5 0.0 collective-permute-done.2.before
  107.5 0.0 collective-permute-done.3.after
  107.5 10.4 %flow.1 = (f32[6,64,512]{2,1,0:T(8,128)}, f32[6,64,512]{2,1,0:T(8,128)}, f32[6,64,512]{2,1,0:T(8,128)}, f32[6,64,512]{2,1,0:T(8,128)}) custom-call(f32[6,64,512]{2,1,0:T(8,128)} %bitcast.30, f32[6,64,512]{2,1,0:T(8,128)} %bitcast.20, f32[6,64,512]{2,1,0:T(8,128)} %bitcast.32, f32[9,64,512]{2,1,0:T(8,128)} %collective-permute-done.2.before, ...), custom_call_target="tpu_custom_call" | custom-call | flops 7000000 | bytes 21000000 | tf_op jit(solution)/shard_map/flow/pallas_call | solution.py:533
Async XLA Ops:
  3.6 23.9 %collective-permute-start = (f32[11,64,512]{2,1,0:T(8,128)}, f32[11,64,512]{2,1,0:T(8,128)}, u32[]{:S(2)}, u32[]{:S(2)}) collective-permute-start(f32[11,64,512]{2,1,0:T(8,128)} %get-tuple-element.35), channel_id=1, source_target_pairs={{0,2},{2,4},{4,6},{6,8},{8,10},{10,12},{12,14},{14,16},{16,18},{18... | collective-permute-start | bytes 4325384 | tf_op jit(solution)/shard_map/ppermute | solution.py:582
  7.1 15.3 %collective-permute-start.1 = (f32[6,64,512]{2,1,0:T(8,128)}, f32[6,64,512]{2,1,0:T(8,128)}, u32[]{:S(2)}, u32[]{:S(2)}) collective-permute-start(f32[6,64,512]{2,1,0:T(8,128)} %get-tuple-element.36), channel_id=1, source_target_pairs={{2,0},{4,2},{6,4},{8,6},{10,8},{12,10},{14,12},{16,14},{18,16},{20... | collective-permute-start | bytes 2359304 | tf_op jit(solution)/shard_map/ppermute | solution.py:585
  13.1 24.6 %all-to-all-start = ((f32[32,2,8,256]{3,2,1,0:T(8,128)}), f32[32,2,8,256]{3,2,1,0:T(8,128)S(1)}, u32[]{:S(2)}, u32[]{:S(2)}) async-start(f32[32,2,8,256]{3,2,1,0:T(8,128)} %get-tuple-element.42), calls=%async_computation | async-start | bytes 1048576 | tf_op jit(solution)/shard_map/all_to_all | solution.py:629
  27.5 16.9 %copy-start = (f32[8,256]{1,0:T(8,128)S(1)}, f32[8,256]{1,0:T(8,128)}, u32[]{:S(2)}) copy-start(f32[8,256]{1,0:T(8,128)} %get-tuple-element.49.decay) | copy-start | bytes 24580
  37.7 42.5 %collective-permute-start.4 = (f32[6,64,512]{2,1,0:T(8,128)}, f32[6,64,512]{2,1,0:T(8,128)}, u32[]{:S(2)}, u32[]{:S(2)}) collective-permute-start(f32[6,64,512]{2,1,0:T(8,128)} %get-tuple-element.50.own_at), channel_id=1, source_target_pairs={{0,1},{1,0},{2,3},{3,2},{4,5},{5,4},{6,7},{7,6},{8,9},{9,8},{10,11... | collective-permute-start | bytes 2359304 | tf_op jit(solution)/shard_map/ppermute | solution.py:588
  37.8 69.7 %collective-permute-start.3 = (f32[10,64,512]{2,1,0:T(8,128)}, f32[10,64,512]{2,1,0:T(8,128)}, u32[]{:S(2)}, u32[]{:S(2)}) collective-permute-start(f32[10,64,512]{2,1,0:T(8,128)} %get-tuple-element.40), channel_id=1, source_target_pairs={{2,0},{4,2},{6,4},{8,6},{10,8},{12,10},{14,12},{16,14},{18,16},{20... | collective-permute-start | bytes 3932168 | tf_op jit(solution)/shard_map/ppermute | solution.py:585
  37.9 69.6 %collective-permute-start.2 = (f32[9,64,512]{2,1,0:T(8,128)}, f32[9,64,512]{2,1,0:T(8,128)}, u32[]{:S(2)}, u32[]{:S(2)}) collective-permute-start(f32[9,64,512]{2,1,0:T(8,128)} %get-tuple-element.39), channel_id=1, source_target_pairs={{0,2},{2,4},{4,6},{6,8},{8,10},{10,12},{12,14},{14,16},{16,18},{18... | collective-permute-start | bytes 3538952 | tf_op jit(solution)/shard_map/ppermute | solution.py:582
  44.4 63.1 %collective-permute-start.7 = (f32[6,64,512]{2,1,0:T(8,128)}, f32[6,64,512]{2,1,0:T(8,128)}, u32[]{:S(2)}, u32[]{:S(2)}) collective-permute-start(f32[6,64,512]{2,1,0:T(8,128)} %get-tuple-element.60), channel_id=1, source_target_pairs={{2,0},{4,2},{6,4},{8,6},{10,8},{12,10},{14,12},{16,14},{18,16},{20... | collective-permute-start | bytes 2359304 | tf_op jit(solution)/shard_map/ppermute | solution.py:585
  45.1 35.1 %all-to-all-start.1 = ((f32[8,2,8,256]{3,2,1,0:T(8,128)}), f32[8,2,8,256]{3,2,1,0:T(8,128)S(1)}, u32[]{:S(2)}, u32[]{:S(2)}) async-start(f32[8,2,8,256]{3,2,1,0:T(8,128)} %group_moments.1), calls=%async_computation.1 | async-start | bytes 262144 | tf_op jit(solution)/shard_map/all_to_all | solution.py:665
  55.6 38.4 %collective-permute-start.5 = (f32[5,64,512]{2,1,0:T(8,128)}, f32[5,64,512]{2,1,0:T(8,128)}, u32[]{:S(2)}, u32[]{:S(2)}) collective-permute-start(f32[5,64,512]{2,1,0:T(8,128)} %edge_spectrum.1.edge_at), channel_id=1, source_target_pairs={{0,1},{1,0},{2,3},{3,2},{4,5},{5,4},{6,7},{7,6},{8,9},{9,8},{10,11... | collective-permute-start | bytes 1966088 | tf_op jit(solution)/shard_map/ppermute | solution.py:588
  80.2 27.3 %collective-permute-start.6 = (f32[4,64,512]{2,1,0:T(8,128)}, f32[4,64,512]{2,1,0:T(8,128)}, u32[]{:S(2)}, u32[]{:S(2)}) collective-permute-start(f32[4,64,512]{2,1,0:T(8,128)} %get-tuple-element.59), channel_id=1, source_target_pairs={{0,2},{2,4},{4,6},{6,8},{8,10},{10,12},{12,14},{14,16},{16,18},{18... | collective-permute-start | bytes 1572872 | tf_op jit(solution)/shard_map/ppermute | solution.py:582
  81.1 16.9 %all-to-all-start.2 = ((f32[32,2,8,256]{3,2,1,0:T(8,128)}), f32[32,2,8,256]{3,2,1,0:T(8,128)S(1)}, u32[]{:S(2)}, u32[]{:S(2)}) async-start(f32[32,2,8,256]{3,2,1,0:T(8,128)} %bitcast.10), calls=%async_computation.2 | async-start | bytes 1048576 | tf_op jit(solution)/shard_map/all_to_all | solution.py:674
  98.0 0.8 copy-start.1
